TPU v7x, 32 devices: a whole 2x2x4 slice. The times are simulated.
32 devices in a mesh: cross: 8 (over z, y), along: 4 (over x, core).
Axes of the slice: x: 2, y: 2, z: 4, core: 2. Of those that a mesh axis runs over, the one named last changes fastest.
Arguments:
- source: float32 [16, 64, 2048], P(None, 'along', 'cross'), may hold values from -6 to 6
- inv_density: float32 [16, 64, 2048], P(None, 'along', 'cross'), may hold values from 0.3 to 3
Outputs:
- pressure: float32 [16, 64, 2048], P(None, 'along', 'cross')
- residual: float32 [16, 64, 2048], P(None, 'along', 'cross')
All inputs are finite; a program needn't handle non-finite values.
Results may differ from a plain program's by a relative error of at most 0.0003.
Values sent between devices are 32-bit elements; how exact they have to be, the bound alone decides.
No kernel may reach another device: no remote copies, remote signals or barrier semaphores. Data moves between devices by JAX's collectives and lax.ppermute only.
A program may use at most 128 MiB of HBM per device.

v0:
```python
import functools
import math

import jax
import jax.numpy as jnp
from jax import lax
from jax.experimental import pallas as pl
from jax.experimental.pallas import tpu as pltpu
from jax.sharding import PartitionSpec as P

SWEEPS = 4

along_weight = 0.25
cross_weight = 1.0
vertical_weight = 0.5
relaxation = 0.8

LANES = 128
GUARD = 8
TINY = 1e-30


def rounded_up(count, step):
    return -(-count // step) * step


def shifted(array, axis, by):
    devices = lax.axis_size(axis)
    pairs = [(i, i + by) for i in range(devices) if 0 <= i + by < devices]
    return lax.ppermute(array, axis, pairs)


def beside(block, axis, dim, width):
    size = block.shape[dim]
    before, after = [], []
    hop = 1
    while width > 0:
        take = min(width, size)
        tail = lax.slice_in_dim(block, size - take, size, axis=dim)
        head = lax.slice_in_dim(block, 0, take, axis=dim)
        before.insert(0, shifted(tail, axis, hop))
        after.append(shifted(head, axis, -hop))
        width -= take
        hop += 1
    if len(before) == 1:
        return before[0], after[0]
    return jnp.concatenate(before, dim), jnp.concatenate(after, dim)


class Plan:
    def __init__(self, cross_count, layers, rows, cols):
        self.coarsest = cross_count.bit_length()
        self.layers, self.own_rows, self.own_cols = layers, rows, cols
        self.row_reach = SWEEPS + 2 * self.coarsest
        reach = SWEEPS
        for _ in range(self.coarsest):
            reach = 2 * reach + 1
        self.col_reach = reach + 1
        chunks = 1
        while (chunks * LANES - cols) // 2 < self.col_reach:
            chunks *= 2
        self.chunks = chunks
        self.side_cols = (chunks * LANES - cols) // 2
        self.rows = rounded_up(rows + 2 * self.row_reach, 8)
        self.side_rows = rounded_up(self.row_reach + 1, 8)

    def level_chunks(self, level_no):
        return max(1, self.chunks >> level_no)

    def spread(self, level_no):
        return max(1, (1 << level_no) // self.chunks)


def lane_numbers(rows):
    return lax.broadcasted_iota(jnp.int32, (rows, LANES), 1)


def window_kernel(plan, own_ref, before_ref, after_ref, out_ref):
    chunks, rows = plan.chunks, plan.own_rows
    lane = lane_numbers(rows)
    picks = [(chunks * lane + chunk) % LANES for chunk in range(chunks)]
    part = lane // (LANES // chunks)

    def layer_step(which, layer_no):
        tiles = []
        for ref in (before_ref, own_ref, after_ref):
            for first in range(0, ref.shape[3], LANES):
                tiles.append(ref[which, layer_no, :, first : first + LANES])
        for chunk in range(chunks):
            value = jnp.take_along_axis(tiles[0], picks[chunk], axis=1)
            for tile_no in range(1, chunks):
                other = jnp.take_along_axis(tiles[tile_no], picks[chunk], axis=1)
                value = jnp.where(part == tile_no, other, value)
            out_ref[which, layer_no, chunk] = value

    for which in range(2):
        pl.loop(0, plan.layers)(functools.partial(layer_step, which))


def reciprocal(value):
    guess = pl.reciprocal(value, approx=True)
    return guess * (2.0 - value * guess)


def ratio(first, second):
    return first * second * reciprocal(jnp.maximum(first + second, TINY))


def previous_of(cells, spread):
    return [pltpu.roll(cells[-1], spread, 1)] + cells[:-1]


def next_of(cells, spread):
    return cells[1:] + [pltpu.roll(cells[0], LANES - spread, 1)]


def first_of_pair(value, spread):
    lane = lane_numbers(value.shape[0])
    return (lane // spread) % 2 == 0


def paired(cells, spread):
    if len(cells) > 1:
        return [cells[2 * k] + cells[2 * k + 1] for k in range(len(cells) // 2)]
    value = cells[0]
    other = jnp.where(
        first_of_pair(value, spread),
        pltpu.roll(value, LANES - spread, 1),
        pltpu.roll(value, spread, 1),
    )
    return [value + other]


def firsts(cells, spread):
    if len(cells) > 1:
        return cells[0::2]
    value = cells[0]
    return [jnp.where(first_of_pair(value, spread), value, pltpu.roll(value, spread, 1))]


def cycle_kernel(plan, own_ref, before_ref, after_ref, pressure_ref, residual_ref, *scratch):
    levels = plan.coarsest + 1
    coarsest = plan.coarsest
    layers, rows = plan.layers, plan.rows
    reach, own_rows = plan.row_reach, plan.own_rows
    scratch = list(scratch)
    upright, centre0, upper0 = scratch[:3]
    rest = scratch[3:]
    west, south, factor, inverse, value, forcing = [
        rest[i * levels : (i + 1) * levels] for i in range(6)
    ]
    upper = [upper0] + forcing[1:]
    density = value[0]
    count = [plan.level_chunks(m) for m in range(levels)]
    spread = [plan.spread(m) for m in range(levels)]

    side = before_ref.shape[3]

    def assemble(layer_no):
        zeros = jnp.zeros((GUARD, LANES), jnp.float32)
        for c in range(count[0]):
            density[layer_no, c, 0:GUARD] = zeros
            tail = rounded_up(GUARD + reach + own_rows + reach + 1, 8)
            density[layer_no, c, tail - 8 : tail] = zeros
            density[layer_no, c, GUARD - 1 : GUARD + reach] = before_ref[
                0, layer_no, c, side - reach - 1 : side
            ]
            density[layer_no, c, GUARD + reach : GUARD + reach + own_rows] = own_ref[0, layer_no, c]
            start = GUARD + reach + own_rows
            density[layer_no, c, start : start + reach + 1] = after_ref[0, layer_no, c, 0 : reach + 1]
            forcing[0][layer_no, c, rows - 8 : rows] = zeros
            forcing[0][layer_no, c, 0:reach] = before_ref[1, layer_no, c, side - reach : side]
            forcing[0][layer_no, c, reach : reach + own_rows] = own_ref[1, layer_no, c]
            start = reach + own_rows
            forcing[0][layer_no, c, start : start + reach] = after_ref[1, layer_no, c, 0:reach]

    pl.loop(0, layers)(assemble)

    def faces(layer_no, first):
        wests, souths, uppers = [], [], []
        cells = [density[layer_no, c, GUARD : GUARD + rows] for c in range(count[0])]
        southern = previous_of(cells, 1)
        for c in range(count[0]):
            wests.append(
                2.0
                * along_weight
                * ratio(
                    density[layer_no, c, GUARD : 2 * GUARD + rows],
                    density[layer_no, c, GUARD - 1 : 2 * GUARD + rows - 1],
                )
            )
            souths.append(2.0 * cross_weight * ratio(cells[c], southern[c]))
            if first:
                uppers.append(2.0 * vertical_weight * cells[c])
            else:
                uppers.append(
                    2.0
                    * vertical_weight
                    * ratio(cells[c], density[layer_no - 1, c, GUARD : GUARD + rows])
                )
        for m in range(levels):
            if m > 0:
                wests = paired(wests, spread[m - 1])
                souths = [0.5 * each for each in firsts(souths, spread[m - 1])]
                uppers = paired(uppers, spread[m - 1])
            for c in range(count[m]):
                west[m][layer_no, c] = wests[c]
                south[m][layer_no, c] = souths[c]
                upper[m][layer_no, c] = uppers[c]
            south[m][layer_no, count[m]] = pltpu.roll(souths[0], LANES - spread[m], 1)

    faces(0, True)
    pl.loop(1, layers)(lambda layer_no: faces(layer_no, False))
    for m in range(levels):
        for c in range(count[m]):
            upper[m][layers, c] = jnp.zeros((rows, LANES), jnp.float32)

    def clear_guards(layer_no):
        zeros = jnp.zeros((GUARD, LANES), jnp.float32)
        for m in range(levels):
            for c in range(count[m]):
                value[m][layer_no, c, 0:GUARD] = zeros
                value[m][layer_no, c, GUARD + rows : 2 * GUARD + rows] = zeros

    pl.loop(0, layers)(clear_guards)

    def pivots(layer_no, before, first):
        after = []
        for m in range(levels):
            for c in range(count[m]):
                above = upper[m][layer_no, c]
                centre = (
                    west[m][layer_no, c, 0:rows]
                    + west[m][layer_no, c, 1 : rows + 1]
                    + south[m][layer_no, c]
                    + south[m][layer_no, c + 1]
                    + above
                    + upper[m][layer_no + 1, c]
                )
                if m == 0:
                    centre0[layer_no, c] = centre[reach : reach + own_rows]
                if first:
                    pivot = centre
                else:
                    share = above * before[len(after)]
                    factor[m][layer_no, c] = share
                    pivot = centre - above * share
                inverted = reciprocal(jnp.maximum(pivot, TINY))
                inverse[m][layer_no, c] = relaxation * inverted
                after.append(inverted)
        return tuple(after)

    lax.fori_loop(1, layers, lambda z, before: pivots(z, before, False), pivots(0, None, True))

    def around(m, layer_no, low, high):
        cells = [value[m][layer_no, c, GUARD + low : GUARD + high] for c in range(count[m])]
        behind, ahead = previous_of(cells, spread[m]), next_of(cells, spread[m])
        out = []
        for c in range(count[m]):
            out.append(
                west[m][layer_no, c, low:high]
                * value[m][layer_no, c, GUARD + low - 1 : GUARD + high - 1]
                + west[m][layer_no, c, low + 1 : high + 1]
                * value[m][layer_no, c, GUARD + low + 1 : GUARD + high + 1]
                + south[m][layer_no, c, low:high] * behind[c]
                + south[m][layer_no, c + 1, low:high] * ahead[c]
            )
        return out

    def solve(m, low, high, right_side, held, offset, store):
        span = slice(offset + low, offset + high)

        def down(layer_no, before):
            now = right_side(layer_no)
            if before is not None:
                now = [
                    now[c] + factor[m][layer_no, c, low:high] * before[c] for c in range(count[m])
                ]
            for c in range(count[m]):
                held[layer_no, c, span] = now[c] * inverse[m][layer_no, c, low:high]
            return tuple(now)

        def up(step, below):
            layer_no = layers - 1 - step
            now = [held[layer_no, c, span] for c in range(count[m])]
            if below is not None:
                now = [
                    now[c] + factor[m][layer_no + 1, c, low:high] * below[c]
                    for c in range(count[m])
                ]
            store(layer_no, now)
            return tuple(now)

        lax.fori_loop(1, layers, down, down(0, None))
        lax.fori_loop(1, layers, up, up(0, None))

    def first_sweep(m):
        def right_side(layer_no):
            return [forcing[m][layer_no, c] for c in range(count[m])]

        def store(layer_no, now):
            for c in range(count[m]):
                value[m][layer_no, c, GUARD : GUARD + rows] = now[c]

        solve(m, 0, rows, right_side, value[m], GUARD, store)

    def later_sweep(m, low, high, prolong):
        def right_side(layer_no):
            flow = around(m, layer_no, low, high)
            return [forcing[m][layer_no, c, low:high] + flow[c] for c in range(count[m])]

        def store(layer_no, now):
            for c in range(count[m]):
                span = slice(GUARD + low, GUARD + high)
                new = (1.0 - relaxation) * value[m][layer_no, c, span] + now[c]
                value[m][layer_no, c, span] = new
                if prolong:
                    children = (2 * c, 2 * c + 1) if count[m - 1] > count[m] else (c,)
                    for child in children:
                        value[m - 1][layer_no, child, span] += new

        held = upright if m == coarsest else inverse[m]
        solve(m, low, high, right_side, held, 0, store)

    for m in range(coarsest):
        first_sweep(m)

        def restrict(layer_no, m=m):
            flow = around(m, layer_no, 0, rows)
            remain = [
                (1.0 - relaxation) * forcing[m][layer_no, c] + flow[c] for c in range(count[m])
            ]
            for c, each in enumerate(paired(remain, spread[m])):
                forcing[m + 1][layer_no, c] = each

        pl.loop(0, layers)(restrict)

    first_sweep(coarsest)
    for sweep_no in range(1, SWEEPS):
        later_sweep(coarsest, 0, rows, sweep_no == SWEEPS - 1)

    for m in range(coarsest - 1, -1, -1):
        low = (reach - m - 1) // 8 * 8
        high = rounded_up(reach + own_rows + m + 1, 8)
        later_sweep(m, low, high, m > 0)

    chunks = count[0]
    lane = lane_numbers(own_rows)

    def in_order(cells, tile_no):
        start = (plan.side_cols + tile_no * LANES) // chunks
        pick = start + lane // chunks
        out = jnp.take_along_axis(cells[0], pick, axis=1)
        for c in range(1, chunks):
            out = jnp.where(lane % chunks == c, jnp.take_along_axis(cells[c], pick, axis=1), out)
        return out

    def finish(layer_no, top, bottom):
        low, high = reach, reach + own_rows
        span = slice(GUARD + low, GUARD + high)
        flow = around(0, layer_no, low, high)
        cells, remains = [], []
        for c in range(chunks):
            now = value[0][layer_no, c, span]
            remain = forcing[0][layer_no, c, low:high] - centre0[layer_no, c] * now + flow[c]
            if not top:
                remain += upper[0][layer_no, c, low:high] * value[0][layer_no - 1, c, span]
            if not bottom:
                remain += upper[0][layer_no + 1, c, low:high] * value[0][layer_no + 1, c, span]
            cells.append(now)
            remains.append(remain)
        for tile_no in range(plan.own_cols // LANES):
            columns = slice(tile_no * LANES, (tile_no + 1) * LANES)
            pressure_ref[layer_no, :, columns] = in_order(cells, tile_no)
            residual_ref[layer_no, :, columns] = in_order(remains, tile_no)

    finish(0, True, False)
    pl.loop(1, layers - 1)(lambda layer_no: finish(layer_no, False, False))
    finish(layers - 1, False, True)


def per_device(source, inv_density):
    layers, rows, cols = source.shape
    plan = Plan(lax.axis_size("cross"), layers, rows, cols)
    levels = plan.coarsest + 1
    both = jnp.stack([inv_density, source])
    before, after = beside(both, "cross", 3, plan.side_cols)
    vmem = pl.BlockSpec(memory_space=pltpu.VMEM)
    window = pl.pallas_call(
        functools.partial(window_kernel, plan),
        out_shape=jax.ShapeDtypeStruct((2, layers, plan.chunks, rows, LANES), jnp.float32),
        in_specs=[vmem] * 3,
        out_specs=vmem,
        compiler_params=pltpu.CompilerParams(vmem_limit_bytes=48 << 20),
    )(both, before, after)
    before, after = beside(window, "along", 3, plan.side_rows)

    def room(*shape):
        return pltpu.VMEM(shape + (LANES,), jnp.float32)

    total, high = plan.rows, plan.rows + GUARD
    counts = [plan.level_chunks(m) for m in range(levels)]
    scratch = [
        room(layers, counts[-1], total),
        room(layers, counts[0], rows),
        room(layers + 1, counts[0], total),
    ]
    scratch += [room(layers, n, high) for n in counts]
    scratch += [room(layers, n + 1, total) for n in counts]
    scratch += [room(layers, n, total) for n in counts]
    scratch += [room(layers, n, total) for n in counts]
    scratch += [room(layers, n, high + GUARD) for n in counts]
    scratch += [room(layers, counts[0], total)]
    scratch += [room(layers + 1, n, total) for n in counts[1:]]
    held = sum(math.prod(each.shape) for each in scratch) + window.size + 2 * before.size
    held = 4 * (held + 2 * source.size)
    return pl.pallas_call(
        functools.partial(cycle_kernel, plan),
        out_shape=[jax.ShapeDtypeStruct((layers, rows, cols), jnp.float32)] * 2,
        in_specs=[vmem] * 3,
        out_specs=[vmem] * 2,
        scratch_shapes=scratch,
        compiler_params=pltpu.CompilerParams(vmem_limit_bytes=held + (2 << 20)),
    )(window, before, after)


def solution(mesh):
    return jax.shard_map(
        per_device,
        mesh=mesh,
        in_specs=(P(None, "along", "cross"), P(None, "along", "cross")),
        out_specs=(P(None, "along", "cross"), P(None, "along", "cross")),
        check_vma=False,
    )
```

profile of v0, /device:TPU:1, one launch (start us, length us, event | category | flops | bytes accessed | tf_op | source)
XLA Modules:
  0.0 69.7 jit_solution(17865389996873122355)
XLA Ops:
  0.6 0.0 copy-start
  0.6 0.0 copy-start.1
  0.6 1.2 %fusion.1 = (f32[2,16,16,128]{3,2,1,0:T(8,128)S(1)}, f32[2,16,16,128]{3,2,1,0:T(8,128)S(1)}) fusion(f32[1,16,16,256]{3,2,1,0:T(8,128)} %bitcast.4, f32[1,16,16,256]{3,2,1,0:T(8,128)} %bitcast.2), kind=kLoop, calls=%fused_computation.6 | loop fusion | flops 131072 | bytes 1048576 | tf_op jit(solution)/shard_map/stack | solution.py:386
  1.8 1.3 %collective-permute-start.1 = (f32[2,16,16,128]{3,2,1,0:T(8,128)S(1)}, f32[2,16,16,128]{3,2,1,0:T(8,128)S(1)}, u32[]{:S(2)}, u32[]{:S(2)}) collective-permute-start(f32[2,16,16,128]{3,2,1,0:T(8,128)S(1)} %get-tuple-element.2), channel_id=1, source_target_pairs={{4,0},{8,4},{12,8},{16,12},{20,16},{24,20},{28,24},{5,1},{9,5},{13... | collective-permute-start | bytes 786440 | tf_op jit(solution)/shard_map/ppermute | solution.py:30
  3.1 4.6 %collective-permute-start = (f32[2,16,16,128]{3,2,1,0:T(8,128)S(1)}, f32[2,16,16,128]{3,2,1,0:T(8,128)S(1)}, u32[]{:S(2)}, u32[]{:S(2)}) collective-permute-start(f32[2,16,16,128]{3,2,1,0:T(8,128)S(1)} %get-tuple-element.3), channel_id=1, source_target_pairs={{0,4},{4,8},{8,12},{12,16},{16,20},{20,24},{24,28},{1,5},{5,9},{9,... | collective-permute-start | bytes 786440 | tf_op jit(solution)/shard_map/ppermute | solution.py:30
  7.8 0.0 copy-done
  7.8 0.0 copy-done.1
  7.8 4.0 %collective-permute-done.1.after_ref = f32[2,16,16,128]{3,2,1,0:T(8,128)S(1)} collective-permute-done((f32[2,16,16,128]{3,2,1,0:T(8,128)S(1)}, f32[2,16,16,128]{3,2,1,0:T(8,128)S(1)}, u32[]{:S(2)}, u32[]{:S(2)}) %collective-permute-start.1) | collective-permute-done | bytes 262176 | tf_op jit(solution)/shard_map/ppermute | solution.py:30
  11.8 6.5 %collective-permute-done.before_ref = f32[2,16,16,128]{3,2,1,0:T(8,128)S(1)} collective-permute-done((f32[2,16,16,128]{3,2,1,0:T(8,128)S(1)}, f32[2,16,16,128]{3,2,1,0:T(8,128)S(1)}, u32[]{:S(2)}, u32[]{:S(2)}) %collective-permute-start) | collective-permute-done | bytes 262176 | tf_op jit(solution)/shard_map/ppermute | solution.py:30
  18.3 4.0 %shard_map.41.own_ref = f32[2,16,4,16,128]{4,3,2,1,0:T(8,128)S(1)} custom-call(f32[2,16,16,256]{3,2,1,0:T(8,128)S(1)} %pad_maximum_fusion.own_ref, f32[2,16,16,128]{3,2,1,0:T(8,128)S(1)} %collective-permute-done.before_ref, f32[2,16,16,128]{3,2,1,0:T(8,128)S(1)} %collective-permute-done.1.after_ref), custom_call_target="tpu_custom_call" | custom-call | tf_op jit(solution)/shard_map/pallas_call | solution.py:389
  22.4 2.4 %collective-permute-start.3 = (f32[2,16,4,16,128]{4,3,2,1,0:T(8,128)S(1)}, f32[2,16,4,16,128]{4,3,2,1,0:T(8,128)S(1)}, u32[]{:S(2)}, u32[]{:S(2)}) collective-permute-start(f32[2,16,4,16,128]{4,3,2,1,0:T(8,128)S(1)} %shard_map.41.own_ref), channel_id=1, source_target_pairs={{1,0},{2,1},{3,2},{5,4},{6,5},{7,6},{9,8},{10,9},{11,10},{13,12},{... | collective-permute-start | bytes 3145736 | tf_op jit(solution)/shard_map/ppermute | solution.py:30
  24.8 3.2 %collective-permute-start.2 = (f32[2,16,4,16,128]{4,3,2,1,0:T(8,128)S(1)}, f32[2,16,4,16,128]{4,3,2,1,0:T(8,128)S(1)}, u32[]{:S(2)}, u32[]{:S(2)}) collective-permute-start(f32[2,16,4,16,128]{4,3,2,1,0:T(8,128)S(1)} %shard_map.41.own_ref), channel_id=1, source_target_pairs={{0,1},{1,2},{2,3},{4,5},{5,6},{6,7},{8,9},{9,10},{10,11},{12,13},{... | collective-permute-start | bytes 3145736 | tf_op jit(solution)/shard_map/ppermute | solution.py:30
  28.0 10.5 %collective-permute-done.3.after_ref = f32[2,16,4,16,128]{4,3,2,1,0:T(8,128)S(1)} collective-permute-done((f32[2,16,4,16,128]{4,3,2,1,0:T(8,128)S(1)}, f32[2,16,4,16,128]{4,3,2,1,0:T(8,128)S(1)}, u32[]{:S(2)}, u32[]{:S(2)}) %collective-permute-start.3) | collective-permute-done | bytes 1048608 | tf_op jit(solution)/shard_map/ppermute | solution.py:30
  38.5 1.2 %collective-permute-done.2.before_ref = f32[2,16,4,16,128]{4,3,2,1,0:T(8,128)S(1)} collective-permute-done((f32[2,16,4,16,128]{4,3,2,1,0:T(8,128)S(1)}, f32[2,16,4,16,128]{4,3,2,1,0:T(8,128)S(1)}, u32[]{:S(2)}, u32[]{:S(2)}) %collective-permute-start.2) | collective-permute-done | bytes 1048608 | tf_op jit(solution)/shard_map/ppermute | solution.py:30
  39.7 30.0 %shard_map.42 = (f32[16,16,256]{2,1,0:T(8,128)}, f32[16,16,256]{2,1,0:T(8,128)}) custom-call(f32[2,16,4,16,128]{4,3,2,1,0:T(8,128)S(1)} %shard_map.41.own_ref, f32[2,16,4,16,128]{4,3,2,1,0:T(8,128)S(1)} %collective-permute-done.2.before_ref, f32[2,16,4,16,128]{4,3,2,1,0:T(8,128)S(1)} %collective-permute-done.3.after_ref), custom_call_target="tpu_custom_call" | custom-call | tf_op jit(solution)/shard_map/pallas_call | solution.py:417
  (1 shorter events, 0.0 us)
Async XLA Ops:
  0.6 7.1 %copy-start = (f32[16,16,256]{2,1,0:T(8,128)S(1)}, f32[16,16,256]{2,1,0:T(8,128)}, u32[]{:S(2)}) copy-start(f32[16,16,256]{2,1,0:T(8,128)} %param.2) | copy-start | bytes 786436
  0.6 7.1 %copy-start.1 = (f32[16,16,256]{2,1,0:T(8,128)S(1)}, f32[16,16,256]{2,1,0:T(8,128)}, u32[]{:S(2)}) copy-start(f32[16,16,256]{2,1,0:T(8,128)} %param.3) | copy-start | bytes 786436
  1.8 10.0 %collective-permute-start.1 = (f32[2,16,16,128]{3,2,1,0:T(8,128)S(1)}, f32[2,16,16,128]{3,2,1,0:T(8,128)S(1)}, u32[]{:S(2)}, u32[]{:S(2)}) collective-permute-start(f32[2,16,16,128]{3,2,1,0:T(8,128)S(1)} %get-tuple-element.2), channel_id=1, source_target_pairs={{4,0},{8,4},{12,8},{16,12},{20,16},{24,20},{28,24},{5,1},{9,5},{13... | collective-permute-start | bytes 786440 | tf_op jit(solution)/shard_map/ppermute | solution.py:30
  3.1 15.2 %collective-permute-start = (f32[2,16,16,128]{3,2,1,0:T(8,128)S(1)}, f32[2,16,16,128]{3,2,1,0:T(8,128)S(1)}, u32[]{:S(2)}, u32[]{:S(2)}) collective-permute-start(f32[2,16,16,128]{3,2,1,0:T(8,128)S(1)} %get-tuple-element.3), channel_id=1, source_target_pairs={{0,4},{4,8},{8,12},{12,16},{16,20},{20,24},{24,28},{1,5},{5,9},{9,... | collective-permute-start | bytes 786440 | tf_op jit(solution)/shard_map/ppermute | solution.py:30
  22.4 16.1 %collective-permute-start.3 = (f32[2,16,4,16,128]{4,3,2,1,0:T(8,128)S(1)}, f32[2,16,4,16,128]{4,3,2,1,0:T(8,128)S(1)}, u32[]{:S(2)}, u32[]{:S(2)}) collective-permute-start(f32[2,16,4,16,128]{4,3,2,1,0:T(8,128)S(1)} %shard_map.41.own_ref), channel_id=1, source_target_pairs={{1,0},{2,1},{3,2},{5,4},{6,5},{7,6},{9,8},{10,9},{11,10},{13,12},{... | collective-permute-start | bytes 3145736 | tf_op jit(solution)/shard_map/ppermute | solution.py:30
  24.8 14.9 %collective-permute-start.2 = (f32[2,16,4,16,128]{4,3,2,1,0:T(8,128)S(1)}, f32[2,16,4,16,128]{4,3,2,1,0:T(8,128)S(1)}, u32[]{:S(2)}, u32[]{:S(2)}) collective-permute-start(f32[2,16,4,16,128]{4,3,2,1,0:T(8,128)S(1)} %shard_map.41.own_ref), channel_id=1, source_target_pairs={{0,1},{1,2},{2,3},{4,5},{5,6},{6,7},{8,9},{9,10},{10,11},{12,13},{... | collective-permute-start | bytes 3145736 | tf_op jit(solution)/shard_map/ppermute | solution.py:30
where the time goes:
time: 70.7 us; the launch traced here: 69.7 us
  Pallas kernels  34 us (48%)
  waiting for transfers between devices  22.2 us (31%)
  starting transfers between devices  11.5 us (16%)
  other arithmetic  1.22 us (2%)
  between operations  0.71 us (1%)
    pallas_call x1, Pallas kernels, per_device(): pl.pallas_call(functools.partial(cycle_kernel, plan), out_shape=[jax.Shap...  30 us
    ppermute x4, waiting for transfers between devices, shifted(): return lax.ppermute(array, axis, pairs)  22.2 us
    ppermute x4, starting transfers between devices, shifted(): return lax.ppermute(array, axis, pairs)  11.5 us
    pallas_call x1, Pallas kernels, per_device(): pl.pallas_call(functools.partial(window_kernel, plan), out_shape=jax.Shap...  4.03 us
  transfers between devices with their start and end apart: 4, of which 4 were waited for; matrix products, arithmetic and copies ran while one was open for 0% of the time, Pallas kernels for 0%

commit v1 on v0

--- a/solution.py
+++ b/solution.py
@@ -75,6 +75,10 @@
     return lax.broadcasted_iota(jnp.int32, (rows, LANES), 1)
 
 
+def taken(value, pick):
+    return jnp.take_along_axis(value, pick, axis=1, mode="promise_in_bounds")
+
+
 def window_kernel(plan, own_ref, before_ref, after_ref, out_ref):
     chunks, rows = plan.chunks, plan.own_rows
     lane = lane_numbers(rows)
@@ -87,14 +91,14 @@
             for first in range(0, ref.shape[3], LANES):
                 tiles.append(ref[which, layer_no, :, first : first + LANES])
         for chunk in range(chunks):
-            value = jnp.take_along_axis(tiles[0], picks[chunk], axis=1)
+            value = taken(tiles[0], picks[chunk])
             for tile_no in range(1, chunks):
-                other = jnp.take_along_axis(tiles[tile_no], picks[chunk], axis=1)
+                other = taken(tiles[tile_no], picks[chunk])
                 value = jnp.where(part == tile_no, other, value)
             out_ref[which, layer_no, chunk] = value
 
     for which in range(2):
-        pl.loop(0, plan.layers)(functools.partial(layer_step, which))
+        pl.loop(0, plan.layers, unroll=4)(functools.partial(layer_step, which))
 
 
 def reciprocal(value):
@@ -116,7 +120,7 @@
 
 def first_of_pair(value, spread):
     lane = lane_numbers(value.shape[0])
-    return (lane // spread) % 2 == 0
+    return (lane & spread) == 0
 
 
 def paired(cells, spread):
@@ -144,8 +148,8 @@
     layers, rows = plan.layers, plan.rows
     reach, own_rows = plan.row_reach, plan.own_rows
     scratch = list(scratch)
-    upright, centre0, upper0 = scratch[:3]
-    rest = scratch[3:]
+    upright, centre0, upper0, origin = scratch[:4]
+    rest = scratch[4:]
     west, south, factor, inverse, value, forcing = [
         rest[i * levels : (i + 1) * levels] for i in range(6)
     ]
@@ -154,6 +158,14 @@
     count = [plan.level_chunks(m) for m in range(levels)]
     spread = [plan.spread(m) for m in range(levels)]
 
+    origin[0] = 0
+    start0 = origin[0]
+
+    def span(low, high):
+        if low % 8 == 0 and high % 8 == 0:
+            return pl.ds(low, high - low)
+        return pl.ds(start0 + low, high - low)
+
     side = before_ref.shape[3]
 
     def assemble(layer_no):
@@ -162,19 +174,23 @@
             density[layer_no, c, 0:GUARD] = zeros
             tail = rounded_up(GUARD + reach + own_rows + reach + 1, 8)
             density[layer_no, c, tail - 8 : tail] = zeros
-            density[layer_no, c, GUARD - 1 : GUARD + reach] = before_ref[
-                0, layer_no, c, side - reach - 1 : side
+            density[layer_no, c, span(GUARD - 1, GUARD + reach)] = before_ref[
+                0, layer_no, c, span(side - reach - 1, side)
             ]
-            density[layer_no, c, GUARD + reach : GUARD + reach + own_rows] = own_ref[0, layer_no, c]
+            density[layer_no, c, span(GUARD + reach, GUARD + reach + own_rows)] = own_ref[0, layer_no, c]
             start = GUARD + reach + own_rows
-            density[layer_no, c, start : start + reach + 1] = after_ref[0, layer_no, c, 0 : reach + 1]
+            density[layer_no, c, span(start, start + reach + 1)] = after_ref[
+                0, layer_no, c, span(0, reach + 1)
+            ]
             forcing[0][layer_no, c, rows - 8 : rows] = zeros
-            forcing[0][layer_no, c, 0:reach] = before_ref[1, layer_no, c, side - reach : side]
-            forcing[0][layer_no, c, reach : reach + own_rows] = own_ref[1, layer_no, c]
+            forcing[0][layer_no, c, span(0, reach)] = before_ref[1, layer_no, c, span(side - reach, side)]
+            forcing[0][layer_no, c, span(reach, reach + own_rows)] = own_ref[1, layer_no, c]
             start = reach + own_rows
-            forcing[0][layer_no, c, start : start + reach] = after_ref[1, layer_no, c, 0:reach]
-
-    pl.loop(0, layers)(assemble)
+            forcing[0][layer_no, c, span(start, start + reach)] = after_ref[
+                1, layer_no, c, span(0, reach)
+            ]
+
+    pl.loop(0, layers, unroll=2)(assemble)
 
     def faces(layer_no, first):
         wests, souths, uppers = [], [], []
@@ -186,7 +202,7 @@
                 * along_weight
                 * ratio(
                     density[layer_no, c, GUARD : 2 * GUARD + rows],
-                    density[layer_no, c, GUARD - 1 : 2 * GUARD + rows - 1],
+                    density[layer_no, c, span(GUARD - 1, 2 * GUARD + rows - 1)],
                 )
             )
             souths.append(2.0 * cross_weight * ratio(cells[c], southern[c]))
@@ -210,7 +226,7 @@
             south[m][layer_no, count[m]] = pltpu.roll(souths[0], LANES - spread[m], 1)
 
     faces(0, True)
-    pl.loop(1, layers)(lambda layer_no: faces(layer_no, False))
+    pl.loop(1, layers, unroll=3)(lambda layer_no: faces(layer_no, False))
     for m in range(levels):
         for c in range(count[m]):
             upper[m][layers, c] = jnp.zeros((rows, LANES), jnp.float32)
@@ -222,7 +238,7 @@
                 value[m][layer_no, c, 0:GUARD] = zeros
                 value[m][layer_no, c, GUARD + rows : 2 * GUARD + rows] = zeros
 
-    pl.loop(0, layers)(clear_guards)
+    pl.loop(0, layers, unroll=4)(clear_guards)
 
     def pivots(layer_no, before, first):
         after = []
@@ -231,14 +247,14 @@
                 above = upper[m][layer_no, c]
                 centre = (
                     west[m][layer_no, c, 0:rows]
-                    + west[m][layer_no, c, 1 : rows + 1]
+                    + west[m][layer_no, c, span(1, rows + 1)]
                     + south[m][layer_no, c]
                     + south[m][layer_no, c + 1]
                     + above
                     + upper[m][layer_no + 1, c]
                 )
                 if m == 0:
-                    centre0[layer_no, c] = centre[reach : reach + own_rows]
+                    centre0[layer_no, c] = centre
                 if first:
                     pivot = centre
                 else:
@@ -250,25 +266,27 @@
                 after.append(inverted)
         return tuple(after)
 
-    lax.fori_loop(1, layers, lambda z, before: pivots(z, before, False), pivots(0, None, True))
+    lax.fori_loop(
+        1, layers, lambda z, before: pivots(z, before, False), pivots(0, None, True), unroll=3
+    )
 
     def around(m, layer_no, low, high):
-        cells = [value[m][layer_no, c, GUARD + low : GUARD + high] for c in range(count[m])]
+        cells = [value[m][layer_no, c, span(GUARD + low, GUARD + high)] for c in range(count[m])]
         behind, ahead = previous_of(cells, spread[m]), next_of(cells, spread[m])
         out = []
         for c in range(count[m]):
             out.append(
-                west[m][layer_no, c, low:high]
-                * value[m][layer_no, c, GUARD + low - 1 : GUARD + high - 1]
-                + west[m][layer_no, c, low + 1 : high + 1]
-                * value[m][layer_no, c, GUARD + low + 1 : GUARD + high + 1]
-                + south[m][layer_no, c, low:high] * behind[c]
-                + south[m][layer_no, c + 1, low:high] * ahead[c]
+                west[m][layer_no, c, span(low, high)]
+                * value[m][layer_no, c, span(GUARD + low - 1, GUARD + high - 1)]
+                + west[m][layer_no, c, span(low + 1, high + 1)]
+                * value[m][layer_no, c, span(GUARD + low + 1, GUARD + high + 1)]
+                + south[m][layer_no, c, span(low, high)] * behind[c]
+                + south[m][layer_no, c + 1, span(low, high)] * ahead[c]
             )
         return out
 
     def solve(m, low, high, right_side, held, offset, store):
-        span = slice(offset + low, offset + high)
+        place = slice(offset + low, offset + high)
 
         def down(layer_no, before):
             now = right_side(layer_no)
@@ -277,12 +295,12 @@
                     now[c] + factor[m][layer_no, c, low:high] * before[c] for c in range(count[m])
                 ]
             for c in range(count[m]):
-                held[layer_no, c, span] = now[c] * inverse[m][layer_no, c, low:high]
+                held[layer_no, c, place] = now[c] * inverse[m][layer_no, c, low:high]
             return tuple(now)
 
         def up(step, below):
             layer_no = layers - 1 - step
-            now = [held[layer_no, c, span] for c in range(count[m])]
+            now = [held[layer_no, c, place] for c in range(count[m])]
             if below is not None:
                 now = [
                     now[c] + factor[m][layer_no + 1, c, low:high] * below[c]
@@ -291,8 +309,12 @@
             store(layer_no, now)
             return tuple(now)
 
-        lax.fori_loop(1, layers, down, down(0, None))
-        lax.fori_loop(1, layers, up, up(0, None))
+        now = None
+        for layer_no in range(layers):
+            now = down(layer_no, now)
+        now = None
+        for step in range(layers):
+            now = up(step, now)
 
     def first_sweep(m):
         def right_side(layer_no):
@@ -311,13 +333,13 @@
 
         def store(layer_no, now):
             for c in range(count[m]):
-                span = slice(GUARD + low, GUARD + high)
-                new = (1.0 - relaxation) * value[m][layer_no, c, span] + now[c]
-                value[m][layer_no, c, span] = new
+                place = slice(GUARD + low, GUARD + high)
+                new = (1.0 - relaxation) * value[m][layer_no, c, place] + now[c]
+                value[m][layer_no, c, place] = new
                 if prolong:
                     children = (2 * c, 2 * c + 1) if count[m - 1] > count[m] else (c,)
                     for child in children:
-                        value[m - 1][layer_no, child, span] += new
+                        value[m - 1][layer_no, child, place] += new
 
         held = upright if m == coarsest else inverse[m]
         solve(m, low, high, right_side, held, 0, store)
@@ -333,7 +355,7 @@
             for c, each in enumerate(paired(remain, spread[m])):
                 forcing[m + 1][layer_no, c] = each
 
-        pl.loop(0, layers)(restrict)
+        pl.loop(0, layers, unroll=layers if count[m] == 1 else 4)(restrict)
 
     first_sweep(coarsest)
     for sweep_no in range(1, SWEEPS):
@@ -350,23 +372,24 @@
     def in_order(cells, tile_no):
         start = (plan.side_cols + tile_no * LANES) // chunks
         pick = start + lane // chunks
-        out = jnp.take_along_axis(cells[0], pick, axis=1)
+        out = taken(cells[0], pick)
         for c in range(1, chunks):
-            out = jnp.where(lane % chunks == c, jnp.take_along_axis(cells[c], pick, axis=1), out)
+            out = jnp.where(lane % chunks == c, taken(cells[c], pick), out)
         return out
 
     def finish(layer_no, top, bottom):
         low, high = reach, reach + own_rows
-        span = slice(GUARD + low, GUARD + high)
+        own = span(GUARD + low, GUARD + high)
+        plain = span(low, high)
         flow = around(0, layer_no, low, high)
         cells, remains = [], []
         for c in range(chunks):
-            now = value[0][layer_no, c, span]
-            remain = forcing[0][layer_no, c, low:high] - centre0[layer_no, c] * now + flow[c]
+            now = value[0][layer_no, c, own]
+            remain = forcing[0][layer_no, c, plain] - centre0[layer_no, c, plain] * now + flow[c]
             if not top:
-                remain += upper[0][layer_no, c, low:high] * value[0][layer_no - 1, c, span]
+                remain += upper[0][layer_no, c, plain] * value[0][layer_no - 1, c, own]
             if not bottom:
-                remain += upper[0][layer_no + 1, c, low:high] * value[0][layer_no + 1, c, span]
+                remain += upper[0][layer_no + 1, c, plain] * value[0][layer_no + 1, c, own]
             cells.append(now)
             remains.append(remain)
         for tile_no in range(plan.own_cols // LANES):
@@ -375,7 +398,7 @@
             residual_ref[layer_no, :, columns] = in_order(remains, tile_no)
 
     finish(0, True, False)
-    pl.loop(1, layers - 1)(lambda layer_no: finish(layer_no, False, False))
+    pl.loop(1, layers - 1, unroll=2)(lambda layer_no: finish(layer_no, False, False))
     finish(layers - 1, False, True)
 
 
@@ -402,8 +425,9 @@
     counts = [plan.level_chunks(m) for m in range(levels)]
     scratch = [
         room(layers, counts[-1], total),
-        room(layers, counts[0], rows),
+        room(layers, counts[0], total),
         room(layers + 1, counts[0], total),
+        pltpu.SMEM((1,), jnp.int32),
     ]
     scratch += [room(layers, n, high) for n in counts]
     scratch += [room(layers, n + 1, total) for n in counts]

time: 70.7 us -> 52.5 us (0.74)
  the two profiles are of different devices: /device:TPU:1 before, /device:TPU:6 now
where the time goes in v1:
time: 52.5 us; the launch traced here: 52.3 us
  waiting for transfers between devices  23.4 us (45%)
  Pallas kernels  15.8 us (30%)
  starting transfers between devices  11.1 us (21%)
  other arithmetic  1.22 us (2%)
  between operations  0.71 us (1%)
    ppermute x4, waiting for transfers between devices, shifted(): return lax.ppermute(array, axis, pairs)  23.4 us
    pallas_call x1, Pallas kernels, per_device(): pl.pallas_call(functools.partial(cycle_kernel, plan), out_shape=[jax.Shap...  13.7 us
    ppermute x4, starting transfers between devices, shifted(): return lax.ppermute(array, axis, pairs)  11.1 us
    pallas_call x1, Pallas kernels, per_device(): pl.pallas_call(functools.partial(window_kernel, plan), out_shape=jax.Shap...  2.12 us
    another operation x2, other arithmetic, per_device(): both = jnp.stack([inv_density, source])  1.22 us
  transfers between devices with their start and end apart: 4, of which 4 were waited for; matrix products, arithmetic and copies ran while one was open for 0% of the time, Pallas kernels for 0%

profile of v1, /device:TPU:6, one launch (start us, length us, event | category | flops | bytes accessed | tf_op | source)
XLA Modules:
  0.0 52.3 jit_solution(7672819876022658814)
XLA Ops:
  0.6 0.0 copy-start
  0.6 0.0 copy-start.1
  0.6 1.2 %fusion.1 = (f32[2,16,16,128]{3,2,1,0:T(8,128)S(1)}, f32[2,16,16,128]{3,2,1,0:T(8,128)S(1)}) fusion(f32[1,16,16,256]{3,2,1,0:T(8,128)} %bitcast.4, f32[1,16,16,256]{3,2,1,0:T(8,128)} %bitcast.2), kind=kLoop, calls=%fused_computation.6 | loop fusion | flops 131072 | bytes 1048576 | tf_op jit(solution)/shard_map/stack | solution.py:409
  1.8 2.4 %collective-permute-start.1 = (f32[2,16,16,128]{3,2,1,0:T(8,128)S(1)}, f32[2,16,16,128]{3,2,1,0:T(8,128)S(1)}, u32[]{:S(2)}, u32[]{:S(2)}) collective-permute-start(f32[2,16,16,128]{3,2,1,0:T(8,128)S(1)} %get-tuple-element.2), channel_id=1, source_target_pairs={{4,0},{8,4},{12,8},{16,12},{20,16},{24,20},{28,24},{5,1},{9,5},{13... | collective-permute-start | bytes 786440 | tf_op jit(solution)/shard_map/ppermute | solution.py:30
  4.3 4.3 %collective-permute-start = (f32[2,16,16,128]{3,2,1,0:T(8,128)S(1)}, f32[2,16,16,128]{3,2,1,0:T(8,128)S(1)}, u32[]{:S(2)}, u32[]{:S(2)}) collective-permute-start(f32[2,16,16,128]{3,2,1,0:T(8,128)S(1)} %get-tuple-element.3), channel_id=1, source_target_pairs={{0,4},{4,8},{8,12},{12,16},{16,20},{20,24},{24,28},{1,5},{5,9},{9,... | collective-permute-start | bytes 786440 | tf_op jit(solution)/shard_map/ppermute | solution.py:30
  8.6 0.0 copy-done
  8.6 0.0 copy-done.1
  8.7 4.1 %collective-permute-done.1.after_ref = f32[2,16,16,128]{3,2,1,0:T(8,128)S(1)} collective-permute-done((f32[2,16,16,128]{3,2,1,0:T(8,128)S(1)}, f32[2,16,16,128]{3,2,1,0:T(8,128)S(1)}, u32[]{:S(2)}, u32[]{:S(2)}) %collective-permute-start.1) | collective-permute-done | bytes 262176 | tf_op jit(solution)/shard_map/ppermute | solution.py:30
  12.8 5.5 %collective-permute-done.before_ref = f32[2,16,16,128]{3,2,1,0:T(8,128)S(1)} collective-permute-done((f32[2,16,16,128]{3,2,1,0:T(8,128)S(1)}, f32[2,16,16,128]{3,2,1,0:T(8,128)S(1)}, u32[]{:S(2)}, u32[]{:S(2)}) %collective-permute-start) | collective-permute-done | bytes 262176 | tf_op jit(solution)/shard_map/ppermute | solution.py:30
  18.3 2.1 %shard_map.41.own_ref = f32[2,16,4,16,128]{4,3,2,1,0:T(8,128)S(1)} custom-call(f32[2,16,16,256]{3,2,1,0:T(8,128)S(1)} %pad_maximum_fusion.own_ref, f32[2,16,16,128]{3,2,1,0:T(8,128)S(1)} %collective-permute-done.before_ref, f32[2,16,16,128]{3,2,1,0:T(8,128)S(1)} %collective-permute-done.1.after_ref), custom_call_target="tpu_custom_call" | custom-call | tf_op jit(solution)/shard_map/pallas_call | solution.py:412
  20.4 2.1 %collective-permute-start.3 = (f32[2,16,4,16,128]{4,3,2,1,0:T(8,128)S(1)}, f32[2,16,4,16,128]{4,3,2,1,0:T(8,128)S(1)}, u32[]{:S(2)}, u32[]{:S(2)}) collective-permute-start(f32[2,16,4,16,128]{4,3,2,1,0:T(8,128)S(1)} %shard_map.41.own_ref), channel_id=1, source_target_pairs={{1,0},{2,1},{3,2},{5,4},{6,5},{7,6},{9,8},{10,9},{11,10},{13,12},{... | collective-permute-start | bytes 3145736 | tf_op jit(solution)/shard_map/ppermute | solution.py:30
  22.5 2.3 %collective-permute-start.2 = (f32[2,16,4,16,128]{4,3,2,1,0:T(8,128)S(1)}, f32[2,16,4,16,128]{4,3,2,1,0:T(8,128)S(1)}, u32[]{:S(2)}, u32[]{:S(2)}) collective-permute-start(f32[2,16,4,16,128]{4,3,2,1,0:T(8,128)S(1)} %shard_map.41.own_ref), channel_id=1, source_target_pairs={{0,1},{1,2},{2,3},{4,5},{5,6},{6,7},{8,9},{9,10},{10,11},{12,13},{... | collective-permute-start | bytes 3145736 | tf_op jit(solution)/shard_map/ppermute | solution.py:30
  24.8 10.0 %collective-permute-done.3.after_ref = f32[2,16,4,16,128]{4,3,2,1,0:T(8,128)S(1)} collective-permute-done((f32[2,16,4,16,128]{4,3,2,1,0:T(8,128)S(1)}, f32[2,16,4,16,128]{4,3,2,1,0:T(8,128)S(1)}, u32[]{:S(2)}, u32[]{:S(2)}) %collective-permute-start.3) | collective-permute-done | bytes 1048608 | tf_op jit(solution)/shard_map/ppermute | solution.py:30
  34.8 3.8 %collective-permute-done.2.before_ref = f32[2,16,4,16,128]{4,3,2,1,0:T(8,128)S(1)} collective-permute-done((f32[2,16,4,16,128]{4,3,2,1,0:T(8,128)S(1)}, f32[2,16,4,16,128]{4,3,2,1,0:T(8,128)S(1)}, u32[]{:S(2)}, u32[]{:S(2)}) %collective-permute-start.2) | collective-permute-done | bytes 1048608 | tf_op jit(solution)/shard_map/ppermute | solution.py:30
  38.6 13.7 %shard_map.42 = (f32[16,16,256]{2,1,0:T(8,128)}, f32[16,16,256]{2,1,0:T(8,128)}) custom-call(f32[2,16,4,16,128]{4,3,2,1,0:T(8,128)S(1)} %shard_map.41.own_ref, f32[2,16,4,16,128]{4,3,2,1,0:T(8,128)S(1)} %collective-permute-done.2.before_ref, f32[2,16,4,16,128]{4,3,2,1,0:T(8,128)S(1)} %collective-permute-done.3.after_ref), custom_call_target="tpu_custom_call" | custom-call | tf_op jit(solution)/shard_map/pallas_call | solution.py:441
  (1 shorter events, 0.0 us)
Async XLA Ops:
  0.6 8.0 %copy-start = (f32[16,16,256]{2,1,0:T(8,128)S(1)}, f32[16,16,256]{2,1,0:T(8,128)}, u32[]{:S(2)}) copy-start(f32[16,16,256]{2,1,0:T(8,128)} %param.2) | copy-start | bytes 786436
  0.6 8.0 %copy-start.1 = (f32[16,16,256]{2,1,0:T(8,128)S(1)}, f32[16,16,256]{2,1,0:T(8,128)}, u32[]{:S(2)}) copy-start(f32[16,16,256]{2,1,0:T(8,128)} %param.3) | copy-start | bytes 786436
  1.8 10.9 %collective-permute-start.1 = (f32[2,16,16,128]{3,2,1,0:T(8,128)S(1)}, f32[2,16,16,128]{3,2,1,0:T(8,128)S(1)}, u32[]{:S(2)}, u32[]{:S(2)}) collective-permute-start(f32[2,16,16,128]{3,2,1,0:T(8,128)S(1)} %get-tuple-element.2), channel_id=1, source_target_pairs={{4,0},{8,4},{12,8},{16,12},{20,16},{24,20},{28,24},{5,1},{9,5},{13... | collective-permute-start | bytes 786440 | tf_op jit(solution)/shard_map/ppermute | solution.py:30
  4.3 14.0 %collective-permute-start = (f32[2,16,16,128]{3,2,1,0:T(8,128)S(1)}, f32[2,16,16,128]{3,2,1,0:T(8,128)S(1)}, u32[]{:S(2)}, u32[]{:S(2)}) collective-permute-start(f32[2,16,16,128]{3,2,1,0:T(8,128)S(1)} %get-tuple-element.3), channel_id=1, source_target_pairs={{0,4},{4,8},{8,12},{12,16},{16,20},{20,24},{24,28},{1,5},{5,9},{9,... | collective-permute-start | bytes 786440 | tf_op jit(solution)/shard_map/ppermute | solution.py:30
  20.4 14.4 %collective-permute-start.3 = (f32[2,16,4,16,128]{4,3,2,1,0:T(8,128)S(1)}, f32[2,16,4,16,128]{4,3,2,1,0:T(8,128)S(1)}, u32[]{:S(2)}, u32[]{:S(2)}) collective-permute-start(f32[2,16,4,16,128]{4,3,2,1,0:T(8,128)S(1)} %shard_map.41.own_ref), channel_id=1, source_target_pairs={{1,0},{2,1},{3,2},{5,4},{6,5},{7,6},{9,8},{10,9},{11,10},{13,12},{... | collective-permute-start | bytes 3145736 | tf_op jit(solution)/shard_map/ppermute | solution.py:30
  22.5 16.1 %collective-permute-start.2 = (f32[2,16,4,16,128]{4,3,2,1,0:T(8,128)S(1)}, f32[2,16,4,16,128]{4,3,2,1,0:T(8,128)S(1)}, u32[]{:S(2)}, u32[]{:S(2)}) collective-permute-start(f32[2,16,4,16,128]{4,3,2,1,0:T(8,128)S(1)} %shard_map.41.own_ref), channel_id=1, source_target_pairs={{0,1},{1,2},{2,3},{4,5},{5,6},{6,7},{8,9},{9,10},{10,11},{12,13},{... | collective-permute-start | bytes 3145736 | tf_op jit(solution)/shard_map/ppermute | solution.py:30

commit v2 on v1

--- a/solution.py
+++ b/solution.py
@@ -30,21 +30,37 @@
     return lax.ppermute(array, axis, pairs)
 
 
-def beside(block, axis, dim, width):
-    size = block.shape[dim]
-    before, after = [], []
-    hop = 1
-    while width > 0:
-        take = min(width, size)
-        tail = lax.slice_in_dim(block, size - take, size, axis=dim)
-        head = lax.slice_in_dim(block, 0, take, axis=dim)
-        before.insert(0, shifted(tail, axis, hop))
-        after.append(shifted(head, axis, -hop))
-        width -= take
-        hop += 1
-    if len(before) == 1:
-        return before[0], after[0]
-    return jnp.concatenate(before, dim), jnp.concatenate(after, dim)
+def runs_of(first, count, widest):
+    runs, last = [], first + count
+    while first < last:
+        run = widest
+        while first % run or first + run > last:
+            run //= 2
+        runs.append((first, run))
+        first += run
+    return runs
+
+
+class Packing:
+    def __init__(self, layers, widest, parts):
+        self.pieces, self.size = [], 0
+        for which, first, count in parts:
+            for start, run in runs_of(first, count, widest):
+                share = widest // run
+                self.pieces.append((which, start, run, share, self.size))
+                self.size += layers // share
+
+    def place(self, piece, layer_no):
+        which, start, run, share, base = piece
+        return base + layer_no // share, layer_no % share * run
+
+
+def hops_of(size, reach):
+    hops = []
+    while reach > 0:
+        hops.append(min(size, reach))
+        reach -= hops[-1]
+    return hops
 
 
 class Plan:
@@ -62,7 +78,18 @@
         self.chunks = chunks
         self.side_cols = (chunks * LANES - cols) // 2
         self.rows = rounded_up(rows + 2 * self.row_reach, 8)
-        self.side_rows = rounded_up(self.row_reach + 1, 8)
+        self.cross_hops = hops_of(cols, rounded_up(self.col_reach, chunks))
+        self.cross_tails = [
+            Packing(layers, LANES, [(0, cols - n, n), (1, cols - n, n)]) for n in self.cross_hops
+        ]
+        self.cross_heads = [Packing(layers, LANES, [(0, 0, n), (1, 0, n)]) for n in self.cross_hops]
+        dense, plain = hops_of(rows, self.row_reach + 1), hops_of(rows, self.row_reach)
+        plain += [0] * (len(dense) - len(plain))
+        self.along_hops = list(zip(dense, plain))
+        self.along_tails = [
+            Packing(layers, 8, [(0, rows - n, n), (1, rows - k, k)]) for n, k in self.along_hops
+        ]
+        self.along_heads = [Packing(layers, 8, [(0, 0, n), (1, 0, k)]) for n, k in self.along_hops]
 
     def level_chunks(self, level_no):
         return max(1, self.chunks >> level_no)
@@ -79,26 +106,62 @@
     return jnp.take_along_axis(value, pick, axis=1, mode="promise_in_bounds")
 
 
-def window_kernel(plan, own_ref, before_ref, after_ref, out_ref):
-    chunks, rows = plan.chunks, plan.own_rows
+def edge_kernel(plan, density_ref, source_ref, *out_refs):
+    lane = lane_numbers(plan.own_rows)
+    arrays = (density_ref, source_ref)
+    for packing, out_ref in zip(plan.cross_tails + plan.cross_heads, out_refs):
+        for piece in packing.pieces:
+            which, start, run, share, _ = piece
+            tile = slice(start // LANES * LANES, start // LANES * LANES + LANES)
+            for first in range(0, plan.layers, share):
+                value = None
+                for layer_no in range(first, first + share):
+                    row, offset = packing.place(piece, layer_no)
+                    each = arrays[which][layer_no, :, tile]
+                    turn = (offset - start) % LANES
+                    if turn:
+                        each = pltpu.roll(each, turn, 1)
+                    value = each if value is None else jnp.where(lane >= offset, each, value)
+                out_ref[row] = value
+
+
+def window_kernel(plan, density_ref, source_ref, *refs):
+    hops = len(plan.cross_hops)
+    before_refs, after_refs = refs[:hops], refs[hops : 2 * hops]
+    out_ref, send_refs = refs[2 * hops], refs[2 * hops + 1 :]
+    chunks, rows, cols = plan.chunks, plan.own_rows, plan.own_cols
     lane = lane_numbers(rows)
-    picks = [(chunks * lane + chunk) % LANES for chunk in range(chunks)]
-    part = lane // (LANES // chunks)
-
-    def layer_step(which, layer_no):
-        tiles = []
-        for ref in (before_ref, own_ref, after_ref):
-            for first in range(0, ref.shape[3], LANES):
-                tiles.append(ref[which, layer_no, :, first : first + LANES])
-        for chunk in range(chunks):
-            value = taken(tiles[0], picks[chunk])
-            for tile_no in range(1, chunks):
-                other = taken(tiles[tile_no], picks[chunk])
-                value = jnp.where(part == tile_no, other, value)
-            out_ref[which, layer_no, chunk] = value
-
-    for which in range(2):
-        pl.loop(0, plan.layers, unroll=4)(functools.partial(layer_step, which))
+    own_first = plan.side_cols
+    for which, own_ref in enumerate((density_ref, source_ref)):
+        for layer_no in range(plan.layers):
+            sources = []
+            for start in range(0, cols, LANES):
+                sources.append(
+                    (own_first + start, LANES, own_ref[layer_no, :, start : start + LANES], 0)
+                )
+            for refs_of, packings, side in (
+                (before_refs, plan.cross_tails, -1),
+                (after_refs, plan.cross_heads, 1),
+            ):
+                for hop in range(hops):
+                    block = own_first + side * (hop + 1) * cols
+                    for piece in packings[hop].pieces:
+                        if piece[0] == which:
+                            row, offset = packings[hop].place(piece, layer_no)
+                            sources.append((block + piece[1], piece[2], refs_of[hop][row], offset))
+            for chunk in range(chunks):
+                value = jnp.zeros((rows, LANES), jnp.float32)
+                for first, count, cells, offset in sources:
+                    pick = (chunks * lane + (chunk - first + offset)) & (LANES - 1)
+                    inside = (lane >= first // chunks) & (lane < (first + count) // chunks)
+                    value = jnp.where(inside, taken(cells, pick), value)
+                out_ref[which, layer_no, chunk] = value
+                for packing, send_ref in zip(plan.along_tails + plan.along_heads, send_refs):
+                    for piece in packing.pieces:
+                        if piece[0] == which:
+                            start, run = piece[1], piece[2]
+                            tile, offset = packing.place(piece, layer_no)
+                            send_ref[tile, chunk, offset : offset + run] = value[start : start + run]
 
 
 def reciprocal(value):
@@ -127,12 +190,7 @@
     if len(cells) > 1:
         return [cells[2 * k] + cells[2 * k + 1] for k in range(len(cells) // 2)]
     value = cells[0]
-    other = jnp.where(
-        first_of_pair(value, spread),
-        pltpu.roll(value, LANES - spread, 1),
-        pltpu.roll(value, spread, 1),
-    )
-    return [value + other]
+    return [value + taken(value, lane_numbers(value.shape[0]) ^ spread)]
 
 
 def firsts(cells, spread):
@@ -142,7 +200,11 @@
     return [jnp.where(first_of_pair(value, spread), value, pltpu.roll(value, spread, 1))]
 
 
-def cycle_kernel(plan, own_ref, before_ref, after_ref, pressure_ref, residual_ref, *scratch):
+def cycle_kernel(plan, own_ref, *refs):
+    hops = len(plan.along_hops)
+    before_refs, after_refs = refs[:hops], refs[hops : 2 * hops]
+    pressure_ref, residual_ref = refs[2 * hops : 2 * hops + 2]
+    scratch = refs[2 * hops + 2 :]
     levels = plan.coarsest + 1
     coarsest = plan.coarsest
     layers, rows = plan.layers, plan.rows
@@ -166,31 +228,31 @@
             return pl.ds(low, high - low)
         return pl.ds(start0 + low, high - low)
 
-    side = before_ref.shape[3]
-
-    def assemble(layer_no):
+    for layer_no in range(layers):
         zeros = jnp.zeros((GUARD, LANES), jnp.float32)
+        tail = rounded_up(GUARD + reach + own_rows + reach + 1, 8)
         for c in range(count[0]):
             density[layer_no, c, 0:GUARD] = zeros
-            tail = rounded_up(GUARD + reach + own_rows + reach + 1, 8)
             density[layer_no, c, tail - 8 : tail] = zeros
-            density[layer_no, c, span(GUARD - 1, GUARD + reach)] = before_ref[
-                0, layer_no, c, span(side - reach - 1, side)
-            ]
-            density[layer_no, c, span(GUARD + reach, GUARD + reach + own_rows)] = own_ref[0, layer_no, c]
-            start = GUARD + reach + own_rows
-            density[layer_no, c, span(start, start + reach + 1)] = after_ref[
-                0, layer_no, c, span(0, reach + 1)
-            ]
             forcing[0][layer_no, c, rows - 8 : rows] = zeros
-            forcing[0][layer_no, c, span(0, reach)] = before_ref[1, layer_no, c, span(side - reach, side)]
-            forcing[0][layer_no, c, span(reach, reach + own_rows)] = own_ref[1, layer_no, c]
-            start = reach + own_rows
-            forcing[0][layer_no, c, span(start, start + reach)] = after_ref[
-                1, layer_no, c, span(0, reach)
-            ]
-
-    pl.loop(0, layers, unroll=2)(assemble)
+        for which, target, base in ((0, density, GUARD + reach), (1, forcing[0], reach)):
+            for c in range(count[0]):
+                target[layer_no, c, span(base, base + own_rows)] = own_ref[which, layer_no, c]
+            for refs_of, packings, side in (
+                (before_refs, plan.along_tails, -1),
+                (after_refs, plan.along_heads, 1),
+            ):
+                for hop in range(hops):
+                    block = base + side * (hop + 1) * own_rows
+                    for piece in packings[hop].pieces:
+                        if piece[0] != which:
+                            continue
+                        start, run = piece[1], piece[2]
+                        tile, offset = packings[hop].place(piece, layer_no)
+                        for c in range(count[0]):
+                            target[layer_no, c, span(block + start, block + start + run)] = refs_of[
+                                hop
+                            ][tile, c, span(offset, offset + run)]
 
     def faces(layer_no, first):
         wests, souths, uppers = [], [], []
@@ -406,17 +468,36 @@
     layers, rows, cols = source.shape
     plan = Plan(lax.axis_size("cross"), layers, rows, cols)
     levels = plan.coarsest + 1
-    both = jnp.stack([inv_density, source])
-    before, after = beside(both, "cross", 3, plan.side_cols)
     vmem = pl.BlockSpec(memory_space=pltpu.VMEM)
-    window = pl.pallas_call(
+
+    def exchange(sent, axis):
+        hops = len(sent) // 2
+        got = [shifted(sent[hop], axis, hop + 1) for hop in range(hops)]
+        return got + [shifted(sent[hops + hop], axis, -hop - 1) for hop in range(hops)]
+
+    sent = pl.pallas_call(
+        functools.partial(edge_kernel, plan),
+        out_shape=[
+            jax.ShapeDtypeStruct((each.size, rows, LANES), jnp.float32)
+            for each in plan.cross_tails + plan.cross_heads
+        ],
+        in_specs=[vmem] * 2,
+        out_specs=[vmem] * (2 * len(plan.cross_hops)),
+        compiler_params=pltpu.CompilerParams(vmem_limit_bytes=16 << 20),
+    )(inv_density, source)
+    got = exchange(sent, "cross")
+    window, *sent = pl.pallas_call(
         functools.partial(window_kernel, plan),
-        out_shape=jax.ShapeDtypeStruct((2, layers, plan.chunks, rows, LANES), jnp.float32),
-        in_specs=[vmem] * 3,
-        out_specs=vmem,
-        compiler_params=pltpu.CompilerParams(vmem_limit_bytes=48 << 20),
-    )(both, before, after)
-    before, after = beside(window, "along", 3, plan.side_rows)
+        out_shape=[jax.ShapeDtypeStruct((2, layers, plan.chunks, rows, LANES), jnp.float32)]
+        + [
+            jax.ShapeDtypeStruct((each.size, plan.chunks, 8, LANES), jnp.float32)
+            for each in plan.along_tails + plan.along_heads
+        ],
+        in_specs=[vmem] * (2 + len(got)),
+        out_specs=[vmem] * (1 + 2 * len(plan.along_hops)),
+        compiler_params=pltpu.CompilerParams(vmem_limit_bytes=32 << 20),
+    )(inv_density, source, *got)
+    got = exchange(sent, "along")
 
     def room(*shape):
         return pltpu.VMEM(shape + (LANES,), jnp.float32)
@@ -436,16 +517,16 @@
     scratch += [room(layers, n, high + GUARD) for n in counts]
     scratch += [room(layers, counts[0], total)]
     scratch += [room(layers + 1, n, total) for n in counts[1:]]
-    held = sum(math.prod(each.shape) for each in scratch) + window.size + 2 * before.size
+    held = sum(math.prod(each.shape) for each in scratch) + window.size + sum(each.size for each in got)
     held = 4 * (held + 2 * source.size)
     return pl.pallas_call(
         functools.partial(cycle_kernel, plan),
         out_shape=[jax.ShapeDtypeStruct((layers, rows, cols), jnp.float32)] * 2,
-        in_specs=[vmem] * 3,
+        in_specs=[vmem] * (1 + len(got)),
         out_specs=[vmem] * 2,
         scratch_shapes=scratch,
         compiler_params=pltpu.CompilerParams(vmem_limit_bytes=held + (2 << 20)),
-    )(window, before, after)
+    )(window, *got)
 
 
 def solution(mesh):

time: 52.5 us -> 48.9 us (0.931)
  the two profiles are of different devices: /device:TPU:6 before, /device:TPU:1 now
where the time goes in v2:
time: 48.9 us; the launch traced here: 48.2 us
  waiting for transfers between devices  17.1 us (35%)
  Pallas kernels  16.5 us (34%)
  starting transfers between devices  12.1 us (25%)
  local copies, waits for them, and re-layouts  1.9 us (4%)
  between operations  0.69 us (1%)
    ppermute x4, waiting for transfers between devices, shifted(): return lax.ppermute(array, axis, pairs)  17.1 us
    pallas_call x1, Pallas kernels, per_device(): pl.pallas_call(functools.partial(cycle_kernel, plan), out_shape=[jax.Shap...  12.5 us
    ppermute x4, starting transfers between devices, shifted(): return lax.ppermute(array, axis, pairs)  12.1 us
    pallas_call x1, Pallas kernels, per_device(): pl.pallas_call(functools.partial(window_kernel, plan), out_shape=[jax.Sha...  3.77 us
    unnamed x8, local copies, waits for them, and re-layouts  1.9 us
  transfers between devices with their start and end apart: 4, of which 4 were waited for; matrix products, arithmetic and copies ran while one was open for 0% of the time, Pallas kernels for 0%

profile of v2, /device:TPU:1, one launch (start us, length us, event | category | flops | bytes accessed | tf_op | source)
XLA Modules:
  0.0 48.2 jit_solution(15833402191837089011)
XLA Ops:
  0.6 0.0 copy-start
  0.6 0.9 %copy-done = f32[16,16,256]{2,1,0:T(8,128)S(1)} copy-done((f32[16,16,256]{2,1,0:T(8,128)S(1)}, f32[16,16,256]{2,1,0:T(8,128)}, u32[]{:S(2)}) %copy-start) | copy-done | bytes 262168
  1.6 0.0 copy-start.2
  1.6 0.9 %copy-done.2 = f32[16,16,256]{2,1,0:T(8,128)S(1)} copy-done((f32[16,16,256]{2,1,0:T(8,128)S(1)}, f32[16,16,256]{2,1,0:T(8,128)}, u32[]{:S(2)}) %copy-start.2) | copy-done | bytes 262168
  2.5 0.0 copy-start.1
  2.5 0.0 copy-start.3
  2.5 0.2 shard_map.41
  2.8 4.0 %collective-permute-start = (f32[20,16,128]{2,1,0:T(8,128)S(1)}, f32[20,16,128]{2,1,0:T(8,128)S(1)}, u32[]{:S(2)}, u32[]{:S(2)}) collective-permute-start(f32[20,16,128]{2,1,0:T(8,128)S(1)} %get-tuple-element.7), channel_id=1, source_target_pairs={{0,4},{4,8},{8,12},{12,16},{16,20},{20,24},{24,28},{1,5},{5,9},{9,... | collective-permute-start | bytes 491528 | tf_op jit(solution)/shard_map/ppermute | solution.py:30
  6.8 1.3 %collective-permute-start.1 = (f32[20,16,128]{2,1,0:T(8,128)S(1)}, f32[20,16,128]{2,1,0:T(8,128)S(1)}, u32[]{:S(2)}, u32[]{:S(2)}) collective-permute-start(f32[20,16,128]{2,1,0:T(8,128)S(1)} %get-tuple-element.8), channel_id=1, source_target_pairs={{4,0},{8,4},{12,8},{16,12},{20,16},{24,20},{28,24},{5,1},{9,5},{13... | collective-permute-start | bytes 491528 | tf_op jit(solution)/shard_map/ppermute | solution.py:30
  8.1 1.5 %collective-permute-done.refs_0_ = f32[20,16,128]{2,1,0:T(8,128)S(1)} collective-permute-done((f32[20,16,128]{2,1,0:T(8,128)S(1)}, f32[20,16,128]{2,1,0:T(8,128)S(1)}, u32[]{:S(2)}, u32[]{:S(2)}) %collective-permute-start) | collective-permute-done | bytes 163872 | tf_op jit(solution)/shard_map/ppermute | solution.py:30
  9.6 3.8 %collective-permute-done.1.refs_1_ = f32[20,16,128]{2,1,0:T(8,128)S(1)} collective-permute-done((f32[20,16,128]{2,1,0:T(8,128)S(1)}, f32[20,16,128]{2,1,0:T(8,128)S(1)}, u32[]{:S(2)}, u32[]{:S(2)}) %collective-permute-start.1) | collective-permute-done | bytes 163872 | tf_op jit(solution)/shard_map/ppermute | solution.py:30
  13.4 0.0 copy-done.1
  13.4 0.0 copy-done.3
  13.4 3.8 %shard_map.42 = (f32[2,16,4,16,128]{4,3,2,1,0:T(8,128)S(1)}, f32[50,4,8,128]{3,2,1,0:T(8,128)S(1)}, f32[50,4,8,128]{3,2,1,0:T(8,128)S(1)}) custom-call(f32[16,16,256]{2,1,0:T(8,128)S(1)} %copy-done.1, f32[16,16,256]{2,1,0:T(8,128)S(1)} %copy-done.3, f32[20,16,128]{2,1,0:T(8,128)S(1)} %collective-permute-done.refs_0_, ...), custom_call_target="tpu_custom_call" | custom-call | tf_op jit(solution)/shard_map/pallas_call | solution.py:489
  17.2 4.9 %collective-permute-start.2 = (f32[50,4,8,128]{3,2,1,0:T(8,128)S(1)}, f32[50,4,8,128]{3,2,1,0:T(8,128)S(1)}, u32[]{:S(2)}, u32[]{:S(2)}) collective-permute-start(f32[50,4,8,128]{3,2,1,0:T(8,128)S(1)} %get-tuple-element.10), channel_id=1, source_target_pairs={{0,1},{1,2},{2,3},{4,5},{5,6},{6,7},{8,9},{9,10},{10,11},{12,13},{... | collective-permute-start | bytes 2457608 | tf_op jit(solution)/shard_map/ppermute | solution.py:30
  22.1 1.9 %collective-permute-start.3 = (f32[50,4,8,128]{3,2,1,0:T(8,128)S(1)}, f32[50,4,8,128]{3,2,1,0:T(8,128)S(1)}, u32[]{:S(2)}, u32[]{:S(2)}) collective-permute-start(f32[50,4,8,128]{3,2,1,0:T(8,128)S(1)} %get-tuple-element.11), channel_id=1, source_target_pairs={{1,0},{2,1},{3,2},{5,4},{6,5},{7,6},{9,8},{10,9},{11,10},{13,12},{... | collective-permute-start | bytes 2457608 | tf_op jit(solution)/shard_map/ppermute | solution.py:30
  24.0 7.3 %collective-permute-done.2.refs_0_ = f32[50,4,8,128]{3,2,1,0:T(8,128)S(1)} collective-permute-done((f32[50,4,8,128]{3,2,1,0:T(8,128)S(1)}, f32[50,4,8,128]{3,2,1,0:T(8,128)S(1)}, u32[]{:S(2)}, u32[]{:S(2)}) %collective-permute-start.2) | collective-permute-done | bytes 819232 | tf_op jit(solution)/shard_map/ppermute | solution.py:30
  31.4 4.4 %collective-permute-done.3.refs_1_ = f32[50,4,8,128]{3,2,1,0:T(8,128)S(1)} collective-permute-done((f32[50,4,8,128]{3,2,1,0:T(8,128)S(1)}, f32[50,4,8,128]{3,2,1,0:T(8,128)S(1)}, u32[]{:S(2)}, u32[]{:S(2)}) %collective-permute-start.3) | collective-permute-done | bytes 819232 | tf_op jit(solution)/shard_map/ppermute | solution.py:30
  35.7 12.5 %shard_map.43 = (f32[16,16,256]{2,1,0:T(8,128)}, f32[16,16,256]{2,1,0:T(8,128)}) custom-call(f32[2,16,4,16,128]{4,3,2,1,0:T(8,128)S(1)} %get-tuple-element.9.own_ref, f32[50,4,8,128]{3,2,1,0:T(8,128)S(1)} %collective-permute-done.2.refs_0_, f32[50,4,8,128]{3,2,1,0:T(8,128)S(1)} %collective-permute-done.3.refs_1_), custom_call_target="tpu_custom_call" | custom-call | tf_op jit(solution)/shard_map/pallas_call | solution.py:522
Async XLA Ops:
  0.6 1.0 %copy-start = (f32[16,16,256]{2,1,0:T(8,128)S(1)}, f32[16,16,256]{2,1,0:T(8,128)}, u32[]{:S(2)}) copy-start(f32[16,16,256]{2,1,0:T(8,128)} %density_ref.3) | copy-start | bytes 786436
  1.6 0.9 %copy-start.2 = (f32[16,16,256]{2,1,0:T(8,128)S(1)}, f32[16,16,256]{2,1,0:T(8,128)}, u32[]{:S(2)}) copy-start(f32[16,16,256]{2,1,0:T(8,128)} %source_ref.3) | copy-start | bytes 786436
  2.5 10.9 %copy-start.1 = (f32[16,16,256]{2,1,0:T(8,128)S(1)}, f32[16,16,256]{2,1,0:T(8,128)}, u32[]{:S(2)}) copy-start(f32[16,16,256]{2,1,0:T(8,128)} %density_ref.3) | copy-start | bytes 786436
  2.5 10.9 %copy-start.3 = (f32[16,16,256]{2,1,0:T(8,128)S(1)}, f32[16,16,256]{2,1,0:T(8,128)}, u32[]{:S(2)}) copy-start(f32[16,16,256]{2,1,0:T(8,128)} %source_ref.3) | copy-start | bytes 786436
  2.8 6.8 %collective-permute-start = (f32[20,16,128]{2,1,0:T(8,128)S(1)}, f32[20,16,128]{2,1,0:T(8,128)S(1)}, u32[]{:S(2)}, u32[]{:S(2)}) collective-permute-start(f32[20,16,128]{2,1,0:T(8,128)S(1)} %get-tuple-element.7), channel_id=1, source_target_pairs={{0,4},{4,8},{8,12},{12,16},{16,20},{20,24},{24,28},{1,5},{5,9},{9,... | collective-permute-start | bytes 491528 | tf_op jit(solution)/shard_map/ppermute | solution.py:30
  6.8 6.6 %collective-permute-start.1 = (f32[20,16,128]{2,1,0:T(8,128)S(1)}, f32[20,16,128]{2,1,0:T(8,128)S(1)}, u32[]{:S(2)}, u32[]{:S(2)}) collective-permute-start(f32[20,16,128]{2,1,0:T(8,128)S(1)} %get-tuple-element.8), channel_id=1, source_target_pairs={{4,0},{8,4},{12,8},{16,12},{20,16},{24,20},{28,24},{5,1},{9,5},{13... | collective-permute-start | bytes 491528 | tf_op jit(solution)/shard_map/ppermute | solution.py:30
  17.2 14.1 %collective-permute-start.2 = (f32[50,4,8,128]{3,2,1,0:T(8,128)S(1)}, f32[50,4,8,128]{3,2,1,0:T(8,128)S(1)}, u32[]{:S(2)}, u32[]{:S(2)}) collective-permute-start(f32[50,4,8,128]{3,2,1,0:T(8,128)S(1)} %get-tuple-element.10), channel_id=1, source_target_pairs={{0,1},{1,2},{2,3},{4,5},{5,6},{6,7},{8,9},{9,10},{10,11},{12,13},{... | collective-permute-start | bytes 2457608 | tf_op jit(solution)/shard_map/ppermute | solution.py:30
  22.1 13.7 %collective-permute-start.3 = (f32[50,4,8,128]{3,2,1,0:T(8,128)S(1)}, f32[50,4,8,128]{3,2,1,0:T(8,128)S(1)}, u32[]{:S(2)}, u32[]{:S(2)}) collective-permute-start(f32[50,4,8,128]{3,2,1,0:T(8,128)S(1)} %get-tuple-element.11), channel_id=1, source_target_pairs={{1,0},{2,1},{3,2},{5,4},{6,5},{7,6},{9,8},{10,9},{11,10},{13,12},{... | collective-permute-start | bytes 2457608 | tf_op jit(solution)/shard_map/ppermute | solution.py:30

commit v3 on v1

--- a/solution.py
+++ b/solution.py
@@ -30,21 +30,24 @@
     return lax.ppermute(array, axis, pairs)
 
 
-def beside(block, axis, dim, width):
-    size = block.shape[dim]
-    before, after = [], []
-    hop = 1
-    while width > 0:
-        take = min(width, size)
-        tail = lax.slice_in_dim(block, size - take, size, axis=dim)
-        head = lax.slice_in_dim(block, 0, take, axis=dim)
-        before.insert(0, shifted(tail, axis, hop))
-        after.append(shifted(head, axis, -hop))
-        width -= take
-        hop += 1
-    if len(before) == 1:
-        return before[0], after[0]
-    return jnp.concatenate(before, dim), jnp.concatenate(after, dim)
+class Packing:
+    def __init__(self, layers, chunks, first, count):
+        self.first, self.lanes, self.chunks = first, count // chunks, chunks
+        self.share = LANES // self.lanes
+        self.each = -(-layers * chunks // self.share)
+        self.size = 2 * self.each
+
+    def place(self, which, layer_no, chunk):
+        item = layer_no * self.chunks + chunk
+        return which * self.each + item // self.share, item % self.share * self.lanes
+
+
+def hops_of(size, reach):
+    hops = []
+    while reach > 0:
+        hops.append(min(size, reach))
+        reach -= hops[-1]
+    return hops
 
 
 class Plan:
@@ -62,7 +65,19 @@
         self.chunks = chunks
         self.side_cols = (chunks * LANES - cols) // 2
         self.rows = rounded_up(rows + 2 * self.row_reach, 8)
-        self.side_rows = rounded_up(self.row_reach + 1, 8)
+        cross_hops = hops_of(cols, rounded_up(self.col_reach, chunks))
+        self.cross_count = len(cross_hops)
+        self.cross = [Packing(layers, chunks, cols - n, n) for n in cross_hops]
+        self.cross += [Packing(layers, chunks, 0, n) for n in cross_hops]
+        self.halo_size = sum(each.size for each in self.cross)
+        own_lane, own_lanes = self.side_cols // chunks, cols // chunks
+        self.own_lane, self.own_lanes = own_lane, own_lanes
+        self.cross_lane = [
+            own_lane - hop * own_lanes - self.cross[hop].lanes for hop in range(len(cross_hops))
+        ] + [own_lane + (hop + 1) * own_lanes for hop in range(len(cross_hops))]
+        self.along_hops = hops_of(rows, rounded_up(self.row_reach + 1, 8))
+        self.side_rows = sum(self.along_hops)
+        self.lead = rounded_up(max(0, self.along_hops[0] - self.row_reach), 8)
 
     def level_chunks(self, level_no):
         return max(1, self.chunks >> level_no)
@@ -79,26 +94,103 @@
     return jnp.take_along_axis(value, pick, axis=1, mode="promise_in_bounds")
 
 
-def window_kernel(plan, own_ref, before_ref, after_ref, out_ref):
-    chunks, rows = plan.chunks, plan.own_rows
-    lane = lane_numbers(rows)
-    picks = [(chunks * lane + chunk) % LANES for chunk in range(chunks)]
-    part = lane // (LANES // chunks)
+def edge_kernel(plan, density_ref, source_ref, both_ref, *refs):
+    out_refs, semaphore = refs[:-1], refs[-1]
+    copies = [
+        pltpu.make_async_copy(ref, both_ref.at[which], semaphore.at[which])
+        for which, ref in enumerate((density_ref, source_ref))
+    ]
+    for copy in copies:
+        copy.start()
+    for copy in copies:
+        copy.wait()
+    lane = lane_numbers(plan.own_rows)
+    chunks, layers = plan.chunks, plan.layers
+    for packing, out_ref in zip(plan.cross, out_refs):
+        lanes, share = packing.lanes, packing.share
+        for which in range(2):
+            for group in range(packing.each):
+                items = range(group * share, min(group * share + share, layers * chunks))
+                value = None
+                for layer_no in sorted({item // chunks for item in items}):
+                    low = max(layer_no * chunks - group * share, 0)
+                    slot = lane // lanes
+                    cell = packing.first + chunks * (lane - slot * lanes)
+                    cell = cell + (slot + group * share) % chunks
+                    for start in range(0, plan.own_cols, LANES):
+                        if start + LANES <= packing.first:
+                            continue
+                        if start >= packing.first + lanes * chunks:
+                            continue
+                        each = taken(
+                            both_ref[which, layer_no, :, start : start + LANES], cell & (LANES - 1)
+                        )
+                        if value is None:
+                            value = each
+                        else:
+                            value = jnp.where((slot >= low) & (cell >= start), each, value)
+                out_ref[which * packing.each + group] = value
+
+
+def halo_kernel(plan, *refs):
+    base = 0
+    for ref in refs[:-1]:
+        refs[-1][base : base + ref.shape[0]] = ref[...]
+        base += ref.shape[0]
+
+
+def with_halos(plan, value, which, layer_no, chunk, halo_of):
+    lane = lane_numbers(value.shape[0])
+    hops = plan.cross_count
+    for message, packing in enumerate(plan.cross):
+        group, offset = packing.place(which, layer_no, chunk)
+        first = plan.cross_lane[message]
+        turn = (first - offset) % LANES
+        cells = halo_of(message, group)
+        if turn:
+            cells = pltpu.roll(cells, turn, 1)
+        if message < hops:
+            inside = lane < first + packing.lanes
+        else:
+            inside = lane >= first
+        value = jnp.where(inside, cells, value)
+    return value
+
+
+def window_kernel(plan, both_ref, *refs):
+    hops, halos = len(plan.along_hops), len(plan.cross)
+    before_refs, after_refs = refs[:hops], refs[hops : 2 * hops]
+    halo_refs, out_ref = refs[2 * hops : 2 * hops + halos], refs[-1]
+    chunks, rows, cols = plan.chunks, plan.own_rows, plan.own_cols
+    parts = [(both_ref, plan.side_rows, rows)]
+    row = plan.side_rows
+    for ref in before_refs:
+        row -= ref.shape[2]
+        parts.append((ref, row, ref.shape[2]))
+    row = plan.side_rows + rows
+    for ref in after_refs:
+        parts.append((ref, row, ref.shape[2]))
+        row += ref.shape[2]
 
     def layer_step(which, layer_no):
-        tiles = []
-        for ref in (before_ref, own_ref, after_ref):
-            for first in range(0, ref.shape[3], LANES):
-                tiles.append(ref[which, layer_no, :, first : first + LANES])
-        for chunk in range(chunks):
-            value = taken(tiles[0], picks[chunk])
-            for tile_no in range(1, chunks):
-                other = taken(tiles[tile_no], picks[chunk])
-                value = jnp.where(part == tile_no, other, value)
-            out_ref[which, layer_no, chunk] = value
+        for ref, row, height in parts:
+            lane = lane_numbers(height)
+            tiles = [ref[which, layer_no, :, i : i + LANES] for i in range(0, cols, LANES)]
+            for chunk in range(chunks):
+                pick = (chunks * (lane - plan.own_lane) + chunk) & (LANES - 1)
+                value = taken(tiles[0], pick)
+                for tile_no in range(1, len(tiles)):
+                    inside = lane >= plan.own_lane + tile_no * LANES // chunks
+                    value = jnp.where(inside, taken(tiles[tile_no], pick), value)
+                if ref is both_ref:
+                    value = with_halos(
+                        plan, value, which, layer_no, chunk, lambda k, group: halo_refs[k][group]
+                    )
+                out_ref[which, layer_no, chunk, row : row + height] = value
 
     for which in range(2):
-        pl.loop(0, plan.layers, unroll=4)(functools.partial(layer_step, which))
+        for layer_no in range(plan.layers):
+            layer_step(which, layer_no)
 
 
 def reciprocal(value):
@@ -127,12 +219,7 @@
     if len(cells) > 1:
         return [cells[2 * k] + cells[2 * k + 1] for k in range(len(cells) // 2)]
     value = cells[0]
-    other = jnp.where(
-        first_of_pair(value, spread),
-        pltpu.roll(value, LANES - spread, 1),
-        pltpu.roll(value, spread, 1),
-    )
-    return [value + other]
+    return [value + taken(value, lane_numbers(value.shape[0]) ^ spread)]
 
 
 def firsts(cells, spread):
@@ -142,14 +229,18 @@
     return [jnp.where(first_of_pair(value, spread), value, pltpu.roll(value, spread, 1))]
 
 
-def cycle_kernel(plan, own_ref, before_ref, after_ref, pressure_ref, residual_ref, *scratch):
+def cycle_kernel(plan, window_ref, *refs):
+    hops = len(plan.along_hops)
+    before_refs, after_refs = refs[:hops], refs[hops : 2 * hops]
+    pressure_ref, residual_ref = refs[2 * hops : 2 * hops + 2]
+    scratch = refs[2 * hops + 2 :]
     levels = plan.coarsest + 1
     coarsest = plan.coarsest
     layers, rows = plan.layers, plan.rows
     reach, own_rows = plan.row_reach, plan.own_rows
     scratch = list(scratch)
-    upright, centre0, upper0, origin = scratch[:4]
-    rest = scratch[4:]
+    upright, upper0, origin = scratch[:3]
+    rest = scratch[3:]
     west, south, factor, inverse, value, forcing = [
         rest[i * levels : (i + 1) * levels] for i in range(6)
     ]
@@ -166,31 +257,40 @@
             return pl.ds(low, high - low)
         return pl.ds(start0 + low, high - low)
 
-    side = before_ref.shape[3]
-
-    def assemble(layer_no):
-        zeros = jnp.zeros((GUARD, LANES), jnp.float32)
-        for c in range(count[0]):
-            density[layer_no, c, 0:GUARD] = zeros
-            tail = rounded_up(GUARD + reach + own_rows + reach + 1, 8)
-            density[layer_no, c, tail - 8 : tail] = zeros
-            density[layer_no, c, span(GUARD - 1, GUARD + reach)] = before_ref[
-                0, layer_no, c, span(side - reach - 1, side)
-            ]
-            density[layer_no, c, span(GUARD + reach, GUARD + reach + own_rows)] = own_ref[0, layer_no, c]
-            start = GUARD + reach + own_rows
-            density[layer_no, c, span(start, start + reach + 1)] = after_ref[
-                0, layer_no, c, span(0, reach + 1)
-            ]
-            forcing[0][layer_no, c, rows - 8 : rows] = zeros
-            forcing[0][layer_no, c, span(0, reach)] = before_ref[1, layer_no, c, span(side - reach, side)]
-            forcing[0][layer_no, c, span(reach, reach + own_rows)] = own_ref[1, layer_no, c]
-            start = reach + own_rows
-            forcing[0][layer_no, c, span(start, start + reach)] = after_ref[
-                1, layer_no, c, span(0, reach)
-            ]
-
-    pl.loop(0, layers, unroll=2)(assemble)
+    def forced(m, layer_no, c, low, high):
+        base = plan.lead if m == 0 else 0
+        return forcing[m][layer_no, c, span(base + low, base + high)]
+
+    starts = {}
+    for message, packing in enumerate(plan.cross):
+        starts[message] = sum(each.size for each in plan.cross[:message])
+    parts = [(None, plan.side_rows, own_rows)]
+    row = plan.side_rows
+    for ref in before_refs:
+        row -= ref.shape[1]
+        parts.append((ref, row, ref.shape[1]))
+    row = plan.side_rows + own_rows
+    for ref in after_refs:
+        parts.append((ref, row, ref.shape[1]))
+        row += ref.shape[1]
+    for which, target, guard in ((0, density, GUARD), (1, forcing[0], plan.lead)):
+        for layer_no in range(layers):
+            for c in range(count[0]):
+                for ref, row, height in parts:
+                    first = guard + reach - plan.side_rows + row
+                    if which == 1 and (first + height <= guard or first >= guard + rows):
+                        continue
+                    value_now = window_ref[which, layer_no, c, row : row + height]
+                    if ref is not None:
+                        value_now = with_halos(
+                            plan,
+                            value_now,
+                            which,
+                            layer_no,
+                            c,
+                            lambda k, group, ref=ref: ref[starts[k] + group],
+                        )
+                    target[layer_no, c, span(first, first + height)] = value_now
 
     def faces(layer_no, first):
         wests, souths, uppers = [], [], []
@@ -253,8 +353,6 @@
                     + above
                     + upper[m][layer_no + 1, c]
                 )
-                if m == 0:
-                    centre0[layer_no, c] = centre
                 if first:
                     pivot = centre
                 else:
@@ -318,7 +416,7 @@
 
     def first_sweep(m):
         def right_side(layer_no):
-            return [forcing[m][layer_no, c] for c in range(count[m])]
+            return [forced(m, layer_no, c, 0, rows) for c in range(count[m])]
 
         def store(layer_no, now):
             for c in range(count[m]):
@@ -329,7 +427,7 @@
     def later_sweep(m, low, high, prolong):
         def right_side(layer_no):
             flow = around(m, layer_no, low, high)
-            return [forcing[m][layer_no, c, low:high] + flow[c] for c in range(count[m])]
+            return [forced(m, layer_no, c, low, high) + flow[c] for c in range(count[m])]
 
         def store(layer_no, now):
             for c in range(count[m]):
@@ -350,7 +448,7 @@
         def restrict(layer_no, m=m):
             flow = around(m, layer_no, 0, rows)
             remain = [
-                (1.0 - relaxation) * forcing[m][layer_no, c] + flow[c] for c in range(count[m])
+                (1.0 - relaxation) * forced(m, layer_no, c, 0, rows) + flow[c] for c in range(count[m])
             ]
             for c, each in enumerate(paired(remain, spread[m])):
                 forcing[m + 1][layer_no, c] = each
@@ -385,7 +483,15 @@
         cells, remains = [], []
         for c in range(chunks):
             now = value[0][layer_no, c, own]
-            remain = forcing[0][layer_no, c, plain] - centre0[layer_no, c, plain] * now + flow[c]
+            centre = (
+                west[0][layer_no, c, plain]
+                + west[0][layer_no, c, span(low + 1, high + 1)]
+                + south[0][layer_no, c, plain]
+                + south[0][layer_no, c + 1, plain]
+                + upper[0][layer_no, c, plain]
+                + upper[0][layer_no + 1, c, plain]
+            )
+            remain = forced(0, layer_no, c, low, high) - centre * now + flow[c]
             if not top:
                 remain += upper[0][layer_no, c, plain] * value[0][layer_no - 1, c, own]
             if not bottom:
@@ -406,17 +512,50 @@
     layers, rows, cols = source.shape
     plan = Plan(lax.axis_size("cross"), layers, rows, cols)
     levels = plan.coarsest + 1
-    both = jnp.stack([inv_density, source])
-    before, after = beside(both, "cross", 3, plan.side_cols)
     vmem = pl.BlockSpec(memory_space=pltpu.VMEM)
+
+    shape = functools.partial(jax.ShapeDtypeStruct, dtype=jnp.float32)
+    outside = pl.BlockSpec(memory_space=pltpu.HBM)
+    both, *sent = pl.pallas_call(
+        functools.partial(edge_kernel, plan),
+        out_shape=[shape((2, layers, rows, cols))]
+        + [shape((each.size, rows, LANES)) for each in plan.cross],
+        in_specs=[outside] * 2,
+        out_specs=[vmem] * (1 + len(plan.cross)),
+        scratch_shapes=[pltpu.SemaphoreType.DMA((2,))],
+        compiler_params=pltpu.CompilerParams(vmem_limit_bytes=16 << 20),
+    )(inv_density, source)
+
+    def along(block, dim):
+        got = []
+        for side in (1, -1):
+            for hop, height in enumerate(plan.along_hops):
+                first = rows - height if side > 0 else 0
+                part = lax.slice_in_dim(block, first, first + height, axis=dim)
+                got.append(shifted(part, "along", side * (hop + 1)))
+        return got
+
+    hops = plan.cross_count
+    halos = [shifted(sent[hop], "cross", hop + 1) for hop in range(hops)]
+    halos += [shifted(sent[hops + hop], "cross", -hop - 1) for hop in range(hops)]
+    beside = along(both, 2)
+    halo = pl.pallas_call(
+        functools.partial(halo_kernel, plan),
+        out_shape=shape((plan.halo_size, rows, LANES)),
+        in_specs=[vmem] * len(halos),
+        out_specs=vmem,
+        compiler_params=pltpu.CompilerParams(vmem_limit_bytes=16 << 20),
+    )(*halos)
+    got = along(halo, 1)
+    height = rows + 2 * plan.side_rows
     window = pl.pallas_call(
         functools.partial(window_kernel, plan),
-        out_shape=jax.ShapeDtypeStruct((2, layers, plan.chunks, rows, LANES), jnp.float32),
-        in_specs=[vmem] * 3,
+        out_shape=shape((2, layers, plan.chunks, height, LANES)),
+        in_specs=[vmem] * (1 + len(beside) + len(halos)),
         out_specs=vmem,
-        compiler_params=pltpu.CompilerParams(vmem_limit_bytes=48 << 20),
-    )(both, before, after)
-    before, after = beside(window, "along", 3, plan.side_rows)
+        compiler_params=pltpu.CompilerParams(vmem_limit_bytes=32 << 20),
+        cost_estimate=pl.CostEstimate(flops=10**7, bytes_accessed=4 << 20, transcendentals=0),
+    )(both, *beside, *halos)
 
     def room(*shape):
         return pltpu.VMEM(shape + (LANES,), jnp.float32)
@@ -425,7 +564,6 @@
     counts = [plan.level_chunks(m) for m in range(levels)]
     scratch = [
         room(layers, counts[-1], total),
-        room(layers, counts[0], total),
         room(layers + 1, counts[0], total),
         pltpu.SMEM((1,), jnp.int32),
     ]
@@ -434,18 +572,18 @@
     scratch += [room(layers, n, total) for n in counts]
     scratch += [room(layers, n, total) for n in counts]
     scratch += [room(layers, n, high + GUARD) for n in counts]
-    scratch += [room(layers, counts[0], total)]
+    scratch += [room(layers, counts[0], total + 2 * plan.lead)]
     scratch += [room(layers + 1, n, total) for n in counts[1:]]
-    held = sum(math.prod(each.shape) for each in scratch) + window.size + 2 * before.size
+    held = sum(math.prod(each.shape) for each in scratch) + window.size + sum(each.size for each in got)
     held = 4 * (held + 2 * source.size)
     return pl.pallas_call(
         functools.partial(cycle_kernel, plan),
         out_shape=[jax.ShapeDtypeStruct((layers, rows, cols), jnp.float32)] * 2,
-        in_specs=[vmem] * 3,
+        in_specs=[vmem] * (1 + len(got)),
         out_specs=[vmem] * 2,
         scratch_shapes=scratch,
-        compiler_params=pltpu.CompilerParams(vmem_limit_bytes=held + (2 << 20)),
-    )(window, before, after)
+        compiler_params=pltpu.CompilerParams(vmem_limit_bytes=held + (1 << 20)),
+    )(window, *got)
 
 
 def solution(mesh):

time: 52.5 us -> 42 us (0.80)
  the two profiles are of different devices: /device:TPU:6 before, /device:TPU:9 now
where the time goes in v3:
time: 42 us; the launch traced here: 41.7 us
  starting transfers between devices  17.8 us (42%)
  Pallas kernels  17.2 us (41%)
  waiting for transfers between devices  4.11 us (10%)
  local copies, waits for them, and re-layouts  1.89 us (4%)
  between operations  0.73 us (2%)
    ppermute x6, starting transfers between devices, shifted(): return lax.ppermute(array, axis, pairs)  17.8 us
    pallas_call x1, Pallas kernels, per_device(): pl.pallas_call(functools.partial(cycle_kernel, plan), out_shape=[jax.Shap...  13.3 us
    ppermute x6, waiting for transfers between devices, shifted(): return lax.ppermute(array, axis, pairs)  4.11 us
    pallas_call x1, Pallas kernels, per_device(): pl.pallas_call(functools.partial(window_kernel, plan), out_shape=shape((2...  3.42 us
    unnamed x4, local copies, waits for them, and re-layouts  1.89 us
  transfers between devices with their start and end apart: 6, of which 3 were waited for; matrix products, arithmetic and copies ran while one was open for 0% of the time, Pallas kernels for 8%

profile of v3, /device:TPU:9, one launch (start us, length us, event | category | flops | bytes accessed | tf_op | source)
XLA Modules:
  0.0 41.7 jit_solution(14350832763974257587)
XLA Ops:
  0.6 0.0 copy-start
  0.6 0.9 %copy-done = f32[16,16,256]{2,1,0:T(8,128)S(1)} copy-done((f32[16,16,256]{2,1,0:T(8,128)S(1)}, f32[16,16,256]{2,1,0:T(8,128)}, u32[]{:S(2)}) %copy-start) | copy-done | bytes 262168
  1.6 0.0 copy-start.1
  1.6 0.9 %copy-done.1 = f32[16,16,256]{2,1,0:T(8,128)S(1)} copy-done((f32[16,16,256]{2,1,0:T(8,128)S(1)}, f32[16,16,256]{2,1,0:T(8,128)}, u32[]{:S(2)}) %copy-start.1) | copy-done | bytes 262168
  2.5 0.5 %shard_map.41 = (f32[2,16,16,256]{3,2,1,0:T(8,128)S(1)}, f32[22,16,128]{2,1,0:T(8,128)S(1)}, f32[22,16,128]{2,1,0:T(8,128)S(1)}) custom-call(f32[16,16,256]{2,1,0:T(8,128)S(1)} %copy-done, f32[16,16,256]{2,1,0:T(8,128)S(1)} %copy-done.1), custom_call_target="tpu_custom_call" | custom-call | tf_op jit(solution)/shard_map/pallas_call | solution.py:519
  3.0 3.1 %collective-permute-start.2 = (f32[22,16,128]{2,1,0:T(8,128)S(1)}, f32[22,16,128]{2,1,0:T(8,128)S(1)}, u32[]{:S(2)}, u32[]{:S(2)}) collective-permute-start(f32[22,16,128]{2,1,0:T(8,128)S(1)} %get-tuple-element.6), channel_id=1, source_target_pairs={{0,4},{4,8},{8,12},{12,16},{16,20},{20,24},{24,28},{1,5},{5,9},{9,... | collective-permute-start | bytes 540680 | tf_op jit(solution)/shard_map/ppermute | solution.py:30
  6.1 3.0 %collective-permute-start.3 = (f32[22,16,128]{2,1,0:T(8,128)S(1)}, f32[22,16,128]{2,1,0:T(8,128)S(1)}, u32[]{:S(2)}, u32[]{:S(2)}) collective-permute-start(f32[22,16,128]{2,1,0:T(8,128)S(1)} %get-tuple-element.7), channel_id=1, source_target_pairs={{4,0},{8,4},{12,8},{16,12},{20,16},{24,20},{28,24},{5,1},{9,5},{13... | collective-permute-start | bytes 540680 | tf_op jit(solution)/shard_map/ppermute | solution.py:30
  9.2 4.2 %collective-permute-start = (f32[2,16,16,256]{3,2,1,0:T(8,128)S(1)}, f32[2,16,16,256]{3,2,1,0:T(8,128)S(1)}, u32[]{:S(2)}, u32[]{:S(2)}) collective-permute-start(f32[2,16,16,256]{3,2,1,0:T(8,128)S(1)} %get-tuple-element.5.both_ref), channel_id=1, source_target_pairs={{0,1},{1,2},{2,3},{4,5},{5,6},{6,7},{8,9},{9,10},{10,11},{12,13},{... | collective-permute-start | bytes 1572872 | tf_op jit(solution)/shard_map/ppermute | solution.py:30
  13.4 1.9 %collective-permute-start.1 = (f32[2,16,16,256]{3,2,1,0:T(8,128)S(1)}, f32[2,16,16,256]{3,2,1,0:T(8,128)S(1)}, u32[]{:S(2)}, u32[]{:S(2)}) collective-permute-start(f32[2,16,16,256]{3,2,1,0:T(8,128)S(1)} %get-tuple-element.5.both_ref), channel_id=1, source_target_pairs={{1,0},{2,1},{3,2},{5,4},{6,5},{7,6},{9,8},{10,9},{11,10},{13,12},{... | collective-permute-start | bytes 1572872 | tf_op jit(solution)/shard_map/ppermute | solution.py:30
  15.4 0.0 collective-permute-done.2.refs_2_.refs_0_
  15.4 0.7 %collective-permute-done.3.refs_3_.refs_1_ = f32[22,16,128]{2,1,0:T(8,128)S(1)} collective-permute-done((f32[22,16,128]{2,1,0:T(8,128)S(1)}, f32[22,16,128]{2,1,0:T(8,128)S(1)}, u32[]{:S(2)}, u32[]{:S(2)}) %collective-permute-start.3) | collective-permute-done | bytes 180256 | tf_op jit(solution)/shard_map/ppermute | solution.py:30
  16.1 3.5 %collective-permute-start.4 = (f32[44,16,128]{2,1,0:T(8,128)S(1)}, f32[44,16,128]{2,1,0:T(8,128)S(1)}, u32[]{:S(2)}, u32[]{:S(2)}) collective-permute-start(f32[44,16,128]{2,1,0:T(8,128)S(1)} %shard_map.43), channel_id=1, source_target_pairs={{0,1},{1,2},{2,3},{4,5},{5,6},{6,7},{8,9},{9,10},{10,11},{12,13},{... | collective-permute-start | bytes 1081352 | tf_op jit(solution)/shard_map/ppermute | solution.py:30
  19.7 1.9 %collective-permute-start.5 = (f32[44,16,128]{2,1,0:T(8,128)S(1)}, f32[44,16,128]{2,1,0:T(8,128)S(1)}, u32[]{:S(2)}, u32[]{:S(2)}) collective-permute-start(f32[44,16,128]{2,1,0:T(8,128)S(1)} %shard_map.43), channel_id=1, source_target_pairs={{1,0},{2,1},{3,2},{5,4},{6,5},{7,6},{9,8},{10,9},{11,10},{13,12},{... | collective-permute-start | bytes 1081352 | tf_op jit(solution)/shard_map/ppermute | solution.py:30
  21.6 0.0 collective-permute-done.refs_0_
  21.6 2.3 %collective-permute-done.1.refs_1_ = f32[2,16,16,256]{3,2,1,0:T(8,128)S(1)} collective-permute-done((f32[2,16,16,256]{3,2,1,0:T(8,128)S(1)}, f32[2,16,16,256]{3,2,1,0:T(8,128)S(1)}, u32[]{:S(2)}, u32[]{:S(2)}) %collective-permute-start.1) | collective-permute-done | bytes 524320 | tf_op jit(solution)/shard_map/ppermute | solution.py:30
  23.9 3.4 %shard_map.42.window_ref = f32[2,16,4,48,128]{4,3,2,1,0:T(8,128)S(1)} custom-call(f32[2,16,16,256]{3,2,1,0:T(8,128)S(1)} %get-tuple-element.5.both_ref, f32[2,16,16,256]{3,2,1,0:T(8,128)S(1)} %collective-permute-done.refs_0_, f32[2,16,16,256]{3,2,1,0:T(8,128)S(1)} %collective-permute-done.1.refs_1_, ...), custom_call_target="tpu_custom_call" | custom-call | flops 10000000 | bytes 4194304 | tf_op jit(solution)/shard_map/pallas_call | solution.py:551
  27.4 0.0 collective-permute-done.4.refs_0_
  27.4 1.0 %collective-permute-done.5.refs_1_ = f32[44,16,128]{2,1,0:T(8,128)S(1)} collective-permute-done((f32[44,16,128]{2,1,0:T(8,128)S(1)}, f32[44,16,128]{2,1,0:T(8,128)S(1)}, u32[]{:S(2)}, u32[]{:S(2)}) %collective-permute-start.5) | collective-permute-done | bytes 360480 | tf_op jit(solution)/shard_map/ppermute | solution.py:30
  28.4 13.3 %shard_map.44 = (f32[16,16,256]{2,1,0:T(8,128)}, f32[16,16,256]{2,1,0:T(8,128)}) custom-call(f32[2,16,4,48,128]{4,3,2,1,0:T(8,128)S(1)} %shard_map.42.window_ref, f32[44,16,128]{2,1,0:T(8,128)S(1)} %collective-permute-done.4.refs_0_, f32[44,16,128]{2,1,0:T(8,128)S(1)} %collective-permute-done.5.refs_1_), custom_call_target="tpu_custom_call" | custom-call | tf_op jit(solution)/shard_map/pallas_call | solution.py:579
  (1 shorter events, 0.0 us)
Async XLA Ops:
  0.6 1.0 %copy-start = (f32[16,16,256]{2,1,0:T(8,128)S(1)}, f32[16,16,256]{2,1,0:T(8,128)}, u32[]{:S(2)}) copy-start(f32[16,16,256]{2,1,0:T(8,128)} %density_ref.1) | copy-start | bytes 786436
  1.6 0.9 %copy-start.1 = (f32[16,16,256]{2,1,0:T(8,128)S(1)}, f32[16,16,256]{2,1,0:T(8,128)}, u32[]{:S(2)}) copy-start(f32[16,16,256]{2,1,0:T(8,128)} %source_ref.1) | copy-start | bytes 786436
  3.0 12.4 %collective-permute-start.2 = (f32[22,16,128]{2,1,0:T(8,128)S(1)}, f32[22,16,128]{2,1,0:T(8,128)S(1)}, u32[]{:S(2)}, u32[]{:S(2)}) collective-permute-start(f32[22,16,128]{2,1,0:T(8,128)S(1)} %get-tuple-element.6), channel_id=1, source_target_pairs={{0,4},{4,8},{8,12},{12,16},{16,20},{20,24},{24,28},{1,5},{5,9},{9,... | collective-permute-start | bytes 540680 | tf_op jit(solution)/shard_map/ppermute | solution.py:30
  6.1 10.0 %collective-permute-start.3 = (f32[22,16,128]{2,1,0:T(8,128)S(1)}, f32[22,16,128]{2,1,0:T(8,128)S(1)}, u32[]{:S(2)}, u32[]{:S(2)}) collective-permute-start(f32[22,16,128]{2,1,0:T(8,128)S(1)} %get-tuple-element.7), channel_id=1, source_target_pairs={{4,0},{8,4},{12,8},{16,12},{20,16},{24,20},{28,24},{5,1},{9,5},{13... | collective-permute-start | bytes 540680 | tf_op jit(solution)/shard_map/ppermute | solution.py:30
  9.2 12.4 %collective-permute-start = (f32[2,16,16,256]{3,2,1,0:T(8,128)S(1)}, f32[2,16,16,256]{3,2,1,0:T(8,128)S(1)}, u32[]{:S(2)}, u32[]{:S(2)}) collective-permute-start(f32[2,16,16,256]{3,2,1,0:T(8,128)S(1)} %get-tuple-element.5.both_ref), channel_id=1, source_target_pairs={{0,1},{1,2},{2,3},{4,5},{5,6},{6,7},{8,9},{9,10},{10,11},{12,13},{... | collective-permute-start | bytes 1572872 | tf_op jit(solution)/shard_map/ppermute | solution.py:30
  13.4 10.5 %collective-permute-start.1 = (f32[2,16,16,256]{3,2,1,0:T(8,128)S(1)}, f32[2,16,16,256]{3,2,1,0:T(8,128)S(1)}, u32[]{:S(2)}, u32[]{:S(2)}) collective-permute-start(f32[2,16,16,256]{3,2,1,0:T(8,128)S(1)} %get-tuple-element.5.both_ref), channel_id=1, source_target_pairs={{1,0},{2,1},{3,2},{5,4},{6,5},{7,6},{9,8},{10,9},{11,10},{13,12},{... | collective-permute-start | bytes 1572872 | tf_op jit(solution)/shard_map/ppermute | solution.py:30
  16.1 11.2 %collective-permute-start.4 = (f32[44,16,128]{2,1,0:T(8,128)S(1)}, f32[44,16,128]{2,1,0:T(8,128)S(1)}, u32[]{:S(2)}, u32[]{:S(2)}) collective-permute-start(f32[44,16,128]{2,1,0:T(8,128)S(1)} %shard_map.43), channel_id=1, source_target_pairs={{0,1},{1,2},{2,3},{4,5},{5,6},{6,7},{8,9},{9,10},{10,11},{12,13},{... | collective-permute-start | bytes 1081352 | tf_op jit(solution)/shard_map/ppermute | solution.py:30
  19.7 8.7 %collective-permute-start.5 = (f32[44,16,128]{2,1,0:T(8,128)S(1)}, f32[44,16,128]{2,1,0:T(8,128)S(1)}, u32[]{:S(2)}, u32[]{:S(2)}) collective-permute-start(f32[44,16,128]{2,1,0:T(8,128)S(1)} %shard_map.43), channel_id=1, source_target_pairs={{1,0},{2,1},{3,2},{5,4},{6,5},{7,6},{9,8},{10,9},{11,10},{13,12},{... | collective-permute-start | bytes 1081352 | tf_op jit(solution)/shard_map/ppermute | solution.py:30

commit v4 on v1

v4 whole, which is shorter than its diff:
```python
import functools
import math

import jax
import jax.numpy as jnp
from jax import lax
from jax.experimental import pallas as pl
from jax.experimental.pallas import tpu as pltpu
from jax.sharding import PartitionSpec as P

SWEEPS = 4

along_weight = 0.25
cross_weight = 1.0
vertical_weight = 0.5
relaxation = 0.8

LANES = 128
GUARD = 8
TINY = 1e-30


def rounded_up(count, step):
    return -(-count // step) * step


def shifted(array, axis, by):
    devices = lax.axis_size(axis)
    pairs = [(i, i + by) for i in range(devices) if 0 <= i + by < devices]
    return lax.ppermute(array, axis, pairs)


def runs_of(first, count):
    runs, last = [], first + count
    while first < last:
        run = 8 if first % 8 == 0 and first + 8 <= last else 4
        runs.append((first, run))
        first += run
    return runs


def hops_of(size, reach):
    hops = []
    while reach > 0:
        hops.append(min(size, reach))
        reach -= hops[-1]
    return hops


class CrossMessage:
    def __init__(self, layers, chunks, first, count):
        self.first, self.lanes, self.chunks = first, count // chunks, chunks
        self.share = LANES // self.lanes
        self.items = layers // 2 * chunks
        self.each = -(-self.items // self.share)
        self.size = 4 * self.each

    def place(self, layer_no, chunk):
        item = layer_no // 2 * self.chunks + chunk
        return item // self.share, item % self.share * self.lanes


class RowMessage:
    def __init__(self, layers, first, count, extra, tiles_of):
        self.parts, self.size = [], 0
        for which in range(2):
            for start, run in runs_of(first, count):
                self.parts.append((which, start, run, self.size))
                self.size += tiles_of(run)
        if extra is not None:
            self.parts.append((0, extra, 1, self.size))
            self.size += tiles_of(1)


class Plan:
    def __init__(self, cross_count, layers, rows, cols):
        self.coarsest = cross_count.bit_length()
        self.layers, self.own_rows, self.own_cols = layers, rows, cols
        self.row_reach = rounded_up(SWEEPS + 2 * self.coarsest, 4)
        reach = SWEEPS
        for _ in range(self.coarsest):
            reach = 2 * reach + 1
        self.col_reach = reach + 1
        chunks = 1
        while (chunks * LANES - cols) // 2 < self.col_reach:
            chunks *= 2
        self.chunks = chunks
        self.side_cols = (chunks * LANES - cols) // 2
        self.rows = rounded_up(rows + 2 * self.row_reach, 8)
        self.own_lane, self.own_lanes = self.side_cols // chunks, cols // chunks
        self.fold = LANES // self.own_lanes
        self.halves = chunks // self.fold
        hops = hops_of(cols, rounded_up(self.col_reach, chunks))
        self.cross_count = len(hops)
        self.cross = [CrossMessage(layers, chunks, cols - n, n) for n in hops]
        self.cross += [CrossMessage(layers, chunks, 0, n) for n in hops]
        self.cross_lane = [
            self.own_lane - hop * self.own_lanes - self.cross[hop].lanes for hop in range(len(hops))
        ] + [self.own_lane + (hop + 1) * self.own_lanes for hop in range(len(hops))]
        counts = hops_of(rows, self.row_reach)
        extra_hop, extra_row = divmod(self.row_reach, rows)
        counts += [0] * (extra_hop + 1 - len(counts))
        self.along_count = len(counts)
        self.along, self.corners, self.along_row = [], [], []
        for side in (-1, 1):
            for hop, n in enumerate(counts):
                first = rows - n if side < 0 else 0
                extra = None
                if hop == extra_hop:
                    extra = rows - 1 - extra_row if side < 0 else extra_row
                self.along.append(
                    RowMessage(layers, first, n, extra, lambda run: layers * run // 8 * self.halves)
                )
                self.corners.append(
                    RowMessage(
                        layers,
                        first,
                        n,
                        None,
                        lambda run: sum(each.each * run // 4 for each in self.cross),
                    )
                )
                self.along_row.append(self.row_reach + side * (hop + 1) * rows)

    def level_chunks(self, level_no):
        return max(1, self.chunks >> level_no)

    def spread(self, level_no):
        return max(1, (1 << level_no) // self.chunks)

    def own_tile(self, part, layer_no, half):
        share = 8 // part[2]
        return part[3] + layer_no // share * self.halves + half

    def corner_tile(self, part, message, parity, group):
        wide = part[2] // 4
        base = sum(each.each for each in self.cross[:message]) * wide
        return part[3] + base + (parity * self.cross[message].each if wide == 2 else 0) + group


def lane_numbers(rows):
    return lax.broadcasted_iota(jnp.int32, (rows, LANES), 1)


def taken(value, pick):
    return jnp.take_along_axis(value, pick, axis=1, mode="promise_in_bounds")


def edge_kernel(plan, both_ref, cells_ref, *out_refs):
    lane = lane_numbers(plan.own_rows)
    chunks, layers, cols = plan.chunks, plan.layers, plan.own_cols
    tiles = range(0, cols, LANES)
    cross_refs, along_refs = out_refs[: len(plan.cross)], out_refs[len(plan.cross) :]
    for message, out_ref in zip(plan.cross, cross_refs):
        lanes, share = message.lanes, message.share
        slot = lane // lanes
        for which in range(2):
            for group in range(message.each):
                low_item = group * share
                cell = message.first + chunks * (lane - slot * lanes)
                cell = cell + ((slot + low_item) & (chunks - 1))
                items = range(low_item, min(low_item + share, message.items))
                for parity in range(2):
                    value = None
                    for pair in sorted({item // chunks for item in items}):
                        low = max(pair * chunks - low_item, 0)
                        for start in tiles:
                            if start + LANES <= message.first:
                                continue
                            if start >= message.first + lanes * chunks:
                                continue
                            each = both_ref[which, 2 * pair + parity, :, start : start + LANES]
                            each = taken(each, cell & (LANES - 1))
                            if value is None:
                                value = each
                            else:
                                value = jnp.where((slot >= low) & (cell >= start), each, value)
                    out_ref[(which * 2 + parity) * message.each + group] = value
    place = (lane - plan.own_lane) & (LANES - 1)
    within = place & (plan.own_lanes - 1)
    for half in range(plan.halves):
        cell = chunks * within + half * plan.fold + place // plan.own_lanes
        pick = cell & (LANES - 1)
        for which in range(2):
            for layer_no in range(layers):
                value = None
                for start in tiles:
                    each = taken(both_ref[which, layer_no, :, start : start + LANES], pick)
                    value = each if value is None else jnp.where(cell >= start, each, value)
                cells_ref[which, layer_no, half] = value
                for message, out_ref in zip(plan.along, along_refs):
                    for part in message.parts:
                        if part[0] == which:
                            start, run = part[1], part[2]
                            low = layer_no % (8 // run) * run
                            tile = plan.own_tile(part, layer_no, half)
                            out_ref[tile, low : low + run] = value[start : start + run]


def corner_kernel(plan, *refs):
    halo_refs, out_refs = refs[: len(plan.cross)], refs[len(plan.cross) :]
    for corner, out_ref in zip([each for each in plan.corners if each.size], out_refs):
        for part in corner.parts:
            which, start, run, _ = part
            for message, halo_ref in enumerate(halo_refs):
                each = plan.cross[message].each
                for parity in range(2):
                    low = parity * 4 if run == 4 else 0
                    for group in range(each):
                        tile = plan.corner_tile(part, message, parity, group)
                        out_ref[tile, low : low + run] = halo_ref[
                            (which * 2 + parity) * each + group, start : start + run
                        ]


def turned(value, by):
    by %= LANES
    return pltpu.roll(value, by, 1) if by else value


def with_halos(plan, value, layer_no, chunk, halo_of):
    lane = lane_numbers(value.shape[0])
    value = turned(value, -(chunk % plan.fold) * plan.own_lanes)
    for message, packed in enumerate(plan.cross):
        group, offset = packed.place(layer_no, chunk)
        first = plan.cross_lane[message]
        cells = turned(halo_of(message, group), first - offset)
        if message < plan.cross_count:
            inside = lane < first + packed.lanes
        else:
            inside = lane >= first
        value = jnp.where(inside, cells, value)
    return value


def reciprocal(value):
    guess = pl.reciprocal(value, approx=True)
    return guess * (2.0 - value * guess)


def ratio(first, second):
    return first * second * reciprocal(jnp.maximum(first + second, TINY))


def first_of_pair(value, spread):
    lane = lane_numbers(value.shape[0])
    return (lane & spread) == 0


def paired(cells, spread):
    if len(cells) > 1:
        return [cells[2 * k] + cells[2 * k + 1] for k in range(len(cells) // 2)]
    value = cells[0]
    return [value + taken(value, lane_numbers(value.shape[0]) ^ spread)]


def firsts(cells, spread):
    if len(cells) > 1:
        return cells[0::2]
    value = cells[0]
    return [jnp.where(first_of_pair(value, spread), value, pltpu.roll(value, spread, 1))]


def cycle_kernel(plan, cells_ref, *refs):
    halos, hops = len(plan.cross), len(plan.along)
    halo_refs, refs = refs[:halos], refs[halos:]
    along_refs, refs = refs[:hops], refs[hops:]
    sent = [each for each in plan.corners if each.size]
    corner_refs, refs = refs[: len(sent)], refs[len(sent) :]
    corner_refs = {id(each): ref for each, ref in zip(sent, corner_refs)}
    pressure_ref, residual_ref = refs[:2]
    upright, upper0, origin = refs[2:5]
    rest = refs[5:]
    levels = plan.coarsest + 1
    coarsest = plan.coarsest
    layers, rows = plan.layers, plan.rows
    reach, own_rows = plan.row_reach, plan.own_rows
    west, south, factor, inverse, value, forcing = [
        rest[i * levels : (i + 1) * levels] for i in range(6)
    ]
    upper = [upper0] + list(forcing[1:])
    density = value[0]
    count = [plan.level_chunks(m) for m in range(levels)]
    spread = [plan.spread(m) for m in range(levels)]

    origin[0] = 0
    start0 = origin[0]

    def span(low, high):
        if low % 8 == 0 and high % 8 == 0:
            return pl.ds(low, high - low)
        return pl.ds(start0 + low, high - low)

    for which, target, guard in ((0, density, GUARD), (1, forcing[0], 0)):
        for c in range(count[0]):
            half = c // plan.fold
            for layer_no in range(layers):
                parity = layer_no % 2
                target[layer_no, c, span(guard + reach, guard + reach + own_rows)] = with_halos(
                    plan,
                    cells_ref[which, layer_no, half],
                    layer_no,
                    c,
                    lambda k, group: halo_refs[k][
                        (which * 2 + parity) * plan.cross[k].each + group
                    ],
                )
            for message, corner, along_ref, row in zip(
                plan.along, plan.corners, along_refs, plan.along_row
            ):
                for index, part in enumerate(message.parts):
                    if part[0] != which:
                        continue
                    first, run = guard + row + part[1], part[2]
                    share = 8 // run
                    for layer_no in range(0, layers, share):
                        now = along_ref[plan.own_tile(part, layer_no, half)]
                        if run == 1:
                            now = turned(now, -(c % plan.fold) * plan.own_lanes)
                        else:
                            now = with_halos(
                                plan,
                                now,
                                layer_no,
                                c,
                                lambda k, group: corner_refs[id(corner)][
                                    plan.corner_tile(corner.parts[index], k, layer_no % 2, group)
                                ],
                            )
                        for i in range(share):
                            target[layer_no + i, c, span(first, first + run)] = now[
                                i * run : (i + 1) * run
                            ]

    def faces(layer_no, first):
        cells = [density[layer_no, c, GUARD : GUARD + rows] for c in range(count[0])]
        souths = []
        for c in range(count[0]):
            behind = cells[c - 1] if c else pltpu.roll(cells[-1], 1, 1)
            souths.append(2.0 * cross_weight * ratio(cells[c], behind))
        for m in range(levels):
            if m > 0:
                souths = [0.5 * each for each in firsts(souths, spread[m - 1])]
            for c in range(count[m]):
                south[m][layer_no, c] = souths[c]
            south[m][layer_no, count[m]] = pltpu.roll(souths[0], LANES - spread[m], 1)
        uppers = []
        for c in range(count[0]):
            if first:
                uppers.append(2.0 * vertical_weight * cells[c])
            else:
                above = density[layer_no - 1, c, GUARD : GUARD + rows]
                uppers.append(2.0 * vertical_weight * ratio(cells[c], above))
        for m in range(levels):
            if m > 0:
                uppers = paired(uppers, spread[m - 1])
            for c in range(count[m]):
                upper[m][layer_no, c] = uppers[c]
        wests = []
        for c in range(count[0]):
            here = density[layer_no, c, GUARD : 2 * GUARD + rows]
            behind = density[layer_no, c, span(GUARD - 1, 2 * GUARD + rows - 1)]
            wests.append(2.0 * along_weight * ratio(here, behind))
        for m in range(levels):
            if m > 0:
                wests = paired(wests, spread[m - 1])
            for c in range(count[m]):
                west[m][layer_no, c] = wests[c]

    faces(0, True)
    pl.loop(1, layers, unroll=3)(lambda layer_no: faces(layer_no, False))
    for m in range(levels):
        for c in range(count[m]):
            upper[m][layers, c] = jnp.zeros((rows, LANES), jnp.float32)

    def clear_guards(layer_no):
        zeros = jnp.zeros((GUARD, LANES), jnp.float32)
        for m in range(levels):
            for c in range(count[m]):
                value[m][layer_no, c, 0:GUARD] = zeros
                value[m][layer_no, c, GUARD + rows : 2 * GUARD + rows] = zeros

    pl.loop(0, layers, unroll=4)(clear_guards)

    def pivots(some, layer_no, before, first):
        after = []
        for m in some:
            for c in range(count[m]):
                above = upper[m][layer_no, c]
                centre = (
                    west[m][layer_no, c, 0:rows]
                    + west[m][layer_no, c, span(1, rows + 1)]
                    + south[m][layer_no, c]
                    + south[m][layer_no, c + 1]
                    + above
                    + upper[m][layer_no + 1, c]
                )
                if first:
                    pivot = centre
                else:
                    share = above * before[len(after)]
                    factor[m][layer_no, c] = share
                    pivot = centre - above * share
                inverted = reciprocal(jnp.maximum(pivot, TINY))
                inverse[m][layer_no, c] = relaxation * inverted
                after.append(inverted)
        return tuple(after)

    for some in (range(1), range(1, levels)):
        lax.fori_loop(
            1,
            layers,
            lambda z, before: pivots(some, z, before, False),
            pivots(some, 0, None, True),
            unroll=3,
        )

    def around(m, layer_no, c, low, high):
        own = span(GUARD + low, GUARD + high)
        last = count[m] - 1
        behind = value[m][layer_no, c - 1 if c else last, own]
        ahead = value[m][layer_no, 0 if c == last else c + 1, own]
        if c == 0:
            behind = pltpu.roll(behind, spread[m], 1)
        if c == last:
            ahead = pltpu.roll(ahead, LANES - spread[m], 1)
        return (
            west[m][layer_no, c, span(low, high)]
            * value[m][layer_no, c, span(GUARD + low - 1, GUARD + high - 1)]
            + west[m][layer_no, c, span(low + 1, high + 1)]
            * value[m][layer_no, c, span(GUARD + low + 1, GUARD + high + 1)]
            + south[m][layer_no, c, span(low, high)] * behind
            + south[m][layer_no, c + 1, span(low, high)] * ahead
        )

    def solve(m, low, high, right_side, held, offset, store):
        place = slice(offset + low, offset + high)
        now = [None] * count[m]
        for layer_no in range(layers):
            for c in range(count[m]):
                each = right_side(layer_no, c)
                if layer_no:
                    each = each + factor[m][layer_no, c, low:high] * now[c]
                now[c] = each
                held[layer_no, c, place] = each * inverse[m][layer_no, c, low:high]
        for layer_no in range(layers - 1, -1, -1):
            for c in range(count[m]):
                each = held[layer_no, c, place]
                if layer_no < layers - 1:
                    each = each + factor[m][layer_no + 1, c, low:high] * now[c]
                now[c] = each
                store(layer_no, c, each)

    def first_sweep(m):
        def store(layer_no, c, now):
            value[m][layer_no, c, GUARD : GUARD + rows] = now

        solve(m, 0, rows, lambda z, c: forcing[m][z, c], value[m], GUARD, store)

    def later_sweep(m, low, high, prolong):
        place = slice(GUARD + low, GUARD + high)

        def right_side(layer_no, c):
            return forcing[m][layer_no, c, low:high] + around(m, layer_no, c, low, high)

        def store(layer_no, c, now):
            new = (1.0 - relaxation) * value[m][layer_no, c, place] + now
            value[m][layer_no, c, place] = new
            if prolong:
                children = (2 * c, 2 * c + 1) if count[m - 1] > count[m] else (c,)
                for child in children:
                    value[m - 1][layer_no, child, place] += new

        held = upright if m == coarsest else inverse[m]
        solve(m, low, high, right_side, held, 0, store)

    for m in range(coarsest):
        first_sweep(m)

        def remain_of(layer_no, c, m=m):
            kept = (1.0 - relaxation) * forcing[m][layer_no, c]
            return kept + around(m, layer_no, c, 0, rows)

        def restrict(layer_no, m=m, remain_of=remain_of):
            for c in range(count[m + 1]):
                if count[m] > 1:
                    both = remain_of(layer_no, 2 * c) + remain_of(layer_no, 2 * c + 1)
                else:
                    (both,) = paired([remain_of(layer_no, c)], spread[m])
                forcing[m + 1][layer_no, c] = both

        pl.loop(0, layers, unroll=layers if count[m] == 1 else 4)(restrict)

    first_sweep(coarsest)
    for sweep_no in range(1, SWEEPS):
        later_sweep(coarsest, 0, rows, sweep_no == SWEEPS - 1)

    for m in range(coarsest - 1, -1, -1):
        low = (reach - m - 1) // 8 * 8
        high = rounded_up(reach + own_rows + m + 1, 8)
        later_sweep(m, low, high, m > 0)

    chunks = count[0]
    lane = lane_numbers(own_rows)

    def in_order(cells, tile_no):
        start = (plan.side_cols + tile_no * LANES) // chunks
        pick = start + lane // chunks
        out = taken(cells[0], pick)
        for c in range(1, chunks):
            out = jnp.where((lane & (chunks - 1)) == c, taken(cells[c], pick), out)
        return out

    def finish(layer_no, top, bottom):
        low, high = reach, reach + own_rows
        own = span(GUARD + low, GUARD + high)
        plain = span(low, high)
        cells, remains = [], []
        for c in range(chunks):
            now = value[0][layer_no, c, own]
            centre = (
                west[0][layer_no, c, plain]
                + west[0][layer_no, c, span(low + 1, high + 1)]
                + south[0][layer_no, c, plain]
                + south[0][layer_no, c + 1, plain]
                + upper[0][layer_no, c, plain]
                + upper[0][layer_no + 1, c, plain]
            )
            remain = (
                forcing[0][layer_no, c, plain] - centre * now + around(0, layer_no, c, low, high)
            )
            if not top:
                remain += upper[0][layer_no, c, plain] * value[0][layer_no - 1, c, own]
            if not bottom:
                remain += upper[0][layer_no + 1, c, plain] * value[0][layer_no + 1, c, own]
            cells.append(now)
            remains.append(remain)
        for tile_no in range(plan.own_cols // LANES):
            columns = slice(tile_no * LANES, (tile_no + 1) * LANES)
            pressure_ref[layer_no, :, columns] = in_order(cells, tile_no)
            residual_ref[layer_no, :, columns] = in_order(remains, tile_no)

    finish(0, True, False)
    pl.loop(1, layers - 1, unroll=2)(lambda layer_no: finish(layer_no, False, False))
    finish(layers - 1, False, True)


def per_device(source, inv_density):
    layers, rows, cols = source.shape
    plan = Plan(lax.axis_size("cross"), layers, rows, cols)
    levels = plan.coarsest + 1
    vmem = pl.BlockSpec(memory_space=pltpu.VMEM)

    shape = functools.partial(jax.ShapeDtypeStruct, dtype=jnp.float32)

    def kernel(body, inputs, outputs):
        return pl.pallas_call(
            functools.partial(body, plan),
            out_shape=outputs,
            in_specs=[vmem] * len(inputs),
            out_specs=[vmem] * len(outputs),
            compiler_params=pltpu.CompilerParams(vmem_limit_bytes=16 << 20),
        )(*inputs)

    def exchanged(sent, axis, hops):
        got = [shifted(sent[hop], axis, hop + 1) for hop in range(hops)]
        return got + [shifted(sent[hops + hop], axis, -hop - 1) for hop in range(len(sent) - hops)]

    cells, *sent = kernel(
        edge_kernel,
        [jnp.stack([inv_density, source])],
        [shape((2, layers, plan.halves, rows, LANES))]
        + [shape((each.size, rows, LANES)) for each in plan.cross]
        + [shape((each.size, 8, LANES)) for each in plan.along],
    )
    halos = exchanged(sent[: len(plan.cross)], "cross", plan.cross_count)
    beside = exchanged(sent[len(plan.cross) :], "along", plan.along_count)
    sizes = [each.size for each in plan.corners if each.size]
    sent = kernel(corner_kernel, halos, [shape((size, 8, LANES)) for size in sizes])
    corners = exchanged(sent, "along", len(sent) // 2)
    inputs = [cells, *halos, *beside, *corners]

    def room(*shape):
        return pltpu.VMEM(shape + (LANES,), jnp.float32)

    total, high = plan.rows, plan.rows + GUARD
    counts = [plan.level_chunks(m) for m in range(levels)]
    scratch = [
        room(layers, counts[-1], total),
        room(layers + 1, counts[0], total),
        pltpu.SMEM((1,), jnp.int32),
    ]
    scratch += [room(layers, n, high) for n in counts]
    scratch += [room(layers, n + 1, total) for n in counts]
    scratch += [room(layers, n, total) for n in counts]
    scratch += [room(layers, n, total) for n in counts]
    scratch += [room(layers, n, high + GUARD) for n in counts]
    scratch += [room(layers, counts[0], total)]
    scratch += [room(layers + 1, n, total) for n in counts[1:]]
    held = sum(math.prod(each.shape) for each in scratch) + sum(each.size for each in inputs)
    held = 4 * (held + 2 * source.size)
    return pl.pallas_call(
        functools.partial(cycle_kernel, plan),
        out_shape=[jax.ShapeDtypeStruct((layers, rows, cols), jnp.float32)] * 2,
        in_specs=[vmem] * len(inputs),
        out_specs=[vmem] * 2,
        scratch_shapes=scratch,
        compiler_params=pltpu.CompilerParams(vmem_limit_bytes=held + (3 << 20)),
    )(*inputs)


def solution(mesh):
    return jax.shard_map(
        per_device,
        mesh=mesh,
        in_specs=(P(None, "along", "cross"), P(None, "along", "cross")),
        out_specs=(P(None, "along", "cross"), P(None, "along", "cross")),
        check_vma=False,
    )
```

time: 52.5 us -> 42.6 us (0.81)
  the two profiles are of different devices: /device:TPU:6 before, /device:TPU:9 now
where the time goes in v4:
time: 42.6 us; the launch traced here: 42.4 us
  starting transfers between devices  17.8 us (42%)
  Pallas kernels  15.3 us (36%)
  waiting for transfers between devices  7.55 us (18%)
  other arithmetic  1.06 us (2%)
  between operations  0.7 us (2%)
    ppermute x6, starting transfers between devices, shifted(): return lax.ppermute(array, axis, pairs)  17.8 us
    pallas_call x1, Pallas kernels, per_device(): pl.pallas_call(functools.partial(cycle_kernel, plan), out_shape=[jax.Shap...  14.6 us
    ppermute x6, waiting for transfers between devices, shifted(): return lax.ppermute(array, axis, pairs)  7.55 us
    another operation x1, other arithmetic, per_device(): jnp.stack([inv_density, source])  1.06 us
  transfers between devices with their start and end apart: 6, of which 4 were waited for; matrix products, arithmetic and copies ran while one was open for 0% of the time, Pallas kernels for 0%

profile of v4, /device:TPU:9, one launch (start us, length us, event | category | flops | bytes accessed | tf_op | source)
XLA Modules:
  0.0 42.4 jit_solution(14749523384762606674)
XLA Ops:
  0.6 1.1 %pad_maximum_fusion.both_ref = f32[2,16,16,256]{3,2,1,0:T(8,128)S(1)} fusion(f32[1,16,16,256]{3,2,1,0:T(8,128)} %bitcast.2, f32[1,16,16,256]{3,2,1,0:T(8,128)} %bitcast.3), kind=kLoop, calls=%fused_computation | loop fusion | flops 131072 | bytes 1048576 | tf_op jit(solution)/shard_map/stack | solution.py:571
  1.7 0.6 %shard_map.41 = (f32[2,16,2,16,128]{4,3,2,1,0:T(8,128)S(1)}, f32[24,16,128]{2,1,0:T(8,128)S(1)}, f32[24,16,128]{2,1,0:T(8,128)S(1)}, f32[100,8,128]{2,1,0:T(8,128)S(1)}, f32[100,8,128]{2,1,0:T(8,128)S(1)}) custom-call(f32[2,16,16,256]{3,2,1,0:T(8,128)S(1)} %pad_maximum_fusion.both_ref), custom_call_target="tpu_custom_call" | custom-call | tf_op jit(solution)/shard_map/pallas_call | solution.py:557
  2.3 3.1 %collective-permute-start = (f32[24,16,128]{2,1,0:T(8,128)S(1)}, f32[24,16,128]{2,1,0:T(8,128)S(1)}, u32[]{:S(2)}, u32[]{:S(2)}) collective-permute-start(f32[24,16,128]{2,1,0:T(8,128)S(1)} %get-tuple-element.10), channel_id=1, source_target_pairs={{0,4},{4,8},{8,12},{12,16},{16,20},{20,24},{24,28},{1,5},{5,9},{9,... | collective-permute-start | bytes 589832 | tf_op jit(solution)/shard_map/ppermute | solution.py:30
  5.5 3.0 %collective-permute-start.1 = (f32[24,16,128]{2,1,0:T(8,128)S(1)}, f32[24,16,128]{2,1,0:T(8,128)S(1)}, u32[]{:S(2)}, u32[]{:S(2)}) collective-permute-start(f32[24,16,128]{2,1,0:T(8,128)S(1)} %get-tuple-element.11), channel_id=1, source_target_pairs={{4,0},{8,4},{12,8},{16,12},{20,16},{24,20},{28,24},{5,1},{9,5},{13... | collective-permute-start | bytes 589832 | tf_op jit(solution)/shard_map/ppermute | solution.py:30
  8.5 4.2 %collective-permute-start.2 = (f32[100,8,128]{2,1,0:T(8,128)S(1)}, f32[100,8,128]{2,1,0:T(8,128)S(1)}, u32[]{:S(2)}, u32[]{:S(2)}) collective-permute-start(f32[100,8,128]{2,1,0:T(8,128)S(1)} %get-tuple-element.12), channel_id=1, source_target_pairs={{0,1},{1,2},{2,3},{4,5},{5,6},{6,7},{8,9},{9,10},{10,11},{12,13},{... | collective-permute-start | bytes 1228808 | tf_op jit(solution)/shard_map/ppermute | solution.py:30
  12.8 1.9 %collective-permute-start.3 = (f32[100,8,128]{2,1,0:T(8,128)S(1)}, f32[100,8,128]{2,1,0:T(8,128)S(1)}, u32[]{:S(2)}, u32[]{:S(2)}) collective-permute-start(f32[100,8,128]{2,1,0:T(8,128)S(1)} %get-tuple-element.13), channel_id=1, source_target_pairs={{1,0},{2,1},{3,2},{5,4},{6,5},{7,6},{9,8},{10,9},{11,10},{13,12},{... | collective-permute-start | bytes 1228808 | tf_op jit(solution)/shard_map/ppermute | solution.py:30
  14.7 0.0 collective-permute-done.refs_0_
  14.7 1.4 %collective-permute-done.1.refs_1_ = f32[24,16,128]{2,1,0:T(8,128)S(1)} collective-permute-done((f32[24,16,128]{2,1,0:T(8,128)S(1)}, f32[24,16,128]{2,1,0:T(8,128)S(1)}, u32[]{:S(2)}, u32[]{:S(2)}) %collective-permute-start.1) | collective-permute-done | bytes 196640 | tf_op jit(solution)/shard_map/ppermute | solution.py:30
  16.1 0.1 shard_map.42
  16.2 3.5 %collective-permute-start.4 = (f32[72,8,128]{2,1,0:T(8,128)S(1)}, f32[72,8,128]{2,1,0:T(8,128)S(1)}, u32[]{:S(2)}, u32[]{:S(2)}) collective-permute-start(f32[72,8,128]{2,1,0:T(8,128)S(1)} %get-tuple-element.14), channel_id=1, source_target_pairs={{0,1},{1,2},{2,3},{4,5},{5,6},{6,7},{8,9},{9,10},{10,11},{12,13},{... | collective-permute-start | bytes 884744 | tf_op jit(solution)/shard_map/ppermute | solution.py:30
  19.7 1.9 %collective-permute-start.5 = (f32[72,8,128]{2,1,0:T(8,128)S(1)}, f32[72,8,128]{2,1,0:T(8,128)S(1)}, u32[]{:S(2)}, u32[]{:S(2)}) collective-permute-start(f32[72,8,128]{2,1,0:T(8,128)S(1)} %get-tuple-element.15), channel_id=1, source_target_pairs={{1,0},{2,1},{3,2},{5,4},{6,5},{7,6},{9,8},{10,9},{11,10},{13,12},{... | collective-permute-start | bytes 884744 | tf_op jit(solution)/shard_map/ppermute | solution.py:30
  21.6 0.0 collective-permute-done.2.refs_2_
  21.7 0.4 collective-permute-done.3.refs_3_
  22.0 1.3 %collective-permute-done.4.refs_4_ = f32[72,8,128]{2,1,0:T(8,128)S(1)} collective-permute-done((f32[72,8,128]{2,1,0:T(8,128)S(1)}, f32[72,8,128]{2,1,0:T(8,128)S(1)}, u32[]{:S(2)}, u32[]{:S(2)}) %collective-permute-start.4) | collective-permute-done | bytes 294944 | tf_op jit(solution)/shard_map/ppermute | solution.py:30
  23.4 4.4 %collective-permute-done.5.refs_5_ = f32[72,8,128]{2,1,0:T(8,128)S(1)} collective-permute-done((f32[72,8,128]{2,1,0:T(8,128)S(1)}, f32[72,8,128]{2,1,0:T(8,128)S(1)}, u32[]{:S(2)}, u32[]{:S(2)}) %collective-permute-start.5) | collective-permute-done | bytes 294944 | tf_op jit(solution)/shard_map/ppermute | solution.py:30
  27.8 14.6 %shard_map.43 = (f32[16,16,256]{2,1,0:T(8,128)}, f32[16,16,256]{2,1,0:T(8,128)}) custom-call(f32[2,16,2,16,128]{4,3,2,1,0:T(8,128)S(1)} %get-tuple-element.9.cells_ref, f32[24,16,128]{2,1,0:T(8,128)S(1)} %collective-permute-done.refs_0_, f32[24,16,128]{2,1,0:T(8,128)S(1)} %collective-permute-done.1.refs_1_, ...), custom_call_target="tpu_custom_call" | custom-call | tf_op jit(solution)/shard_map/pallas_call | solution.py:602
Async XLA Ops:
  2.3 12.4 %collective-permute-start = (f32[24,16,128]{2,1,0:T(8,128)S(1)}, f32[24,16,128]{2,1,0:T(8,128)S(1)}, u32[]{:S(2)}, u32[]{:S(2)}) collective-permute-start(f32[24,16,128]{2,1,0:T(8,128)S(1)} %get-tuple-element.10), channel_id=1, source_target_pairs={{0,4},{4,8},{8,12},{12,16},{16,20},{20,24},{24,28},{1,5},{5,9},{9,... | collective-permute-start | bytes 589832 | tf_op jit(solution)/shard_map/ppermute | solution.py:30
  5.5 10.7 %collective-permute-start.1 = (f32[24,16,128]{2,1,0:T(8,128)S(1)}, f32[24,16,128]{2,1,0:T(8,128)S(1)}, u32[]{:S(2)}, u32[]{:S(2)}) collective-permute-start(f32[24,16,128]{2,1,0:T(8,128)S(1)} %get-tuple-element.11), channel_id=1, source_target_pairs={{4,0},{8,4},{12,8},{16,12},{20,16},{24,20},{28,24},{5,1},{9,5},{13... | collective-permute-start | bytes 589832 | tf_op jit(solution)/shard_map/ppermute | solution.py:30
  8.5 13.1 %collective-permute-start.2 = (f32[100,8,128]{2,1,0:T(8,128)S(1)}, f32[100,8,128]{2,1,0:T(8,128)S(1)}, u32[]{:S(2)}, u32[]{:S(2)}) collective-permute-start(f32[100,8,128]{2,1,0:T(8,128)S(1)} %get-tuple-element.12), channel_id=1, source_target_pairs={{0,1},{1,2},{2,3},{4,5},{5,6},{6,7},{8,9},{9,10},{10,11},{12,13},{... | collective-permute-start | bytes 1228808 | tf_op jit(solution)/shard_map/ppermute | solution.py:30
  12.8 9.3 %collective-permute-start.3 = (f32[100,8,128]{2,1,0:T(8,128)S(1)}, f32[100,8,128]{2,1,0:T(8,128)S(1)}, u32[]{:S(2)}, u32[]{:S(2)}) collective-permute-start(f32[100,8,128]{2,1,0:T(8,128)S(1)} %get-tuple-element.13), channel_id=1, source_target_pairs={{1,0},{2,1},{3,2},{5,4},{6,5},{7,6},{9,8},{10,9},{11,10},{13,12},{... | collective-permute-start | bytes 1228808 | tf_op jit(solution)/shard_map/ppermute | solution.py:30
  16.2 7.2 %collective-permute-start.4 = (f32[72,8,128]{2,1,0:T(8,128)S(1)}, f32[72,8,128]{2,1,0:T(8,128)S(1)}, u32[]{:S(2)}, u32[]{:S(2)}) collective-permute-start(f32[72,8,128]{2,1,0:T(8,128)S(1)} %get-tuple-element.14), channel_id=1, source_target_pairs={{0,1},{1,2},{2,3},{4,5},{5,6},{6,7},{8,9},{9,10},{10,11},{12,13},{... | collective-permute-start | bytes 884744 | tf_op jit(solution)/shard_map/ppermute | solution.py:30
  19.7 8.0 %collective-permute-start.5 = (f32[72,8,128]{2,1,0:T(8,128)S(1)}, f32[72,8,128]{2,1,0:T(8,128)S(1)}, u32[]{:S(2)}, u32[]{:S(2)}) collective-permute-start(f32[72,8,128]{2,1,0:T(8,128)S(1)} %get-tuple-element.15), channel_id=1, source_target_pairs={{1,0},{2,1},{3,2},{5,4},{6,5},{7,6},{9,8},{10,9},{11,10},{13,12},{... | collective-permute-start | bytes 884744 | tf_op jit(solution)/shard_map/ppermute | solution.py:30

commit v5 on v4

--- a/solution.py
+++ b/solution.py
@@ -24,10 +24,21 @@
     return -(-count // step) * step
 
 
-def shifted(array, axis, by):
+def swapped(array, axis, distance, second):
     devices = lax.axis_size(axis)
-    pairs = [(i, i + by) for i in range(devices) if 0 <= i + by < devices]
+    pairs = []
+    for i in range(devices - distance):
+        if i // distance % 2 == second:
+            pairs += [(i, i + distance), (i + distance, i)]
     return lax.ppermute(array, axis, pairs)
+
+
+def is_even(axis, distance):
+    return (lax.axis_index(axis) // distance) % 2 == 0
+
+
+def chosen(condition, first, second):
+    return jnp.where(condition, first, second), jnp.where(condition, second, first)
 
 
 def runs_of(first, count):
@@ -36,7 +47,7 @@
         run = 8 if first % 8 == 0 and first + 8 <= last else 4
         runs.append((first, run))
         first += run
-    return runs
+    return sorted(runs, key=lambda each: -each[1])
 
 
 def hops_of(size, reach):
@@ -151,31 +162,42 @@
     chunks, layers, cols = plan.chunks, plan.layers, plan.own_cols
     tiles = range(0, cols, LANES)
     cross_refs, along_refs = out_refs[: len(plan.cross)], out_refs[len(plan.cross) :]
-    for message, out_ref in zip(plan.cross, cross_refs):
+    def packed(message, which, group, parity):
         lanes, share = message.lanes, message.share
         slot = lane // lanes
+        low_item = group * share
+        cell = message.first + chunks * (lane - slot * lanes)
+        cell = cell + ((slot + low_item) & (chunks - 1))
+        items = range(low_item, min(low_item + share, message.items))
+        value = None
+        for pair in sorted({item // chunks for item in items}):
+            low = max(pair * chunks - low_item, 0)
+            for start in tiles:
+                if start + LANES <= message.first or start >= message.first + lanes * chunks:
+                    continue
+                each = both_ref[which, 2 * pair + parity, :, start : start + LANES]
+                each = taken(each, cell & (LANES - 1))
+                if value is None:
+                    value = each
+                else:
+                    value = jnp.where((slot >= low) & (cell >= start), each, value)
+        return value
+
+    hops = plan.cross_count
+    for hop in range(hops):
+        even = is_even("cross", hop + 1)
+        tail, head = plan.cross[hop], plan.cross[hops + hop]
         for which in range(2):
-            for group in range(message.each):
-                low_item = group * share
-                cell = message.first + chunks * (lane - slot * lanes)
-                cell = cell + ((slot + low_item) & (chunks - 1))
-                items = range(low_item, min(low_item + share, message.items))
-                for parity in range(2):
-                    value = None
-                    for pair in sorted({item // chunks for item in items}):
-                        low = max(pair * chunks - low_item, 0)
-                        for start in tiles:
-                            if start + LANES <= message.first:
-                                continue
-                            if start >= message.first + lanes * chunks:
-                                continue
-                            each = both_ref[which, 2 * pair + parity, :, start : start + LANES]
-                            each = taken(each, cell & (LANES - 1))
-                            if value is None:
-                                value = each
-                            else:
-                                value = jnp.where((slot >= low) & (cell >= start), each, value)
-                    out_ref[(which * 2 + parity) * message.each + group] = value
+            for parity in range(2):
+                for group in range(tail.each):
+                    row = (which * 2 + parity) * tail.each + group
+                    cross_refs[2 * hop + 1][row], cross_refs[2 * hop][row] = chosen(
+                        even,
+                        packed(tail, which, group, parity),
+                        packed(head, which, group, parity),
+                    )
+    hops = plan.along_count
+    evens = [is_even("along", hop + 1) for hop in range(hops)]
     place = (lane - plan.own_lane) & (LANES - 1)
     within = place & (plan.own_lanes - 1)
     for half in range(plan.halves):
@@ -188,29 +210,52 @@
                     each = taken(both_ref[which, layer_no, :, start : start + LANES], pick)
                     value = each if value is None else jnp.where(cell >= start, each, value)
                 cells_ref[which, layer_no, half] = value
-                for message, out_ref in zip(plan.along, along_refs):
-                    for part in message.parts:
-                        if part[0] == which:
-                            start, run = part[1], part[2]
+                for hop in range(hops):
+                    tail, head = plan.along[hop], plan.along[hops + hop]
+                    for last, first in zip(tail.parts, head.parts):
+                        if last[0] == which:
+                            run = last[2]
                             low = layer_no % (8 // run) * run
-                            tile = plan.own_tile(part, layer_no, half)
-                            out_ref[tile, low : low + run] = value[start : start + run]
+                            tile = plan.own_tile(last, layer_no, half)
+                            one, two = chosen(
+                                evens[hop],
+                                value[last[1] : last[1] + run],
+                                value[first[1] : first[1] + run],
+                            )
+                            along_refs[2 * hop + 1][tile, low : low + run] = one
+                            along_refs[2 * hop][tile, low : low + run] = two
 
 
 def corner_kernel(plan, *refs):
-    halo_refs, out_refs = refs[: len(plan.cross)], refs[len(plan.cross) :]
-    for corner, out_ref in zip([each for each in plan.corners if each.size], out_refs):
-        for part in corner.parts:
-            which, start, run, _ = part
+    hops = plan.cross_count
+    got_refs, halo_refs, out_refs = refs[: 2 * hops], refs[2 * hops : 4 * hops], refs[4 * hops :]
+    for hop in range(hops):
+        even = is_even("cross", hop + 1)
+        halo_refs[hops + hop][...], halo_refs[hop][...] = chosen(
+            even, got_refs[2 * hop + 1][...], got_refs[2 * hop][...]
+        )
+    hops = plan.along_count
+    for hop in range(hops):
+        tail, head = plan.corners[hop], plan.corners[hops + hop]
+        if not tail.size:
+            continue
+        even = is_even("along", hop + 1)
+        for last, first in zip(tail.parts, head.parts):
+            which, run = last[0], last[2]
             for message, halo_ref in enumerate(halo_refs):
                 each = plan.cross[message].each
                 for parity in range(2):
                     low = parity * 4 if run == 4 else 0
                     for group in range(each):
-                        tile = plan.corner_tile(part, message, parity, group)
-                        out_ref[tile, low : low + run] = halo_ref[
-                            (which * 2 + parity) * each + group, start : start + run
-                        ]
+                        tile = plan.corner_tile(last, message, parity, group)
+                        row = (which * 2 + parity) * each + group
+                        one, two = chosen(
+                            even,
+                            halo_ref[row, last[1] : last[1] + run],
+                            halo_ref[row, first[1] : first[1] + run],
+                        )
+                        out_refs[2 * hop + 1][tile, low : low + run] = one
+                        out_refs[2 * hop][tile, low : low + run] = two
 
 
 def turned(value, by):
@@ -265,9 +310,8 @@
     halos, hops = len(plan.cross), len(plan.along)
     halo_refs, refs = refs[:halos], refs[halos:]
     along_refs, refs = refs[:hops], refs[hops:]
-    sent = [each for each in plan.corners if each.size]
-    corner_refs, refs = refs[: len(sent)], refs[len(sent) :]
-    corner_refs = {id(each): ref for each, ref in zip(sent, corner_refs)}
+    sent = sum(each.size > 0 for each in plan.corners)
+    corner_refs, refs = refs[:sent], refs[sent:]
     pressure_ref, residual_ref = refs[:2]
     upright, upper0, origin = refs[2:5]
     rest = refs[5:]
@@ -305,16 +349,25 @@
                         (which * 2 + parity) * plan.cross[k].each + group
                     ],
                 )
-            for message, corner, along_ref, row in zip(
-                plan.along, plan.corners, along_refs, plan.along_row
+            for side, (message, corner, row) in enumerate(
+                zip(plan.along, plan.corners, plan.along_row)
             ):
+                after, hop = divmod(side, plan.along_count)
+                even = is_even("along", hop + 1)
+
+                def got(pair, tile):
+                    two, one = pair[2 * hop], pair[2 * hop + 1]
+                    return jnp.where(even, one[tile], two[tile]) if after else jnp.where(
+                        even, two[tile], one[tile]
+                    )
+
                 for index, part in enumerate(message.parts):
                     if part[0] != which:
                         continue
                     first, run = guard + row + part[1], part[2]
                     share = 8 // run
                     for layer_no in range(0, layers, share):
-                        now = along_ref[plan.own_tile(part, layer_no, half)]
+                        now = got(along_refs, plan.own_tile(part, layer_no, half))
                         if run == 1:
                             now = turned(now, -(c % plan.fold) * plan.own_lanes)
                         else:
@@ -323,9 +376,10 @@
                                 now,
                                 layer_no,
                                 c,
-                                lambda k, group: corner_refs[id(corner)][
-                                    plan.corner_tile(corner.parts[index], k, layer_no % 2, group)
-                                ],
+                                lambda k, group: got(
+                                    corner_refs,
+                                    plan.corner_tile(corner.parts[index], k, layer_no % 2, group),
+                                ),
                             )
                         for i in range(share):
                             target[layer_no + i, c, span(first, first + run)] = now[
@@ -562,22 +616,29 @@
             compiler_params=pltpu.CompilerParams(vmem_limit_bytes=16 << 20),
         )(*inputs)
 
-    def exchanged(sent, axis, hops):
-        got = [shifted(sent[hop], axis, hop + 1) for hop in range(hops)]
-        return got + [shifted(sent[hops + hop], axis, -hop - 1) for hop in range(len(sent) - hops)]
-
+    def exchanged(sent, axis):
+        return [
+            swapped(each, axis, index // 2 + 1, 1 - index % 2) for index, each in enumerate(sent)
+        ]
+
+    def pairs_of(messages, *tail):
+        half = len(messages) // 2
+        return [shape((each.size,) + tail) for each in messages[:half] if each.size for _ in range(2)]
+
+    cross_shapes = pairs_of(plan.cross, rows, LANES)
+    halo_shapes = [shape((each.size, rows, LANES)) for each in plan.cross]
     cells, *sent = kernel(
         edge_kernel,
         [jnp.stack([inv_density, source])],
         [shape((2, layers, plan.halves, rows, LANES))]
-        + [shape((each.size, rows, LANES)) for each in plan.cross]
-        + [shape((each.size, 8, LANES)) for each in plan.along],
+        + cross_shapes
+        + pairs_of(plan.along, 8, LANES),
     )
-    halos = exchanged(sent[: len(plan.cross)], "cross", plan.cross_count)
-    beside = exchanged(sent[len(plan.cross) :], "along", plan.along_count)
-    sizes = [each.size for each in plan.corners if each.size]
-    sent = kernel(corner_kernel, halos, [shape((size, 8, LANES)) for size in sizes])
-    corners = exchanged(sent, "along", len(sent) // 2)
+    halos = exchanged(sent[: len(plan.cross)], "cross")
+    beside = exchanged(sent[len(plan.cross) :], "along")
+    sent = kernel(corner_kernel, halos, halo_shapes + pairs_of(plan.corners, 8, LANES))
+    halos, sent = sent[: len(halos)], sent[len(halos) :]
+    corners = exchanged(sent, "along")
     inputs = [cells, *halos, *beside, *corners]
 
     def room(*shape):

time: 42.6 us -> 39.2 us (0.920)
  the two profiles are of different devices: /device:TPU:9 before, /device:TPU:1 now
where the time goes in v5:
time: 39.2 us; the launch traced here: 38.9 us
  Pallas kernels  15.4 us (39%)
  starting transfers between devices  13.1 us (33%)
  waiting for transfers between devices  8.53 us (22%)
  other arithmetic  1.06 us (3%)
  between operations  0.71 us (2%)
    pallas_call x1, Pallas kernels, per_device(): pl.pallas_call(functools.partial(cycle_kernel, plan), out_shape=[jax.Shap...  14.6 us
    ppermute x6, starting transfers between devices, swapped(): return lax.ppermute(array, axis, pairs)  13.1 us
    ppermute x6, waiting for transfers between devices, swapped(): return lax.ppermute(array, axis, pairs)  8.53 us
    another operation x1, other arithmetic, per_device(): jnp.stack([inv_density, source])  1.06 us
    pallas_call x2, Pallas kernels, kernel(): pl.pallas_call(functools.partial(body, plan), out_shape=outputs, in_specs...  0.8 us
  transfers between devices with their start and end apart: 6, of which 2 were waited for; matrix products, arithmetic and copies ran while one was open for 0% of the time, Pallas kernels for 0%

profile of v5, /device:TPU:1, one launch (start us, length us, event | category | flops | bytes accessed | tf_op | source)
XLA Modules:
  0.0 38.9 jit_solution(10627254075289828354)
XLA Ops:
  0.6 1.1 %pad_maximum_fusion.both_ref = f32[2,16,16,256]{3,2,1,0:T(8,128)S(1)} fusion(f32[1,16,16,256]{3,2,1,0:T(8,128)} %bitcast.2, f32[1,16,16,256]{3,2,1,0:T(8,128)} %bitcast.3), kind=kLoop, calls=%fused_computation | loop fusion | flops 131072 | bytes 1048576 | tf_op jit(solution)/shard_map/stack | solution.py:632
  1.7 0.7 %shard_map.41 = (f32[2,16,2,16,128]{4,3,2,1,0:T(8,128)S(1)}, f32[24,16,128]{2,1,0:T(8,128)S(1)}, f32[24,16,128]{2,1,0:T(8,128)S(1)}, f32[100,8,128]{2,1,0:T(8,128)S(1)}, f32[100,8,128]{2,1,0:T(8,128)S(1)}) custom-call(f32[2,16,16,256]{3,2,1,0:T(8,128)S(1)} %pad_maximum_fusion.both_ref), custom_call_target="tpu_custom_call" | custom-call | tf_op jit(solution)/shard_map/pallas_call | solution.py:611
  2.4 0.7 %collective-permute-start = (f32[24,16,128]{2,1,0:T(8,128)S(1)}, f32[24,16,128]{2,1,0:T(8,128)S(1)}, u32[]{:S(2)}, u32[]{:S(2)}) collective-permute-start(f32[24,16,128]{2,1,0:T(8,128)S(1)} %get-tuple-element.12), channel_id=1, source_target_pairs={{4,8},{8,4},{12,16},{16,12},{20,24},{24,20},{5,9},{9,5},{13,17},{1... | collective-permute-start | bytes 589832 | tf_op jit(solution)/shard_map/ppermute | solution.py:33
  3.1 4.6 %collective-permute-start.1 = (f32[24,16,128]{2,1,0:T(8,128)S(1)}, f32[24,16,128]{2,1,0:T(8,128)S(1)}, u32[]{:S(2)}, u32[]{:S(2)}) collective-permute-start(f32[24,16,128]{2,1,0:T(8,128)S(1)} %get-tuple-element.13), channel_id=1, source_target_pairs={{0,4},{4,0},{8,12},{12,8},{16,20},{20,16},{24,28},{28,24},{1,5},{5... | collective-permute-start | bytes 589832 | tf_op jit(solution)/shard_map/ppermute | solution.py:33
  7.7 4.2 %collective-permute-start.2 = (f32[100,8,128]{2,1,0:T(8,128)S(1)}, f32[100,8,128]{2,1,0:T(8,128)S(1)}, u32[]{:S(2)}, u32[]{:S(2)}) collective-permute-start(f32[100,8,128]{2,1,0:T(8,128)S(1)} %get-tuple-element.16), channel_id=1, source_target_pairs={{1,2},{2,1},{5,6},{6,5},{9,10},{10,9},{13,14},{14,13},{17,18},{18,... | collective-permute-start | bytes 1228808 | tf_op jit(solution)/shard_map/ppermute | solution.py:33
  11.9 0.1 collective-permute-start.3
  12.0 0.0 collective-permute-done.refs_0_
  12.0 4.1 %collective-permute-done.1.refs_1_ = f32[24,16,128]{2,1,0:T(8,128)S(1)} collective-permute-done((f32[24,16,128]{2,1,0:T(8,128)S(1)}, f32[24,16,128]{2,1,0:T(8,128)S(1)}, u32[]{:S(2)}, u32[]{:S(2)}) %collective-permute-start.1) | collective-permute-done | bytes 196640 | tf_op jit(solution)/shard_map/ppermute | solution.py:33
  16.1 0.1 shard_map.42
  16.2 3.5 %collective-permute-start.4 = (f32[72,8,128]{2,1,0:T(8,128)S(1)}, f32[72,8,128]{2,1,0:T(8,128)S(1)}, u32[]{:S(2)}, u32[]{:S(2)}) collective-permute-start(f32[72,8,128]{2,1,0:T(8,128)S(1)} %get-tuple-element.18), channel_id=1, source_target_pairs={{1,2},{2,1},{5,6},{6,5},{9,10},{10,9},{13,14},{14,13},{17,18},{18,... | collective-permute-start | bytes 884744 | tf_op jit(solution)/shard_map/ppermute | solution.py:33
  19.7 0.1 collective-permute-start.5
  19.8 0.0 collective-permute-done.2.refs_2_
  19.8 0.0 collective-permute-done.3.refs_3_
  19.8 4.4 %collective-permute-done.4.refs_4_ = f32[72,8,128]{2,1,0:T(8,128)S(1)} collective-permute-done((f32[72,8,128]{2,1,0:T(8,128)S(1)}, f32[72,8,128]{2,1,0:T(8,128)S(1)}, u32[]{:S(2)}, u32[]{:S(2)}) %collective-permute-start.4) | collective-permute-done | bytes 294944 | tf_op jit(solution)/shard_map/ppermute | solution.py:33
  24.2 0.0 collective-permute-done.5.refs_5_
  24.3 14.6 %shard_map.43 = (f32[16,16,256]{2,1,0:T(8,128)}, f32[16,16,256]{2,1,0:T(8,128)}) custom-call(f32[2,16,2,16,128]{4,3,2,1,0:T(8,128)S(1)} %get-tuple-element.11.cells_ref, f32[24,16,128]{2,1,0:T(8,128)S(1)} %get-tuple-element.14.refs_0_, f32[24,16,128]{2,1,0:T(8,128)S(1)} %get-tuple-element.15.refs_1_, f32[100,8,128]{2,1,0:T(8,128)S(1)} %collective-permute-done.2.refs_2_, ...), custom_call_target="tpu_custom_call" | custom-call | tf_op jit(solution)/shard_map/pallas_call | solution.py:663
Async XLA Ops:
  2.4 9.6 %collective-permute-start = (f32[24,16,128]{2,1,0:T(8,128)S(1)}, f32[24,16,128]{2,1,0:T(8,128)S(1)}, u32[]{:S(2)}, u32[]{:S(2)}) collective-permute-start(f32[24,16,128]{2,1,0:T(8,128)S(1)} %get-tuple-element.12), channel_id=1, source_target_pairs={{4,8},{8,4},{12,16},{16,12},{20,24},{24,20},{5,9},{9,5},{13,17},{1... | collective-permute-start | bytes 589832 | tf_op jit(solution)/shard_map/ppermute | solution.py:33
  3.1 13.0 %collective-permute-start.1 = (f32[24,16,128]{2,1,0:T(8,128)S(1)}, f32[24,16,128]{2,1,0:T(8,128)S(1)}, u32[]{:S(2)}, u32[]{:S(2)}) collective-permute-start(f32[24,16,128]{2,1,0:T(8,128)S(1)} %get-tuple-element.13), channel_id=1, source_target_pairs={{0,4},{4,0},{8,12},{12,8},{16,20},{20,16},{24,28},{28,24},{1,5},{5... | collective-permute-start | bytes 589832 | tf_op jit(solution)/shard_map/ppermute | solution.py:33
  7.7 12.1 %collective-permute-start.2 = (f32[100,8,128]{2,1,0:T(8,128)S(1)}, f32[100,8,128]{2,1,0:T(8,128)S(1)}, u32[]{:S(2)}, u32[]{:S(2)}) collective-permute-start(f32[100,8,128]{2,1,0:T(8,128)S(1)} %get-tuple-element.16), channel_id=1, source_target_pairs={{1,2},{2,1},{5,6},{6,5},{9,10},{10,9},{13,14},{14,13},{17,18},{18,... | collective-permute-start | bytes 1228808 | tf_op jit(solution)/shard_map/ppermute | solution.py:33
  11.9 7.9 %collective-permute-start.3 = (f32[100,8,128]{2,1,0:T(8,128)S(1)}, f32[100,8,128]{2,1,0:T(8,128)S(1)}, u32[]{:S(2)}, u32[]{:S(2)}) collective-permute-start(f32[100,8,128]{2,1,0:T(8,128)S(1)} %get-tuple-element.17), channel_id=1, source_target_pairs={{0,1},{1,0},{2,3},{3,2},{4,5},{5,4},{6,7},{7,6},{8,9},{9,8},{10,11... | collective-permute-start | bytes 1228808 | tf_op jit(solution)/shard_map/ppermute | solution.py:33
  16.2 8.0 %collective-permute-start.4 = (f32[72,8,128]{2,1,0:T(8,128)S(1)}, f32[72,8,128]{2,1,0:T(8,128)S(1)}, u32[]{:S(2)}, u32[]{:S(2)}) collective-permute-start(f32[72,8,128]{2,1,0:T(8,128)S(1)} %get-tuple-element.18), channel_id=1, source_target_pairs={{1,2},{2,1},{5,6},{6,5},{9,10},{10,9},{13,14},{14,13},{17,18},{18,... | collective-permute-start | bytes 884744 | tf_op jit(solution)/shard_map/ppermute | solution.py:33
  19.7 4.5 %collective-permute-start.5 = (f32[72,8,128]{2,1,0:T(8,128)S(1)}, f32[72,8,128]{2,1,0:T(8,128)S(1)}, u32[]{:S(2)}, u32[]{:S(2)}) collective-permute-start(f32[72,8,128]{2,1,0:T(8,128)S(1)} %get-tuple-element.19), channel_id=1, source_target_pairs={{0,1},{1,0},{2,3},{3,2},{4,5},{5,4},{6,7},{7,6},{8,9},{9,8},{10,11... | collective-permute-start | bytes 884744 | tf_op jit(solution)/shard_map/ppermute | solution.py:33

commit v6 on v5

--- a/solution.py
+++ b/solution.py
@@ -62,19 +62,19 @@
     def __init__(self, layers, chunks, first, count):
         self.first, self.lanes, self.chunks = first, count // chunks, chunks
         self.share = LANES // self.lanes
-        self.items = layers // 2 * chunks
-        self.each = -(-self.items // self.share)
-        self.size = 4 * self.each
-
-    def place(self, layer_no, chunk):
-        item = layer_no // 2 * self.chunks + chunk
+        self.half = layers // 2 * chunks
+        self.each = -(-2 * self.half // self.share)
+        self.size = 2 * self.each
+
+    def place(self, which, layer_no, chunk):
+        item = which * self.half + layer_no // 2 * self.chunks + chunk
         return item // self.share, item % self.share * self.lanes
 
 
 class RowMessage:
-    def __init__(self, layers, first, count, extra, tiles_of):
+    def __init__(self, arrays, first, count, extra, tiles_of):
         self.parts, self.size = [], 0
-        for which in range(2):
+        for which in range(arrays):
             for start, run in runs_of(first, count):
                 self.parts.append((which, start, run, self.size))
                 self.size += tiles_of(run)
@@ -120,16 +120,13 @@
                 if hop == extra_hop:
                     extra = rows - 1 - extra_row if side < 0 else extra_row
                 self.along.append(
-                    RowMessage(layers, first, n, extra, lambda run: layers * run // 8 * self.halves)
+                    RowMessage(2, first, n, extra, lambda run: layers * run // 8 * self.halves)
                 )
                 self.corners.append(
-                    RowMessage(
-                        layers,
-                        first,
-                        n,
-                        None,
-                        lambda run: sum(each.each * run // 4 for each in self.cross),
-                    )
+                    [
+                        RowMessage(1, first, n, None, lambda run: each.each * run // 4)
+                        for each in self.cross[: self.cross_count]
+                    ]
                 )
                 self.along_row.append(self.row_reach + side * (hop + 1) * rows)
 
@@ -143,10 +140,8 @@
         share = 8 // part[2]
         return part[3] + layer_no // share * self.halves + half
 
-    def corner_tile(self, part, message, parity, group):
-        wide = part[2] // 4
-        base = sum(each.each for each in self.cross[:message]) * wide
-        return part[3] + base + (parity * self.cross[message].each if wide == 2 else 0) + group
+    def corner_tile(self, part, cross_hop, parity, group):
+        return part[3] + (parity * self.cross[cross_hop].each if part[2] == 8 else 0) + group
 
 
 def lane_numbers(rows):
@@ -162,16 +157,17 @@
     chunks, layers, cols = plan.chunks, plan.layers, plan.own_cols
     tiles = range(0, cols, LANES)
     cross_refs, along_refs = out_refs[: len(plan.cross)], out_refs[len(plan.cross) :]
-    def packed(message, which, group, parity):
+    def packed(message, group, parity):
         lanes, share = message.lanes, message.share
         slot = lane // lanes
         low_item = group * share
         cell = message.first + chunks * (lane - slot * lanes)
         cell = cell + ((slot + low_item) & (chunks - 1))
-        items = range(low_item, min(low_item + share, message.items))
+        items = range(low_item, min(low_item + share, 2 * message.half))
         value = None
-        for pair in sorted({item // chunks for item in items}):
-            low = max(pair * chunks - low_item, 0)
+        for first in sorted({item // chunks * chunks for item in items}):
+            low = max(first - low_item, 0)
+            which, pair = first // message.half, first % message.half // chunks
             for start in tiles:
                 if start + LANES <= message.first or start >= message.first + lanes * chunks:
                     continue
@@ -187,15 +183,12 @@
     for hop in range(hops):
         even = is_even("cross", hop + 1)
         tail, head = plan.cross[hop], plan.cross[hops + hop]
-        for which in range(2):
-            for parity in range(2):
-                for group in range(tail.each):
-                    row = (which * 2 + parity) * tail.each + group
-                    cross_refs[2 * hop + 1][row], cross_refs[2 * hop][row] = chosen(
-                        even,
-                        packed(tail, which, group, parity),
-                        packed(head, which, group, parity),
-                    )
+        for parity in range(2):
+            for group in range(tail.each):
+                row = parity * tail.each + group
+                cross_refs[2 * hop + 1][row], cross_refs[2 * hop][row] = chosen(
+                    even, packed(tail, group, parity), packed(head, group, parity)
+                )
     hops = plan.along_count
     evens = [is_even("along", hop + 1) for hop in range(hops)]
     place = (lane - plan.own_lane) & (LANES - 1)
@@ -226,36 +219,28 @@
                             along_refs[2 * hop][tile, low : low + run] = two
 
 
-def corner_kernel(plan, *refs):
-    hops = plan.cross_count
-    got_refs, halo_refs, out_refs = refs[: 2 * hops], refs[2 * hops : 4 * hops], refs[4 * hops :]
-    for hop in range(hops):
-        even = is_even("cross", hop + 1)
-        halo_refs[hops + hop][...], halo_refs[hop][...] = chosen(
-            even, got_refs[2 * hop + 1][...], got_refs[2 * hop][...]
-        )
+def corner_kernel(cross_hop, plan, halo_ref, *out_refs):
+    each = plan.cross[cross_hop].each
     hops = plan.along_count
     for hop in range(hops):
-        tail, head = plan.corners[hop], plan.corners[hops + hop]
+        tail, head = plan.corners[hop][cross_hop], plan.corners[hops + hop][cross_hop]
         if not tail.size:
             continue
         even = is_even("along", hop + 1)
         for last, first in zip(tail.parts, head.parts):
-            which, run = last[0], last[2]
-            for message, halo_ref in enumerate(halo_refs):
-                each = plan.cross[message].each
-                for parity in range(2):
-                    low = parity * 4 if run == 4 else 0
-                    for group in range(each):
-                        tile = plan.corner_tile(last, message, parity, group)
-                        row = (which * 2 + parity) * each + group
-                        one, two = chosen(
-                            even,
-                            halo_ref[row, last[1] : last[1] + run],
-                            halo_ref[row, first[1] : first[1] + run],
-                        )
-                        out_refs[2 * hop + 1][tile, low : low + run] = one
-                        out_refs[2 * hop][tile, low : low + run] = two
+            run = last[2]
+            for parity in range(2):
+                low = parity * 4 if run == 4 else 0
+                for group in range(each):
+                    tile = plan.corner_tile(last, cross_hop, parity, group)
+                    row = parity * each + group
+                    one, two = chosen(
+                        even,
+                        halo_ref[row, last[1] : last[1] + run],
+                        halo_ref[row, first[1] : first[1] + run],
+                    )
+                    out_refs[2 * hop + 1][tile, low : low + run] = one
+                    out_refs[2 * hop][tile, low : low + run] = two
 
 
 def turned(value, by):
@@ -263,19 +248,53 @@
     return pltpu.roll(value, by, 1) if by else value
 
 
-def with_halos(plan, value, layer_no, chunk, halo_of):
-    lane = lane_numbers(value.shape[0])
-    value = turned(value, -(chunk % plan.fold) * plan.own_lanes)
-    for message, packed in enumerate(plan.cross):
-        group, offset = packed.place(layer_no, chunk)
-        first = plan.cross_lane[message]
-        cells = turned(halo_of(message, group), first - offset)
-        if message < plan.cross_count:
-            inside = lane < first + packed.lanes
-        else:
-            inside = lane >= first
-        value = jnp.where(inside, cells, value)
-    return value
+class Halos:
+    def __init__(self, plan):
+        self.plan, self.swaps, self.masks = plan, [], {}
+        for hop in range(plan.cross_count):
+            even = is_even("cross", hop + 1)
+            for before in (even, jnp.logical_not(even)):
+                low = jnp.where(before, 0, plan.cross_lane[plan.cross_count + hop])
+                high = jnp.where(before, plan.cross_lane[hop] + plan.cross[hop].lanes, LANES)
+                self.swaps.append((hop, before, low, high))
+
+    def beside(self, value, which, layer_no, chunk, halo_of):
+        plan = self.plan
+        height = value.shape[0]
+        if height not in self.masks:
+            lane = lane_numbers(height)
+            self.masks[height] = [
+                (lane >= low) & (lane < high) for _, _, low, high in self.swaps
+            ]
+        value = turned(value, -(chunk % plan.fold) * plan.own_lanes)
+        for swap, (hop, before, _, _) in enumerate(self.swaps):
+            group, offset = plan.cross[hop].place(which, layer_no, chunk)
+            by = jnp.where(
+                before,
+                (plan.cross_lane[hop] - offset) % LANES,
+                (plan.cross_lane[plan.cross_count + hop] - offset) % LANES,
+            )
+            cells = pltpu.roll(halo_of(swap, group), by, 1)
+            value = jnp.where(self.masks[height][swap], cells, value)
+        return value
+
+
+def own_kernel(plan, cells_ref, *refs):
+    halos = Halos(plan)
+    for which in range(2):
+        for layer_no in range(plan.layers):
+            for chunk in range(plan.chunks):
+
+                def halo_of(swap, group):
+                    return refs[swap][layer_no % 2 * plan.cross[swap // 2].each + group]
+
+                refs[-1][which, layer_no, chunk] = halos.beside(
+                    cells_ref[which, layer_no, chunk // plan.fold],
+                    which,
+                    layer_no,
+                    chunk,
+                    halo_of,
+                )
 
 
 def reciprocal(value):
@@ -306,12 +325,12 @@
     return [jnp.where(first_of_pair(value, spread), value, pltpu.roll(value, spread, 1))]
 
 
-def cycle_kernel(plan, cells_ref, *refs):
-    halos, hops = len(plan.cross), len(plan.along)
-    halo_refs, refs = refs[:halos], refs[halos:]
+def cycle_kernel(plan, own_ref, *refs):
+    hops, swaps = len(plan.along), 2 * plan.cross_count
     along_refs, refs = refs[:hops], refs[hops:]
-    sent = sum(each.size > 0 for each in plan.corners)
-    corner_refs, refs = refs[:sent], refs[sent:]
+    sent = 2 * sum(each[0].size > 0 for each in plan.corners[: plan.along_count])
+    corner_refs = [refs[i * sent : (i + 1) * sent] for i in range(swaps)]
+    refs = refs[swaps * sent :]
     pressure_ref, residual_ref = refs[:2]
     upright, upper0, origin = refs[2:5]
     rest = refs[5:]
@@ -335,35 +354,26 @@
             return pl.ds(low, high - low)
         return pl.ds(start0 + low, high - low)
 
+    with_halos = Halos(plan)
+    evens = [is_even("along", hop + 1) for hop in range(plan.along_count)]
     for which, target, guard in ((0, density, GUARD), (1, forcing[0], 0)):
         for c in range(count[0]):
             half = c // plan.fold
             for layer_no in range(layers):
-                parity = layer_no % 2
-                target[layer_no, c, span(guard + reach, guard + reach + own_rows)] = with_halos(
-                    plan,
-                    cells_ref[which, layer_no, half],
-                    layer_no,
-                    c,
-                    lambda k, group: halo_refs[k][
-                        (which * 2 + parity) * plan.cross[k].each + group
-                    ],
-                )
-            for side, (message, corner, row) in enumerate(
-                zip(plan.along, plan.corners, plan.along_row)
-            ):
+                target[layer_no, c, span(guard + reach, guard + reach + own_rows)] = own_ref[
+                    which, layer_no, c
+                ]
+            for side, (message, row) in enumerate(zip(plan.along, plan.along_row)):
                 after, hop = divmod(side, plan.along_count)
-                even = is_even("along", hop + 1)
 
                 def got(pair, tile):
                     two, one = pair[2 * hop], pair[2 * hop + 1]
-                    return jnp.where(even, one[tile], two[tile]) if after else jnp.where(
-                        even, two[tile], one[tile]
-                    )
-
-                for index, part in enumerate(message.parts):
-                    if part[0] != which:
-                        continue
+                    if after:
+                        return jnp.where(evens[hop], one[tile], two[tile])
+                    return jnp.where(evens[hop], two[tile], one[tile])
+
+                parts = [part for part in message.parts if part[0] == which]
+                for index, part in enumerate(parts):
                     first, run = guard + row + part[1], part[2]
                     share = 8 // run
                     for layer_no in range(0, layers, share):
@@ -371,16 +381,13 @@
                         if run == 1:
                             now = turned(now, -(c % plan.fold) * plan.own_lanes)
                         else:
-                            now = with_halos(
-                                plan,
-                                now,
-                                layer_no,
-                                c,
-                                lambda k, group: got(
-                                    corner_refs,
-                                    plan.corner_tile(corner.parts[index], k, layer_no % 2, group),
-                                ),
-                            )
+
+                            def halo_of(swap, group):
+                                corner = plan.corners[side][swap // 2].parts[index]
+                                tile = plan.corner_tile(corner, swap // 2, layer_no % 2, group)
+                                return got(corner_refs[swap], tile)
+
+                            now = with_halos.beside(now, which, layer_no, c, halo_of)
                         for i in range(share):
                             target[layer_no + i, c, span(first, first + run)] = now[
                                 i * run : (i + 1) * run
@@ -626,7 +633,6 @@
         return [shape((each.size,) + tail) for each in messages[:half] if each.size for _ in range(2)]
 
     cross_shapes = pairs_of(plan.cross, rows, LANES)
-    halo_shapes = [shape((each.size, rows, LANES)) for each in plan.cross]
     cells, *sent = kernel(
         edge_kernel,
         [jnp.stack([inv_density, source])],
@@ -636,10 +642,17 @@
     )
     halos = exchanged(sent[: len(plan.cross)], "cross")
     beside = exchanged(sent[len(plan.cross) :], "along")
-    sent = kernel(corner_kernel, halos, halo_shapes + pairs_of(plan.corners, 8, LANES))
-    halos, sent = sent[: len(halos)], sent[len(halos) :]
-    corners = exchanged(sent, "along")
-    inputs = [cells, *halos, *beside, *corners]
+    corners = []
+    for swap, halo in enumerate(halos):
+        messages = [each[swap // 2] for each in plan.corners]
+        sent = kernel(
+            functools.partial(corner_kernel, swap // 2), [halo], pairs_of(messages, 8, LANES)
+        )
+        corners += exchanged(sent, "along")
+    (own,) = kernel(
+        own_kernel, [cells, *halos], [shape((2, layers, plan.chunks, rows, LANES))]
+    )
+    inputs = [own, *beside, *corners]
 
     def room(*shape):
         return pltpu.VMEM(shape + (LANES,), jnp.float32)

time: 39.2 us -> 36.8 us (0.939)
  waiting for transfers between devices: 8.53 us -> 4.92 us
  starting transfers between devices: 13.1 us -> 14.4 us
    ppermute x6 -> x8, waiting for transfers between devices: 8.53 us -> 4.92 us  [swapped(): return lax.ppermute(array, axis, pairs)]
    ppermute x6 -> x8, starting transfers between devices: 13.1 us -> 14.4 us  [swapped(): return lax.ppermute(array, axis, pairs)]
    pallas_call x2 -> x4, Pallas kernels: 0.8 us -> 1.49 us  [kernel(): pl.pallas_call(functools.partial(body, plan), out_shape=outputs, in_specs...]
    pallas_call x1, Pallas kernels: 14.6 us -> 14 us  [per_device(): pl.pallas_call(functools.partial(cycle_kernel, plan), out_shape=[jax.Shap...]
  transfers between devices with their start and end apart: 6 -> 8, of which waited for: 2 -> 2; matrix products, arithmetic and copies ran while one was open for 0% -> 0% of each run, Pallas kernels for 0% -> 2%
where the time goes in v6:
time: 36.8 us; the launch traced here: 36.6 us
  Pallas kernels  15.5 us (42%)
  starting transfers between devices  14.4 us (39%)
  waiting for transfers between devices  4.92 us (13%)
  other arithmetic  1.06 us (3%)
  between operations  0.74 us (2%)
    ppermute x8, starting transfers between devices, swapped(): return lax.ppermute(array, axis, pairs)  14.4 us
    pallas_call x1, Pallas kernels, per_device(): pl.pallas_call(functools.partial(cycle_kernel, plan), out_shape=[jax.Shap...  14 us
    ppermute x8, waiting for transfers between devices, swapped(): return lax.ppermute(array, axis, pairs)  4.92 us
    pallas_call x4, Pallas kernels, kernel(): pl.pallas_call(functools.partial(body, plan), out_shape=outputs, in_specs...  1.49 us
    another operation x1, other arithmetic, per_device(): jnp.stack([inv_density, source])  1.06 us
  transfers between devices with their start and end apart: 8, of which 2 were waited for; matrix products, arithmetic and copies ran while one was open for 0% of the time, Pallas kernels for 2%

profile of v6, /device:TPU:1, one launch (start us, length us, event | category | flops | bytes accessed | tf_op | source)
XLA Modules:
  0.0 36.6 jit_solution(11455739699741596302)
XLA Ops:
  0.6 1.1 %pad_maximum_fusion.both_ref = f32[2,16,16,256]{3,2,1,0:T(8,128)S(1)} fusion(f32[1,16,16,256]{3,2,1,0:T(8,128)} %bitcast.2, f32[1,16,16,256]{3,2,1,0:T(8,128)} %bitcast.3), kind=kLoop, calls=%fused_computation | loop fusion | flops 131072 | bytes 1048576 | tf_op jit(solution)/shard_map/stack | solution.py:638
  1.7 0.7 %shard_map.41 = (f32[2,16,2,16,128]{4,3,2,1,0:T(8,128)S(1)}, f32[22,16,128]{2,1,0:T(8,128)S(1)}, f32[22,16,128]{2,1,0:T(8,128)S(1)}, f32[100,8,128]{2,1,0:T(8,128)S(1)}, f32[100,8,128]{2,1,0:T(8,128)S(1)}) custom-call(f32[2,16,16,256]{3,2,1,0:T(8,128)S(1)} %pad_maximum_fusion.both_ref), custom_call_target="tpu_custom_call" | custom-call | tf_op jit(solution)/shard_map/pallas_call | solution.py:618
  2.4 0.7 %collective-permute-start = (f32[22,16,128]{2,1,0:T(8,128)S(1)}, f32[22,16,128]{2,1,0:T(8,128)S(1)}, u32[]{:S(2)}, u32[]{:S(2)}) collective-permute-start(f32[22,16,128]{2,1,0:T(8,128)S(1)} %get-tuple-element.12), channel_id=1, source_target_pairs={{4,8},{8,4},{12,16},{16,12},{20,24},{24,20},{5,9},{9,5},{13,17},{1... | collective-permute-start | bytes 540680 | tf_op jit(solution)/shard_map/ppermute | solution.py:33
  3.1 4.5 %collective-permute-start.2 = (f32[100,8,128]{2,1,0:T(8,128)S(1)}, f32[100,8,128]{2,1,0:T(8,128)S(1)}, u32[]{:S(2)}, u32[]{:S(2)}) collective-permute-start(f32[100,8,128]{2,1,0:T(8,128)S(1)} %get-tuple-element.14), channel_id=1, source_target_pairs={{1,2},{2,1},{5,6},{6,5},{9,10},{10,9},{13,14},{14,13},{17,18},{18,... | collective-permute-start | bytes 1228808 | tf_op jit(solution)/shard_map/ppermute | solution.py:33
  7.6 0.1 collective-permute-start.3
  7.6 4.1 %collective-permute-start.1 = (f32[22,16,128]{2,1,0:T(8,128)S(1)}, f32[22,16,128]{2,1,0:T(8,128)S(1)}, u32[]{:S(2)}, u32[]{:S(2)}) collective-permute-start(f32[22,16,128]{2,1,0:T(8,128)S(1)} %get-tuple-element.13), channel_id=1, source_target_pairs={{0,4},{4,0},{8,12},{12,8},{16,20},{20,16},{24,28},{28,24},{1,5},{5... | collective-permute-start | bytes 540680 | tf_op jit(solution)/shard_map/ppermute | solution.py:33
  11.7 0.0 collective-permute-done.refs_0_.halo_ref
  11.8 2.2 %collective-permute-start.4 = (f32[33,8,128]{2,1,0:T(8,128)S(1)}, f32[33,8,128]{2,1,0:T(8,128)S(1)}, u32[]{:S(2)}, u32[]{:S(2)}) collective-permute-start(f32[33,8,128]{2,1,0:T(8,128)S(1)} %get-tuple-element.16), channel_id=1, source_target_pairs={{1,2},{2,1},{5,6},{6,5},{9,10},{10,9},{13,14},{14,13},{17,18},{18,... | collective-permute-start | bytes 405512 | tf_op jit(solution)/shard_map/ppermute | solution.py:33
  14.0 0.1 collective-permute-start.5
  14.0 2.2 %collective-permute-done.1.refs_1_.halo_ref = f32[22,16,128]{2,1,0:T(8,128)S(1)} collective-permute-done((f32[22,16,128]{2,1,0:T(8,128)S(1)}, f32[22,16,128]{2,1,0:T(8,128)S(1)}, u32[]{:S(2)}, u32[]{:S(2)}) %collective-permute-start.1) | collective-permute-done | bytes 180256 | tf_op jit(solution)/shard_map/ppermute | solution.py:33
  16.3 2.8 %collective-permute-start.6 = (f32[33,8,128]{2,1,0:T(8,128)S(1)}, f32[33,8,128]{2,1,0:T(8,128)S(1)}, u32[]{:S(2)}, u32[]{:S(2)}) collective-permute-start(f32[33,8,128]{2,1,0:T(8,128)S(1)} %get-tuple-element.18), channel_id=1, source_target_pairs={{1,2},{2,1},{5,6},{6,5},{9,10},{10,9},{13,14},{14,13},{17,18},{18,... | collective-permute-start | bytes 405512 | tf_op jit(solution)/shard_map/ppermute | solution.py:33
  19.1 0.0 collective-permute-done.4.refs_2_
  19.1 0.1 collective-permute-start.7
  19.2 0.8 %shard_map.42.own_ref = f32[2,16,4,16,128]{4,3,2,1,0:T(8,128)S(1)} custom-call(f32[2,16,2,16,128]{4,3,2,1,0:T(8,128)S(1)} %get-tuple-element.11.cells_ref, f32[22,16,128]{2,1,0:T(8,128)S(1)} %collective-permute-done.refs_0_.halo_ref, f32[22,16,128]{2,1,0:T(8,128)S(1)} %collective-permute-done.1.refs_1_.halo_ref), custom_call_target="tpu_custom_call" | custom-call | tf_op jit(solution)/shard_map/pallas_call | solution.py:618
  19.9 0.0 collective-permute-done.5.refs_3_
  20.0 2.7 %collective-permute-done.6.refs_4_ = f32[33,8,128]{2,1,0:T(8,128)S(1)} collective-permute-done((f32[33,8,128]{2,1,0:T(8,128)S(1)}, f32[33,8,128]{2,1,0:T(8,128)S(1)}, u32[]{:S(2)}, u32[]{:S(2)}) %collective-permute-start.6) | collective-permute-done | bytes 135200 | tf_op jit(solution)/shard_map/ppermute | solution.py:33
  22.6 0.0 collective-permute-done.7.refs_5_
  22.6 0.0 collective-permute-done.2.refs_0_
  22.6 0.0 collective-permute-done.3.refs_1_
  22.7 14.0 %shard_map.45 = (f32[16,16,256]{2,1,0:T(8,128)}, f32[16,16,256]{2,1,0:T(8,128)}) custom-call(f32[2,16,4,16,128]{4,3,2,1,0:T(8,128)S(1)} %shard_map.42.own_ref, f32[100,8,128]{2,1,0:T(8,128)S(1)} %collective-permute-done.2.refs_0_, f32[100,8,128]{2,1,0:T(8,128)S(1)} %collective-permute-done.3.refs_1_, f32[33,8,128]{2,1,0:T(8,128)S(1)} %collective-permute-done.4.refs_2_, ...), custom_call_target="tpu_custom_call" | custom-call | tf_op jit(solution)/shard_map/pallas_call | solution.py:676
  (2 shorter events, 0.1 us)
Async XLA Ops:
  2.4 9.3 %collective-permute-start = (f32[22,16,128]{2,1,0:T(8,128)S(1)}, f32[22,16,128]{2,1,0:T(8,128)S(1)}, u32[]{:S(2)}, u32[]{:S(2)}) collective-permute-start(f32[22,16,128]{2,1,0:T(8,128)S(1)} %get-tuple-element.12), channel_id=1, source_target_pairs={{4,8},{8,4},{12,16},{16,12},{20,24},{24,20},{5,9},{9,5},{13,17},{1... | collective-permute-start | bytes 540680 | tf_op jit(solution)/shard_map/ppermute | solution.py:33
  3.1 19.6 %collective-permute-start.2 = (f32[100,8,128]{2,1,0:T(8,128)S(1)}, f32[100,8,128]{2,1,0:T(8,128)S(1)}, u32[]{:S(2)}, u32[]{:S(2)}) collective-permute-start(f32[100,8,128]{2,1,0:T(8,128)S(1)} %get-tuple-element.14), channel_id=1, source_target_pairs={{1,2},{2,1},{5,6},{6,5},{9,10},{10,9},{13,14},{14,13},{17,18},{18,... | collective-permute-start | bytes 1228808 | tf_op jit(solution)/shard_map/ppermute | solution.py:33
  7.6 15.1 %collective-permute-start.3 = (f32[100,8,128]{2,1,0:T(8,128)S(1)}, f32[100,8,128]{2,1,0:T(8,128)S(1)}, u32[]{:S(2)}, u32[]{:S(2)}) collective-permute-start(f32[100,8,128]{2,1,0:T(8,128)S(1)} %get-tuple-element.15), channel_id=1, source_target_pairs={{0,1},{1,0},{2,3},{3,2},{4,5},{5,4},{6,7},{7,6},{8,9},{9,8},{10,11... | collective-permute-start | bytes 1228808 | tf_op jit(solution)/shard_map/ppermute | solution.py:33
  7.6 8.6 %collective-permute-start.1 = (f32[22,16,128]{2,1,0:T(8,128)S(1)}, f32[22,16,128]{2,1,0:T(8,128)S(1)}, u32[]{:S(2)}, u32[]{:S(2)}) collective-permute-start(f32[22,16,128]{2,1,0:T(8,128)S(1)} %get-tuple-element.13), channel_id=1, source_target_pairs={{0,4},{4,0},{8,12},{12,8},{16,20},{20,16},{24,28},{28,24},{1,5},{5... | collective-permute-start | bytes 540680 | tf_op jit(solution)/shard_map/ppermute | solution.py:33
  11.8 7.4 %collective-permute-start.4 = (f32[33,8,128]{2,1,0:T(8,128)S(1)}, f32[33,8,128]{2,1,0:T(8,128)S(1)}, u32[]{:S(2)}, u32[]{:S(2)}) collective-permute-start(f32[33,8,128]{2,1,0:T(8,128)S(1)} %get-tuple-element.16), channel_id=1, source_target_pairs={{1,2},{2,1},{5,6},{6,5},{9,10},{10,9},{13,14},{14,13},{17,18},{18,... | collective-permute-start | bytes 405512 | tf_op jit(solution)/shard_map/ppermute | solution.py:33
  14.0 6.0 %collective-permute-start.5 = (f32[33,8,128]{2,1,0:T(8,128)S(1)}, f32[33,8,128]{2,1,0:T(8,128)S(1)}, u32[]{:S(2)}, u32[]{:S(2)}) collective-permute-start(f32[33,8,128]{2,1,0:T(8,128)S(1)} %get-tuple-element.17), channel_id=1, source_target_pairs={{0,1},{1,0},{2,3},{3,2},{4,5},{5,4},{6,7},{7,6},{8,9},{9,8},{10,11... | collective-permute-start | bytes 405512 | tf_op jit(solution)/shard_map/ppermute | solution.py:33
  16.3 6.3 %collective-permute-start.6 = (f32[33,8,128]{2,1,0:T(8,128)S(1)}, f32[33,8,128]{2,1,0:T(8,128)S(1)}, u32[]{:S(2)}, u32[]{:S(2)}) collective-permute-start(f32[33,8,128]{2,1,0:T(8,128)S(1)} %get-tuple-element.18), channel_id=1, source_target_pairs={{1,2},{2,1},{5,6},{6,5},{9,10},{10,9},{13,14},{14,13},{17,18},{18,... | collective-permute-start | bytes 405512 | tf_op jit(solution)/shard_map/ppermute | solution.py:33
  19.1 3.5 %collective-permute-start.7 = (f32[33,8,128]{2,1,0:T(8,128)S(1)}, f32[33,8,128]{2,1,0:T(8,128)S(1)}, u32[]{:S(2)}, u32[]{:S(2)}) collective-permute-start(f32[33,8,128]{2,1,0:T(8,128)S(1)} %get-tuple-element.19), channel_id=1, source_target_pairs={{0,1},{1,0},{2,3},{3,2},{4,5},{5,4},{6,7},{7,6},{8,9},{9,8},{10,11... | collective-permute-start | bytes 405512 | tf_op jit(solution)/shard_map/ppermute | solution.py:33

commit v7 on v6

--- a/solution.py
+++ b/solution.py
@@ -140,6 +140,14 @@
         share = 8 // part[2]
         return part[3] + layer_no // share * self.halves + half
 
+    def side_tile(self, side, index, layer_no, chunk):
+        parts = self.along[side].parts
+        base = sum(self.layers * part[2] // 8 for part in parts[:index])
+        return (base + layer_no * parts[index][2] // 8) * self.chunks + chunk
+
+    def side_size(self, side):
+        return sum(self.layers * part[2] // 8 for part in self.along[side].parts) * self.chunks
+
     def corner_tile(self, part, cross_hop, parity, group):
         return part[3] + (parity * self.cross[cross_hop].each if part[2] == 8 else 0) + group
 
@@ -152,11 +160,11 @@
     return jnp.take_along_axis(value, pick, axis=1, mode="promise_in_bounds")
 
 
-def edge_kernel(plan, both_ref, cells_ref, *out_refs):
+def edge_kernel(plan, both_ref, *cross_refs):
     lane = lane_numbers(plan.own_rows)
-    chunks, layers, cols = plan.chunks, plan.layers, plan.own_cols
-    tiles = range(0, cols, LANES)
-    cross_refs, along_refs = out_refs[: len(plan.cross)], out_refs[len(plan.cross) :]
+    chunks = plan.chunks
+    tiles = range(0, plan.own_cols, LANES)
+
     def packed(message, group, parity):
         lanes, share = message.lanes, message.share
         slot = lane // lanes
@@ -189,6 +197,12 @@
                 cross_refs[2 * hop + 1][row], cross_refs[2 * hop][row] = chosen(
                     even, packed(tail, group, parity), packed(head, group, parity)
                 )
+
+
+def cells_kernel(plan, both_ref, cells_ref, *along_refs):
+    lane = lane_numbers(plan.own_rows)
+    chunks, layers = plan.chunks, plan.layers
+    tiles = range(0, plan.own_cols, LANES)
     hops = plan.along_count
     evens = [is_even("along", hop + 1) for hop in range(hops)]
     place = (lane - plan.own_lane) & (LANES - 1)
@@ -258,7 +272,7 @@
                 high = jnp.where(before, plan.cross_lane[hop] + plan.cross[hop].lanes, LANES)
                 self.swaps.append((hop, before, low, high))
 
-    def beside(self, value, which, layer_no, chunk, halo_of):
+    def beside(self, value, which, layer_no, chunk, halo_of, swaps):
         plan = self.plan
         height = value.shape[0]
         if height not in self.masks:
@@ -266,8 +280,8 @@
             self.masks[height] = [
                 (lane >= low) & (lane < high) for _, _, low, high in self.swaps
             ]
-        value = turned(value, -(chunk % plan.fold) * plan.own_lanes)
-        for swap, (hop, before, _, _) in enumerate(self.swaps):
+        for swap in swaps:
+            hop, before, _, _ = self.swaps[swap]
             group, offset = plan.cross[hop].place(which, layer_no, chunk)
             by = jnp.where(
                 before,
@@ -279,22 +293,56 @@
         return value
 
 
-def own_kernel(plan, cells_ref, *refs):
-    halos = Halos(plan)
+def from_swaps(plan, hop, after, pair, tile):
+    even = is_even("along", hop + 1)
+    two, one = pair[2 * hop], pair[2 * hop + 1]
+    return jnp.where(even, one[tile], two[tile]) if after else jnp.where(even, two[tile], one[tile])
+
+
+def corner_of(plan, side, index, layer_no, corner_refs):
+    after, hop = divmod(side, plan.along_count)
+    index = [part for part in plan.along[side].parts if part[2] > 1].index(
+        plan.along[side].parts[index]
+    )
+
+    def halo_of(swap, group):
+        parts = plan.corners[side][swap // 2].parts
+        tile = plan.corner_tile(parts[index % len(parts)], swap // 2, layer_no % 2, group)
+        return from_swaps(plan, hop, after, corner_refs[swap], tile)
+
+    return halo_of
+
+
+def window_kernel(plan, cells_ref, *refs):
+    halos, swaps, hops = Halos(plan), 2 * plan.cross_count, len(plan.along)
+    halo_refs, along_refs = refs[:swaps], refs[swaps : swaps + hops]
+    corner_refs = refs[swaps + hops : -1 - hops]
+    own_ref, side_refs = refs[-1 - hops], refs[-hops:]
+    turns = [-(chunk % plan.fold) * plan.own_lanes for chunk in range(plan.chunks)]
     for which in range(2):
         for layer_no in range(plan.layers):
             for chunk in range(plan.chunks):
 
                 def halo_of(swap, group):
-                    return refs[swap][layer_no % 2 * plan.cross[swap // 2].each + group]
-
-                refs[-1][which, layer_no, chunk] = halos.beside(
-                    cells_ref[which, layer_no, chunk // plan.fold],
-                    which,
-                    layer_no,
-                    chunk,
-                    halo_of,
+                    return halo_refs[swap][layer_no % 2 * plan.cross[swap // 2].each + group]
+
+                value = turned(cells_ref[which, layer_no, chunk // plan.fold], turns[chunk])
+                own_ref[which, layer_no, chunk] = halos.beside(
+                    value, which, layer_no, chunk, halo_of, range(swaps)
                 )
+    for side, message in enumerate(plan.along):
+        after, hop = divmod(side, plan.along_count)
+        for index, part in enumerate(message.parts):
+            which, _, run, _ = part
+            for layer_no in range(0, plan.layers, 8 // run):
+                for chunk in range(plan.chunks):
+                    tile = plan.own_tile(part, layer_no, chunk // plan.fold)
+                    value = from_swaps(plan, hop, after, along_refs, tile)
+                    value = turned(value, turns[chunk])
+                    if run > 1:
+                        halo_of = corner_of(plan, side, index, layer_no, [corner_refs])
+                        value = halos.beside(value, which, layer_no, chunk, halo_of, range(1))
+                    side_refs[side][plan.side_tile(side, index, layer_no, chunk)] = value
 
 
 def reciprocal(value):
@@ -327,13 +375,13 @@
 
 def cycle_kernel(plan, own_ref, *refs):
     hops, swaps = len(plan.along), 2 * plan.cross_count
-    along_refs, refs = refs[:hops], refs[hops:]
+    side_refs, refs = refs[:hops], refs[hops:]
     sent = 2 * sum(each[0].size > 0 for each in plan.corners[: plan.along_count])
-    corner_refs = [refs[i * sent : (i + 1) * sent] for i in range(swaps)]
-    refs = refs[swaps * sent :]
-    pressure_ref, residual_ref = refs[:2]
-    upright, upper0, origin = refs[2:5]
-    rest = refs[5:]
+    corner_refs = [None] + [refs[i * sent : (i + 1) * sent] for i in range(swaps - 1)]
+    refs = refs[(swaps - 1) * sent :]
+    out_refs, staged = refs[:2], refs[2:4]
+    upright, upper0, origin, semaphore = refs[4:8]
+    rest = refs[8:]
     levels = plan.coarsest + 1
     coarsest = plan.coarsest
     layers, rows = plan.layers, plan.rows
@@ -354,44 +402,30 @@
             return pl.ds(low, high - low)
         return pl.ds(start0 + low, high - low)
 
-    with_halos = Halos(plan)
-    evens = [is_even("along", hop + 1) for hop in range(plan.along_count)]
-    for which, target, guard in ((0, density, GUARD), (1, forcing[0], 0)):
-        for c in range(count[0]):
-            half = c // plan.fold
-            for layer_no in range(layers):
+    halos = Halos(plan)
+    targets = ((density, GUARD), (forcing[0], 0))
+    for which, (target, guard) in enumerate(targets):
+        for layer_no in range(layers):
+            for c in range(count[0]):
                 target[layer_no, c, span(guard + reach, guard + reach + own_rows)] = own_ref[
                     which, layer_no, c
                 ]
-            for side, (message, row) in enumerate(zip(plan.along, plan.along_row)):
-                after, hop = divmod(side, plan.along_count)
-
-                def got(pair, tile):
-                    two, one = pair[2 * hop], pair[2 * hop + 1]
-                    if after:
-                        return jnp.where(evens[hop], one[tile], two[tile])
-                    return jnp.where(evens[hop], two[tile], one[tile])
-
-                parts = [part for part in message.parts if part[0] == which]
-                for index, part in enumerate(parts):
-                    first, run = guard + row + part[1], part[2]
-                    share = 8 // run
-                    for layer_no in range(0, layers, share):
-                        now = got(along_refs, plan.own_tile(part, layer_no, half))
-                        if run == 1:
-                            now = turned(now, -(c % plan.fold) * plan.own_lanes)
-                        else:
-
-                            def halo_of(swap, group):
-                                corner = plan.corners[side][swap // 2].parts[index]
-                                tile = plan.corner_tile(corner, swap // 2, layer_no % 2, group)
-                                return got(corner_refs[swap], tile)
-
-                            now = with_halos.beside(now, which, layer_no, c, halo_of)
-                        for i in range(share):
-                            target[layer_no + i, c, span(first, first + run)] = now[
-                                i * run : (i + 1) * run
-                            ]
+    for side, message in enumerate(plan.along):
+        for index, part in enumerate(message.parts):
+            which, start, run, _ = part
+            target, guard = targets[which]
+            first = guard + plan.along_row[side] + start
+            share = 8 // run
+            for layer_no in range(0, layers, share):
+                for c in range(count[0]):
+                    now = side_refs[side][plan.side_tile(side, index, layer_no, c)]
+                    if run > 1:
+                        halo_of = corner_of(plan, side, index, layer_no, corner_refs)
+                        now = halos.beside(now, which, layer_no, c, halo_of, range(1, swaps))
+                    for i in range(share):
+                        target[layer_no + i, c, span(first, first + run)] = now[
+                            i * run : (i + 1) * run
+                        ]
 
     def faces(layer_no, first):
         cells = [density[layer_no, c, GUARD : GUARD + rows] for c in range(count[0])]
@@ -434,15 +468,6 @@
         for c in range(count[m]):
             upper[m][layers, c] = jnp.zeros((rows, LANES), jnp.float32)
 
-    def clear_guards(layer_no):
-        zeros = jnp.zeros((GUARD, LANES), jnp.float32)
-        for m in range(levels):
-            for c in range(count[m]):
-                value[m][layer_no, c, 0:GUARD] = zeros
-                value[m][layer_no, c, GUARD + rows : 2 * GUARD + rows] = zeros
-
-    pl.loop(0, layers, unroll=4)(clear_guards)
-
     def pivots(some, layer_no, before, first):
         after = []
         for m in some:
@@ -564,13 +589,15 @@
     chunks = count[0]
     lane = lane_numbers(own_rows)
 
+    lanes = LANES // chunks
+    back = (lane & (chunks - 1)) * lanes + lane // chunks
+
     def in_order(cells, tile_no):
         start = (plan.side_cols + tile_no * LANES) // chunks
-        pick = start + lane // chunks
-        out = taken(cells[0], pick)
+        out = turned(cells[0], -start)
         for c in range(1, chunks):
-            out = jnp.where((lane & (chunks - 1)) == c, taken(cells[c], pick), out)
-        return out
+            out = jnp.where(lane >= c * lanes, turned(cells[c], c * lanes - start), out)
+        return taken(out, back)
 
     def finish(layer_no, top, bottom):
         low, high = reach, reach + own_rows
@@ -598,12 +625,22 @@
             remains.append(remain)
         for tile_no in range(plan.own_cols // LANES):
             columns = slice(tile_no * LANES, (tile_no + 1) * LANES)
-            pressure_ref[layer_no, :, columns] = in_order(cells, tile_no)
-            residual_ref[layer_no, :, columns] = in_order(remains, tile_no)
-
-    finish(0, True, False)
-    pl.loop(1, layers - 1, unroll=2)(lambda layer_no: finish(layer_no, False, False))
-    finish(layers - 1, False, True)
+            staged[0][layer_no, :, columns] = in_order(cells, tile_no)
+            staged[1][layer_no, :, columns] = in_order(remains, tile_no)
+
+    copies = []
+    for layer_no in range(layers):
+        finish(layer_no, layer_no == 0, layer_no == layers - 1)
+        if layer_no % 4 == 3:
+            block = pl.ds(layer_no - 3, 4)
+            for i in range(2):
+                copy = pltpu.make_async_copy(
+                    staged[i].at[block], out_refs[i].at[block], semaphore.at[i, layer_no // 4]
+                )
+                copy.start()
+                copies.append(copy)
+    for copy in copies:
+        copy.wait()
 
 
 def per_device(source, inv_density):
@@ -620,7 +657,7 @@
             out_shape=outputs,
             in_specs=[vmem] * len(inputs),
             out_specs=[vmem] * len(outputs),
-            compiler_params=pltpu.CompilerParams(vmem_limit_bytes=16 << 20),
+            compiler_params=pltpu.CompilerParams(vmem_limit_bytes=24 << 20),
         )(*inputs)
 
     def exchanged(sent, axis):
@@ -633,36 +670,40 @@
         return [shape((each.size,) + tail) for each in messages[:half] if each.size for _ in range(2)]
 
     cross_shapes = pairs_of(plan.cross, rows, LANES)
+    both = jnp.stack([inv_density, source])
+    halos = exchanged(kernel(edge_kernel, [both], cross_shapes), "cross")
     cells, *sent = kernel(
-        edge_kernel,
-        [jnp.stack([inv_density, source])],
-        [shape((2, layers, plan.halves, rows, LANES))]
-        + cross_shapes
-        + pairs_of(plan.along, 8, LANES),
+        cells_kernel,
+        [both],
+        [shape((2, layers, plan.halves, rows, LANES))] + pairs_of(plan.along, 8, LANES),
     )
-    halos = exchanged(sent[: len(plan.cross)], "cross")
-    beside = exchanged(sent[len(plan.cross) :], "along")
+    beside = exchanged(sent, "along")
     corners = []
     for swap, halo in enumerate(halos):
         messages = [each[swap // 2] for each in plan.corners]
         sent = kernel(
             functools.partial(corner_kernel, swap // 2), [halo], pairs_of(messages, 8, LANES)
         )
-        corners += exchanged(sent, "along")
-    (own,) = kernel(
-        own_kernel, [cells, *halos], [shape((2, layers, plan.chunks, rows, LANES))]
+        corners.append(exchanged(sent, "along"))
+    window = kernel(
+        window_kernel,
+        [cells, *halos, *beside, *corners[0]],
+        [shape((2, layers, plan.chunks, rows, LANES))]
+        + [shape((plan.side_size(side), 8, LANES)) for side in range(len(plan.along))],
     )
-    inputs = [own, *beside, *corners]
+    inputs = [*window, *sum(corners[1:], [])]
 
     def room(*shape):
         return pltpu.VMEM(shape + (LANES,), jnp.float32)
 
     total, high = plan.rows, plan.rows + GUARD
     counts = [plan.level_chunks(m) for m in range(levels)]
-    scratch = [
+    scratch = [pltpu.VMEM((layers, rows, cols), jnp.float32)] * 2
+    scratch += [
         room(layers, counts[-1], total),
         room(layers + 1, counts[0], total),
         pltpu.SMEM((1,), jnp.int32),
+        pltpu.SemaphoreType.DMA((2, layers // 4)),
     ]
     scratch += [room(layers, n, high) for n in counts]
     scratch += [room(layers, n + 1, total) for n in counts]
@@ -672,12 +713,12 @@
     scratch += [room(layers, counts[0], total)]
     scratch += [room(layers + 1, n, total) for n in counts[1:]]
     held = sum(math.prod(each.shape) for each in scratch) + sum(each.size for each in inputs)
-    held = 4 * (held + 2 * source.size)
+    held = 4 * held
     return pl.pallas_call(
         functools.partial(cycle_kernel, plan),
         out_shape=[jax.ShapeDtypeStruct((layers, rows, cols), jnp.float32)] * 2,
         in_specs=[vmem] * len(inputs),
-        out_specs=[vmem] * 2,
+        out_specs=[pl.BlockSpec(memory_space=pl.ANY)] * 2,
         scratch_shapes=scratch,
         compiler_params=pltpu.CompilerParams(vmem_limit_bytes=held + (3 << 20)),
     )(*inputs)

time: 36.8 us -> 37.5 us (1.019)
  Pallas kernels: 15.5 us -> 16.8 us
  waiting for transfers between devices: 4.92 us -> 4.27 us
    pallas_call x4 -> x5, Pallas kernels: 1.49 us -> 2.17 us  [kernel(): pl.pallas_call(functools.partial(body, plan), out_shape=outputs, in_specs...]
    ppermute x8, waiting for transfers between devices: 4.92 us -> 4.27 us  [swapped(): return lax.ppermute(array, axis, pairs)]
    pallas_call x1, Pallas kernels: 14 us -> 14.6 us  [per_device(): pl.pallas_call(functools.partial(cycle_kernel, plan), out_shape=[jax.Shap...]
  transfers between devices with their start and end apart: 8 -> 8, of which waited for: 2 -> 2; matrix products, arithmetic and copies ran while one was open for 0% -> 0% of each run, Pallas kernels for 2% -> 5%
where the time goes in v7:
time: 37.5 us; the launch traced here: 37.3 us
  Pallas kernels  16.8 us (45%)
  starting transfers between devices  14.4 us (38%)
  waiting for transfers between devices  4.27 us (11%)
  other arithmetic  1.06 us (3%)
  between operations  0.75 us (2%)
    pallas_call x1, Pallas kernels, per_device(): pl.pallas_call(functools.partial(cycle_kernel, plan), out_shape=[jax.Shap...  14.6 us
    ppermute x8, starting transfers between devices, swapped(): return lax.ppermute(array, axis, pairs)  14.4 us
    ppermute x8, waiting for transfers between devices, swapped(): return lax.ppermute(array, axis, pairs)  4.27 us
    pallas_call x5, Pallas kernels, kernel(): pl.pallas_call(functools.partial(body, plan), out_shape=outputs, in_specs...  2.17 us
    another operation x1, other arithmetic, per_device(): both = jnp.stack([inv_density, source])  1.06 us
  transfers between devices with their start and end apart: 8, of which 2 were waited for; matrix products, arithmetic and copies ran while one was open for 0% of the time, Pallas kernels for 5%

profile of v7, /device:TPU:1, one launch (start us, length us, event | category | flops | bytes accessed | tf_op | source)
XLA Modules:
  0.0 37.3 jit_solution(6050506031868413485)
XLA Ops:
  0.6 1.1 %pad_maximum_fusion.both_ref = f32[2,16,16,256]{3,2,1,0:T(8,128)S(1)} fusion(f32[1,16,16,256]{3,2,1,0:T(8,128)} %bitcast.2, f32[1,16,16,256]{3,2,1,0:T(8,128)} %bitcast.3), kind=kLoop, calls=%fused_computation | loop fusion | flops 131072 | bytes 1048576 | tf_op jit(solution)/shard_map/stack | solution.py:673
  1.7 0.4 %shard_map.42 = (f32[22,16,128]{2,1,0:T(8,128)S(1)}, f32[22,16,128]{2,1,0:T(8,128)S(1)}) custom-call(f32[2,16,16,256]{3,2,1,0:T(8,128)S(1)} %pad_maximum_fusion.both_ref), custom_call_target="tpu_custom_call" | custom-call | tf_op jit(solution)/shard_map/pallas_call | solution.py:655
  2.1 0.7 %collective-permute-start = (f32[22,16,128]{2,1,0:T(8,128)S(1)}, f32[22,16,128]{2,1,0:T(8,128)S(1)}, u32[]{:S(2)}, u32[]{:S(2)}) collective-permute-start(f32[22,16,128]{2,1,0:T(8,128)S(1)} %get-tuple-element.15), channel_id=1, source_target_pairs={{4,8},{8,4},{12,16},{16,12},{20,24},{24,20},{5,9},{9,5},{13,17},{1... | collective-permute-start | bytes 540680 | tf_op jit(solution)/shard_map/ppermute | solution.py:33
  2.8 0.3 shard_map.41
  3.1 4.5 %collective-permute-start.2 = (f32[100,8,128]{2,1,0:T(8,128)S(1)}, f32[100,8,128]{2,1,0:T(8,128)S(1)}, u32[]{:S(2)}, u32[]{:S(2)}) collective-permute-start(f32[100,8,128]{2,1,0:T(8,128)S(1)} %get-tuple-element.17), channel_id=1, source_target_pairs={{1,2},{2,1},{5,6},{6,5},{9,10},{10,9},{13,14},{14,13},{17,18},{18,... | collective-permute-start | bytes 1228808 | tf_op jit(solution)/shard_map/ppermute | solution.py:33
  7.6 0.1 collective-permute-start.3
  7.7 4.1 %collective-permute-start.1 = (f32[22,16,128]{2,1,0:T(8,128)S(1)}, f32[22,16,128]{2,1,0:T(8,128)S(1)}, u32[]{:S(2)}, u32[]{:S(2)}) collective-permute-start(f32[22,16,128]{2,1,0:T(8,128)S(1)} %get-tuple-element.16), channel_id=1, source_target_pairs={{0,4},{4,0},{8,12},{12,8},{16,20},{20,16},{24,28},{28,24},{1,5},{5... | collective-permute-start | bytes 540680 | tf_op jit(solution)/shard_map/ppermute | solution.py:33
  11.8 0.0 collective-permute-done.halo_ref.refs_0_
  11.8 2.2 %collective-permute-start.4 = (f32[33,8,128]{2,1,0:T(8,128)S(1)}, f32[33,8,128]{2,1,0:T(8,128)S(1)}, u32[]{:S(2)}, u32[]{:S(2)}) collective-permute-start(f32[33,8,128]{2,1,0:T(8,128)S(1)} %get-tuple-element.19), channel_id=1, source_target_pairs={{1,2},{2,1},{5,6},{6,5},{9,10},{10,9},{13,14},{14,13},{17,18},{18,... | collective-permute-start | bytes 405512 | tf_op jit(solution)/shard_map/ppermute | solution.py:33
  14.0 0.1 collective-permute-start.5
  14.1 2.2 %collective-permute-done.1.refs_1_.halo_ref = f32[22,16,128]{2,1,0:T(8,128)S(1)} collective-permute-done((f32[22,16,128]{2,1,0:T(8,128)S(1)}, f32[22,16,128]{2,1,0:T(8,128)S(1)}, u32[]{:S(2)}, u32[]{:S(2)}) %collective-permute-start.1) | collective-permute-done | bytes 180256 | tf_op jit(solution)/shard_map/ppermute | solution.py:33
  16.4 2.8 %collective-permute-start.6 = (f32[33,8,128]{2,1,0:T(8,128)S(1)}, f32[33,8,128]{2,1,0:T(8,128)S(1)}, u32[]{:S(2)}, u32[]{:S(2)}) collective-permute-start(f32[33,8,128]{2,1,0:T(8,128)S(1)} %get-tuple-element.24), channel_id=1, source_target_pairs={{1,2},{2,1},{5,6},{6,5},{9,10},{10,9},{13,14},{14,13},{17,18},{18,... | collective-permute-start | bytes 405512 | tf_op jit(solution)/shard_map/ppermute | solution.py:33
  19.2 0.0 collective-permute-done.4.refs_4_
  19.2 0.1 collective-permute-start.7
  19.3 0.0 collective-permute-done.5.refs_5_
  19.3 0.0 collective-permute-done.2.refs_2_
  19.3 0.0 collective-permute-done.3.refs_3_
  19.3 1.4 %shard_map.44 = (f32[2,16,4,16,128]{4,3,2,1,0:T(8,128)S(1)}, f32[200,8,128]{2,1,0:T(8,128)S(1)}, f32[200,8,128]{2,1,0:T(8,128)S(1)}) custom-call(f32[2,16,2,16,128]{4,3,2,1,0:T(8,128)S(1)} %get-tuple-element.14.cells_ref, f32[22,16,128]{2,1,0:T(8,128)S(1)} %collective-permute-done.halo_ref.refs_0_, ...), custom_call_target="tpu_custom_call" | custom-call | tf_op jit(solution)/shard_map/pallas_call | solution.py:655
  20.7 2.0 %collective-permute-done.6.refs_2_ = f32[33,8,128]{2,1,0:T(8,128)S(1)} collective-permute-done((f32[33,8,128]{2,1,0:T(8,128)S(1)}, f32[33,8,128]{2,1,0:T(8,128)S(1)}, u32[]{:S(2)}, u32[]{:S(2)}) %collective-permute-start.6) | collective-permute-done | bytes 135200 | tf_op jit(solution)/shard_map/ppermute | solution.py:33
  22.7 0.0 collective-permute-done.7.refs_3_
  22.7 14.6 %shard_map.46 = (f32[16,16,256]{2,1,0:T(8,128)}, f32[16,16,256]{2,1,0:T(8,128)}) custom-call(f32[2,16,4,16,128]{4,3,2,1,0:T(8,128)S(1)} %get-tuple-element.21.own_ref, f32[200,8,128]{2,1,0:T(8,128)S(1)} %get-tuple-element.22.refs_0_, f32[200,8,128]{2,1,0:T(8,128)S(1)} %get-tuple-element.23.refs_1_, f32[33,8,128]{2,1,0:T(8,128)S(1)} %collective-permute-done.6.refs_2_, ...), custom_call_target="tpu_custom_call" | custom-call | tf_op jit(solution)/shard_map/pallas_call | solution.py:717
  (2 shorter events, 0.1 us)
Async XLA Ops:
  2.1 9.7 %collective-permute-start = (f32[22,16,128]{2,1,0:T(8,128)S(1)}, f32[22,16,128]{2,1,0:T(8,128)S(1)}, u32[]{:S(2)}, u32[]{:S(2)}) collective-permute-start(f32[22,16,128]{2,1,0:T(8,128)S(1)} %get-tuple-element.15), channel_id=1, source_target_pairs={{4,8},{8,4},{12,16},{16,12},{20,24},{24,20},{5,9},{9,5},{13,17},{1... | collective-permute-start | bytes 540680 | tf_op jit(solution)/shard_map/ppermute | solution.py:33
  3.1 16.2 %collective-permute-start.2 = (f32[100,8,128]{2,1,0:T(8,128)S(1)}, f32[100,8,128]{2,1,0:T(8,128)S(1)}, u32[]{:S(2)}, u32[]{:S(2)}) collective-permute-start(f32[100,8,128]{2,1,0:T(8,128)S(1)} %get-tuple-element.17), channel_id=1, source_target_pairs={{1,2},{2,1},{5,6},{6,5},{9,10},{10,9},{13,14},{14,13},{17,18},{18,... | collective-permute-start | bytes 1228808 | tf_op jit(solution)/shard_map/ppermute | solution.py:33
  7.6 11.6 %collective-permute-start.3 = (f32[100,8,128]{2,1,0:T(8,128)S(1)}, f32[100,8,128]{2,1,0:T(8,128)S(1)}, u32[]{:S(2)}, u32[]{:S(2)}) collective-permute-start(f32[100,8,128]{2,1,0:T(8,128)S(1)} %get-tuple-element.18), channel_id=1, source_target_pairs={{0,1},{1,0},{2,3},{3,2},{4,5},{5,4},{6,7},{7,6},{8,9},{9,8},{10,11... | collective-permute-start | bytes 1228808 | tf_op jit(solution)/shard_map/ppermute | solution.py:33
  7.7 8.6 %collective-permute-start.1 = (f32[22,16,128]{2,1,0:T(8,128)S(1)}, f32[22,16,128]{2,1,0:T(8,128)S(1)}, u32[]{:S(2)}, u32[]{:S(2)}) collective-permute-start(f32[22,16,128]{2,1,0:T(8,128)S(1)} %get-tuple-element.16), channel_id=1, source_target_pairs={{0,4},{4,0},{8,12},{12,8},{16,20},{20,16},{24,28},{28,24},{1,5},{5... | collective-permute-start | bytes 540680 | tf_op jit(solution)/shard_map/ppermute | solution.py:33
  11.8 7.4 %collective-permute-start.4 = (f32[33,8,128]{2,1,0:T(8,128)S(1)}, f32[33,8,128]{2,1,0:T(8,128)S(1)}, u32[]{:S(2)}, u32[]{:S(2)}) collective-permute-start(f32[33,8,128]{2,1,0:T(8,128)S(1)} %get-tuple-element.19), channel_id=1, source_target_pairs={{1,2},{2,1},{5,6},{6,5},{9,10},{10,9},{13,14},{14,13},{17,18},{18,... | collective-permute-start | bytes 405512 | tf_op jit(solution)/shard_map/ppermute | solution.py:33
  14.0 5.2 %collective-permute-start.5 = (f32[33,8,128]{2,1,0:T(8,128)S(1)}, f32[33,8,128]{2,1,0:T(8,128)S(1)}, u32[]{:S(2)}, u32[]{:S(2)}) collective-permute-start(f32[33,8,128]{2,1,0:T(8,128)S(1)} %get-tuple-element.20), channel_id=1, source_target_pairs={{0,1},{1,0},{2,3},{3,2},{4,5},{5,4},{6,7},{7,6},{8,9},{9,8},{10,11... | collective-permute-start | bytes 405512 | tf_op jit(solution)/shard_map/ppermute | solution.py:33
  16.4 6.3 %collective-permute-start.6 = (f32[33,8,128]{2,1,0:T(8,128)S(1)}, f32[33,8,128]{2,1,0:T(8,128)S(1)}, u32[]{:S(2)}, u32[]{:S(2)}) collective-permute-start(f32[33,8,128]{2,1,0:T(8,128)S(1)} %get-tuple-element.24), channel_id=1, source_target_pairs={{1,2},{2,1},{5,6},{6,5},{9,10},{10,9},{13,14},{14,13},{17,18},{18,... | collective-permute-start | bytes 405512 | tf_op jit(solution)/shard_map/ppermute | solution.py:33
  19.2 3.5 %collective-permute-start.7 = (f32[33,8,128]{2,1,0:T(8,128)S(1)}, f32[33,8,128]{2,1,0:T(8,128)S(1)}, u32[]{:S(2)}, u32[]{:S(2)}) collective-permute-start(f32[33,8,128]{2,1,0:T(8,128)S(1)} %get-tuple-element.25), channel_id=1, source_target_pairs={{0,1},{1,0},{2,3},{3,2},{4,5},{5,4},{6,7},{7,6},{8,9},{9,8},{10,11... | collective-permute-start | bytes 405512 | tf_op jit(solution)/shard_map/ppermute | solution.py:33

commit v8 on v7

--- a/solution.py
+++ b/solution.py
@@ -521,21 +521,35 @@
 
     def solve(m, low, high, right_side, held, offset, store):
         place = slice(offset + low, offset + high)
-        now = [None] * count[m]
-        for layer_no in range(layers):
+
+        def down(layer_no, before):
+            now = []
             for c in range(count[m]):
                 each = right_side(layer_no, c)
-                if layer_no:
-                    each = each + factor[m][layer_no, c, low:high] * now[c]
-                now[c] = each
+                if before is not None:
+                    each = each + factor[m][layer_no, c, low:high] * before[c]
+                now.append(each)
                 held[layer_no, c, place] = each * inverse[m][layer_no, c, low:high]
-        for layer_no in range(layers - 1, -1, -1):
+            return tuple(now)
+
+        def up(step, below):
+            layer_no = layers - 1 - step
+            now = []
             for c in range(count[m]):
                 each = held[layer_no, c, place]
-                if layer_no < layers - 1:
-                    each = each + factor[m][layer_no + 1, c, low:high] * now[c]
-                now[c] = each
+                if below is not None:
+                    each = each + factor[m][layer_no + 1, c, low:high] * below[c]
+                now.append(each)
                 store(layer_no, c, each)
+            return tuple(now)
+
+        for body in (down, up):
+            now = body(0, None)
+            if count[m] > 1:
+                lax.fori_loop(1, layers, body, now, unroll=3 if count[m] == count[0] else 5)
+            else:
+                for step in range(1, layers):
+                    now = body(step, now)
 
     def first_sweep(m):
         def store(layer_no, c, now):
@@ -599,7 +613,7 @@
             out = jnp.where(lane >= c * lanes, turned(cells[c], c * lanes - start), out)
         return taken(out, back)
 
-    def finish(layer_no, top, bottom):
+    def finish(layer_no):
         low, high = reach, reach + own_rows
         own = span(GUARD + low, GUARD + high)
         plain = span(low, high)
@@ -617,10 +631,10 @@
             remain = (
                 forcing[0][layer_no, c, plain] - centre * now + around(0, layer_no, c, low, high)
             )
-            if not top:
-                remain += upper[0][layer_no, c, plain] * value[0][layer_no - 1, c, own]
-            if not bottom:
-                remain += upper[0][layer_no + 1, c, plain] * value[0][layer_no + 1, c, own]
+            above = upper[0][layer_no, c, plain] * value[0][jnp.maximum(layer_no - 1, 0), c, own]
+            remain += jnp.where(layer_no > 0, above, 0.0)
+            beneath = value[0][jnp.minimum(layer_no + 1, layers - 1), c, own]
+            remain += upper[0][layer_no + 1, c, plain] * beneath
             cells.append(now)
             remains.append(remain)
         for tile_no in range(plan.own_cols // LANES):
@@ -628,19 +642,25 @@
             staged[0][layer_no, :, columns] = in_order(cells, tile_no)
             staged[1][layer_no, :, columns] = in_order(remains, tile_no)
 
-    copies = []
-    for layer_no in range(layers):
-        finish(layer_no, layer_no == 0, layer_no == layers - 1)
-        if layer_no % 4 == 3:
-            block = pl.ds(layer_no - 3, 4)
-            for i in range(2):
-                copy = pltpu.make_async_copy(
-                    staged[i].at[block], out_refs[i].at[block], semaphore.at[i, layer_no // 4]
-                )
-                copy.start()
-                copies.append(copy)
-    for copy in copies:
-        copy.wait()
+    def leave(group):
+        block = pl.ds(4 * group, 4)
+        return [
+            pltpu.make_async_copy(
+                staged[i].at[block], out_refs[i].at[block], semaphore.at[i, group]
+            )
+            for i in range(2)
+        ]
+
+    def finish_group(group):
+        for i in range(4):
+            finish(4 * group + i)
+        for copy in leave(group):
+            copy.start()
+
+    pl.loop(0, layers // 4)(finish_group)
+    for group in range(layers // 4):
+        for copy in leave(group):
+            copy.wait()
 
 
 def per_device(source, inv_density):

time: 37.5 us -> 36.6 us (0.976)
  Pallas kernels: 16.8 us -> 15.9 us
    pallas_call x1, Pallas kernels: 14.6 us -> 13.7 us  [per_device(): pl.pallas_call(functools.partial(cycle_kernel, plan), out_shape=[jax.Shap...]
where the time goes in v8:
time: 36.6 us; the launch traced here: 36.4 us
  Pallas kernels  15.9 us (43%)
  starting transfers between devices  14.4 us (39%)
  waiting for transfers between devices  4.27 us (12%)
  other arithmetic  1.06 us (3%)
  between operations  0.75 us (2%)
    ppermute x8, starting transfers between devices, swapped(): return lax.ppermute(array, axis, pairs)  14.4 us
    pallas_call x1, Pallas kernels, per_device(): pl.pallas_call(functools.partial(cycle_kernel, plan), out_shape=[jax.Shap...  13.7 us
    ppermute x8, waiting for transfers between devices, swapped(): return lax.ppermute(array, axis, pairs)  4.27 us
    pallas_call x5, Pallas kernels, kernel(): pl.pallas_call(functools.partial(body, plan), out_shape=outputs, in_specs...  2.17 us
    another operation x1, other arithmetic, per_device(): both = jnp.stack([inv_density, source])  1.06 us
  transfers between devices with their start and end apart: 8, of which 2 were waited for; matrix products, arithmetic and copies ran while one was open for 0% of the time, Pallas kernels for 5%

profile of v8, /device:TPU:1, one launch (start us, length us, event | category | flops | bytes accessed | tf_op | source)
XLA Modules:
  0.0 36.4 jit_solution(2092586062720059172)
XLA Ops:
  0.6 1.1 %pad_maximum_fusion.both_ref = f32[2,16,16,256]{3,2,1,0:T(8,128)S(1)} fusion(f32[1,16,16,256]{3,2,1,0:T(8,128)} %bitcast.2, f32[1,16,16,256]{3,2,1,0:T(8,128)} %bitcast.3), kind=kLoop, calls=%fused_computation | loop fusion | flops 131072 | bytes 1048576 | tf_op jit(solution)/shard_map/stack | solution.py:693
  1.7 0.4 %shard_map.42 = (f32[22,16,128]{2,1,0:T(8,128)S(1)}, f32[22,16,128]{2,1,0:T(8,128)S(1)}) custom-call(f32[2,16,16,256]{3,2,1,0:T(8,128)S(1)} %pad_maximum_fusion.both_ref), custom_call_target="tpu_custom_call" | custom-call | tf_op jit(solution)/shard_map/pallas_call | solution.py:675
  2.1 0.7 %collective-permute-start = (f32[22,16,128]{2,1,0:T(8,128)S(1)}, f32[22,16,128]{2,1,0:T(8,128)S(1)}, u32[]{:S(2)}, u32[]{:S(2)}) collective-permute-start(f32[22,16,128]{2,1,0:T(8,128)S(1)} %get-tuple-element.15), channel_id=1, source_target_pairs={{4,8},{8,4},{12,16},{16,12},{20,24},{24,20},{5,9},{9,5},{13,17},{1... | collective-permute-start | bytes 540680 | tf_op jit(solution)/shard_map/ppermute | solution.py:33
  2.8 0.3 shard_map.41
  3.1 4.5 %collective-permute-start.2 = (f32[100,8,128]{2,1,0:T(8,128)S(1)}, f32[100,8,128]{2,1,0:T(8,128)S(1)}, u32[]{:S(2)}, u32[]{:S(2)}) collective-permute-start(f32[100,8,128]{2,1,0:T(8,128)S(1)} %get-tuple-element.17), channel_id=1, source_target_pairs={{1,2},{2,1},{5,6},{6,5},{9,10},{10,9},{13,14},{14,13},{17,18},{18,... | collective-permute-start | bytes 1228808 | tf_op jit(solution)/shard_map/ppermute | solution.py:33
  7.6 0.1 collective-permute-start.3
  7.7 4.1 %collective-permute-start.1 = (f32[22,16,128]{2,1,0:T(8,128)S(1)}, f32[22,16,128]{2,1,0:T(8,128)S(1)}, u32[]{:S(2)}, u32[]{:S(2)}) collective-permute-start(f32[22,16,128]{2,1,0:T(8,128)S(1)} %get-tuple-element.16), channel_id=1, source_target_pairs={{0,4},{4,0},{8,12},{12,8},{16,20},{20,16},{24,28},{28,24},{1,5},{5... | collective-permute-start | bytes 540680 | tf_op jit(solution)/shard_map/ppermute | solution.py:33
  11.8 0.0 collective-permute-done.halo_ref.refs_0_
  11.8 2.2 %collective-permute-start.4 = (f32[33,8,128]{2,1,0:T(8,128)S(1)}, f32[33,8,128]{2,1,0:T(8,128)S(1)}, u32[]{:S(2)}, u32[]{:S(2)}) collective-permute-start(f32[33,8,128]{2,1,0:T(8,128)S(1)} %get-tuple-element.19), channel_id=1, source_target_pairs={{1,2},{2,1},{5,6},{6,5},{9,10},{10,9},{13,14},{14,13},{17,18},{18,... | collective-permute-start | bytes 405512 | tf_op jit(solution)/shard_map/ppermute | solution.py:33
  14.0 0.1 collective-permute-start.5
  14.1 2.2 %collective-permute-done.1.refs_1_.halo_ref = f32[22,16,128]{2,1,0:T(8,128)S(1)} collective-permute-done((f32[22,16,128]{2,1,0:T(8,128)S(1)}, f32[22,16,128]{2,1,0:T(8,128)S(1)}, u32[]{:S(2)}, u32[]{:S(2)}) %collective-permute-start.1) | collective-permute-done | bytes 180256 | tf_op jit(solution)/shard_map/ppermute | solution.py:33
  16.4 2.8 %collective-permute-start.6 = (f32[33,8,128]{2,1,0:T(8,128)S(1)}, f32[33,8,128]{2,1,0:T(8,128)S(1)}, u32[]{:S(2)}, u32[]{:S(2)}) collective-permute-start(f32[33,8,128]{2,1,0:T(8,128)S(1)} %get-tuple-element.24), channel_id=1, source_target_pairs={{1,2},{2,1},{5,6},{6,5},{9,10},{10,9},{13,14},{14,13},{17,18},{18,... | collective-permute-start | bytes 405512 | tf_op jit(solution)/shard_map/ppermute | solution.py:33
  19.2 0.0 collective-permute-done.4.refs_4_
  19.2 0.1 collective-permute-start.7
  19.3 0.0 collective-permute-done.5.refs_5_
  19.3 0.0 collective-permute-done.2.refs_2_
  19.3 0.0 collective-permute-done.3.refs_3_
  19.3 1.4 %shard_map.44 = (f32[2,16,4,16,128]{4,3,2,1,0:T(8,128)S(1)}, f32[200,8,128]{2,1,0:T(8,128)S(1)}, f32[200,8,128]{2,1,0:T(8,128)S(1)}) custom-call(f32[2,16,2,16,128]{4,3,2,1,0:T(8,128)S(1)} %get-tuple-element.14.cells_ref, f32[22,16,128]{2,1,0:T(8,128)S(1)} %collective-permute-done.halo_ref.refs_0_, ...), custom_call_target="tpu_custom_call" | custom-call | tf_op jit(solution)/shard_map/pallas_call | solution.py:675
  20.7 2.0 %collective-permute-done.6.refs_2_ = f32[33,8,128]{2,1,0:T(8,128)S(1)} collective-permute-done((f32[33,8,128]{2,1,0:T(8,128)S(1)}, f32[33,8,128]{2,1,0:T(8,128)S(1)}, u32[]{:S(2)}, u32[]{:S(2)}) %collective-permute-start.6) | collective-permute-done | bytes 135200 | tf_op jit(solution)/shard_map/ppermute | solution.py:33
  22.7 0.0 collective-permute-done.7.refs_3_
  22.7 13.7 %shard_map.46 = (f32[16,16,256]{2,1,0:T(8,128)}, f32[16,16,256]{2,1,0:T(8,128)}) custom-call(f32[2,16,4,16,128]{4,3,2,1,0:T(8,128)S(1)} %get-tuple-element.21.own_ref, f32[200,8,128]{2,1,0:T(8,128)S(1)} %get-tuple-element.22.refs_0_, f32[200,8,128]{2,1,0:T(8,128)S(1)} %get-tuple-element.23.refs_1_, f32[33,8,128]{2,1,0:T(8,128)S(1)} %collective-permute-done.6.refs_2_, ...), custom_call_target="tpu_custom_call" | custom-call | tf_op jit(solution)/shard_map/pallas_call | solution.py:737
  (2 shorter events, 0.1 us)
Async XLA Ops:
  2.1 9.7 %collective-permute-start = (f32[22,16,128]{2,1,0:T(8,128)S(1)}, f32[22,16,128]{2,1,0:T(8,128)S(1)}, u32[]{:S(2)}, u32[]{:S(2)}) collective-permute-start(f32[22,16,128]{2,1,0:T(8,128)S(1)} %get-tuple-element.15), channel_id=1, source_target_pairs={{4,8},{8,4},{12,16},{16,12},{20,24},{24,20},{5,9},{9,5},{13,17},{1... | collective-permute-start | bytes 540680 | tf_op jit(solution)/shard_map/ppermute | solution.py:33
  3.1 16.2 %collective-permute-start.2 = (f32[100,8,128]{2,1,0:T(8,128)S(1)}, f32[100,8,128]{2,1,0:T(8,128)S(1)}, u32[]{:S(2)}, u32[]{:S(2)}) collective-permute-start(f32[100,8,128]{2,1,0:T(8,128)S(1)} %get-tuple-element.17), channel_id=1, source_target_pairs={{1,2},{2,1},{5,6},{6,5},{9,10},{10,9},{13,14},{14,13},{17,18},{18,... | collective-permute-start | bytes 1228808 | tf_op jit(solution)/shard_map/ppermute | solution.py:33
  7.6 11.6 %collective-permute-start.3 = (f32[100,8,128]{2,1,0:T(8,128)S(1)}, f32[100,8,128]{2,1,0:T(8,128)S(1)}, u32[]{:S(2)}, u32[]{:S(2)}) collective-permute-start(f32[100,8,128]{2,1,0:T(8,128)S(1)} %get-tuple-element.18), channel_id=1, source_target_pairs={{0,1},{1,0},{2,3},{3,2},{4,5},{5,4},{6,7},{7,6},{8,9},{9,8},{10,11... | collective-permute-start | bytes 1228808 | tf_op jit(solution)/shard_map/ppermute | solution.py:33
  7.7 8.6 %collective-permute-start.1 = (f32[22,16,128]{2,1,0:T(8,128)S(1)}, f32[22,16,128]{2,1,0:T(8,128)S(1)}, u32[]{:S(2)}, u32[]{:S(2)}) collective-permute-start(f32[22,16,128]{2,1,0:T(8,128)S(1)} %get-tuple-element.16), channel_id=1, source_target_pairs={{0,4},{4,0},{8,12},{12,8},{16,20},{20,16},{24,28},{28,24},{1,5},{5... | collective-permute-start | bytes 540680 | tf_op jit(solution)/shard_map/ppermute | solution.py:33
  11.8 7.4 %collective-permute-start.4 = (f32[33,8,128]{2,1,0:T(8,128)S(1)}, f32[33,8,128]{2,1,0:T(8,128)S(1)}, u32[]{:S(2)}, u32[]{:S(2)}) collective-permute-start(f32[33,8,128]{2,1,0:T(8,128)S(1)} %get-tuple-element.19), channel_id=1, source_target_pairs={{1,2},{2,1},{5,6},{6,5},{9,10},{10,9},{13,14},{14,13},{17,18},{18,... | collective-permute-start | bytes 405512 | tf_op jit(solution)/shard_map/ppermute | solution.py:33
  14.0 5.2 %collective-permute-start.5 = (f32[33,8,128]{2,1,0:T(8,128)S(1)}, f32[33,8,128]{2,1,0:T(8,128)S(1)}, u32[]{:S(2)}, u32[]{:S(2)}) collective-permute-start(f32[33,8,128]{2,1,0:T(8,128)S(1)} %get-tuple-element.20), channel_id=1, source_target_pairs={{0,1},{1,0},{2,3},{3,2},{4,5},{5,4},{6,7},{7,6},{8,9},{9,8},{10,11... | collective-permute-start | bytes 405512 | tf_op jit(solution)/shard_map/ppermute | solution.py:33
  16.4 6.3 %collective-permute-start.6 = (f32[33,8,128]{2,1,0:T(8,128)S(1)}, f32[33,8,128]{2,1,0:T(8,128)S(1)}, u32[]{:S(2)}, u32[]{:S(2)}) collective-permute-start(f32[33,8,128]{2,1,0:T(8,128)S(1)} %get-tuple-element.24), channel_id=1, source_target_pairs={{1,2},{2,1},{5,6},{6,5},{9,10},{10,9},{13,14},{14,13},{17,18},{18,... | collective-permute-start | bytes 405512 | tf_op jit(solution)/shard_map/ppermute | solution.py:33
  19.2 3.5 %collective-permute-start.7 = (f32[33,8,128]{2,1,0:T(8,128)S(1)}, f32[33,8,128]{2,1,0:T(8,128)S(1)}, u32[]{:S(2)}, u32[]{:S(2)}) collective-permute-start(f32[33,8,128]{2,1,0:T(8,128)S(1)} %get-tuple-element.25), channel_id=1, source_target_pairs={{0,1},{1,0},{2,3},{3,2},{4,5},{5,4},{6,7},{7,6},{8,9},{9,8},{10,11... | collective-permute-start | bytes 405512 | tf_op jit(solution)/shard_map/ppermute | solution.py:33

commit v9 on v8

--- a/solution.py
+++ b/solution.py
@@ -404,12 +404,15 @@
 
     halos = Halos(plan)
     targets = ((density, GUARD), (forcing[0], 0))
-    for which, (target, guard) in enumerate(targets):
-        for layer_no in range(layers):
+
+    def copy_own(layer_no):
+        for which, (target, guard) in enumerate(targets):
             for c in range(count[0]):
                 target[layer_no, c, span(guard + reach, guard + reach + own_rows)] = own_ref[
                     which, layer_no, c
                 ]
+
+    pl.loop(0, layers, unroll=2)(copy_own)
     for side, message in enumerate(plan.along):
         for index, part in enumerate(message.parts):
             which, start, run, _ = part
@@ -592,8 +595,15 @@
         pl.loop(0, layers, unroll=layers if count[m] == 1 else 4)(restrict)
 
     first_sweep(coarsest)
-    for sweep_no in range(1, SWEEPS):
-        later_sweep(coarsest, 0, rows, sweep_no == SWEEPS - 1)
+    pl.loop(1, SWEEPS)(lambda sweep_no: later_sweep(coarsest, 0, rows, False))
+
+    def prolong_coarsest(layer_no):
+        place = slice(GUARD, GUARD + rows)
+        for c in range(count[coarsest - 1]):
+            parent = c * count[coarsest] // count[coarsest - 1]
+            value[coarsest - 1][layer_no, c, place] += value[coarsest][layer_no, parent, place]
+
+    pl.loop(0, layers, unroll=4)(prolong_coarsest)
 
     for m in range(coarsest - 1, -1, -1):
         low = (reach - m - 1) // 8 * 8

time: 36.6 us -> 36.4 us (level)
  no operation moved by 1% of the time
where the time goes in v9:
time: 36.4 us; the launch traced here: 36.2 us
  Pallas kernels  15.7 us (43%)
  starting transfers between devices  14.4 us (40%)
  waiting for transfers between devices  4.27 us (12%)
  other arithmetic  1.06 us (3%)
  between operations  0.75 us (2%)
    ppermute x8, starting transfers between devices, swapped(): return lax.ppermute(array, axis, pairs)  14.4 us
    pallas_call x1, Pallas kernels, per_device(): pl.pallas_call(functools.partial(cycle_kernel, plan), out_shape=[jax.Shap...  13.5 us
    ppermute x8, waiting for transfers between devices, swapped(): return lax.ppermute(array, axis, pairs)  4.27 us
    pallas_call x5, Pallas kernels, kernel(): pl.pallas_call(functools.partial(body, plan), out_shape=outputs, in_specs...  2.17 us
    another operation x1, other arithmetic, per_device(): both = jnp.stack([inv_density, source])  1.06 us
  transfers between devices with their start and end apart: 8, of which 2 were waited for; matrix products, arithmetic and copies ran while one was open for 0% of the time, Pallas kernels for 5%

profile of v9, /device:TPU:1, one launch (start us, length us, event | category | flops | bytes accessed | tf_op | source)
XLA Modules:
  0.0 36.2 jit_solution(10518234541191750079)
XLA Ops:
  0.6 1.1 %pad_maximum_fusion.both_ref = f32[2,16,16,256]{3,2,1,0:T(8,128)S(1)} fusion(f32[1,16,16,256]{3,2,1,0:T(8,128)} %bitcast.2, f32[1,16,16,256]{3,2,1,0:T(8,128)} %bitcast.3), kind=kLoop, calls=%fused_computation | loop fusion | flops 131072 | bytes 1048576 | tf_op jit(solution)/shard_map/stack | solution.py:703
  1.7 0.4 %shard_map.42 = (f32[22,16,128]{2,1,0:T(8,128)S(1)}, f32[22,16,128]{2,1,0:T(8,128)S(1)}) custom-call(f32[2,16,16,256]{3,2,1,0:T(8,128)S(1)} %pad_maximum_fusion.both_ref), custom_call_target="tpu_custom_call" | custom-call | tf_op jit(solution)/shard_map/pallas_call | solution.py:685
  2.1 0.7 %collective-permute-start = (f32[22,16,128]{2,1,0:T(8,128)S(1)}, f32[22,16,128]{2,1,0:T(8,128)S(1)}, u32[]{:S(2)}, u32[]{:S(2)}) collective-permute-start(f32[22,16,128]{2,1,0:T(8,128)S(1)} %get-tuple-element.15), channel_id=1, source_target_pairs={{4,8},{8,4},{12,16},{16,12},{20,24},{24,20},{5,9},{9,5},{13,17},{1... | collective-permute-start | bytes 540680 | tf_op jit(solution)/shard_map/ppermute | solution.py:33
  2.8 0.3 shard_map.41
  3.1 4.5 %collective-permute-start.2 = (f32[100,8,128]{2,1,0:T(8,128)S(1)}, f32[100,8,128]{2,1,0:T(8,128)S(1)}, u32[]{:S(2)}, u32[]{:S(2)}) collective-permute-start(f32[100,8,128]{2,1,0:T(8,128)S(1)} %get-tuple-element.17), channel_id=1, source_target_pairs={{1,2},{2,1},{5,6},{6,5},{9,10},{10,9},{13,14},{14,13},{17,18},{18,... | collective-permute-start | bytes 1228808 | tf_op jit(solution)/shard_map/ppermute | solution.py:33
  7.6 0.1 collective-permute-start.3
  7.7 4.1 %collective-permute-start.1 = (f32[22,16,128]{2,1,0:T(8,128)S(1)}, f32[22,16,128]{2,1,0:T(8,128)S(1)}, u32[]{:S(2)}, u32[]{:S(2)}) collective-permute-start(f32[22,16,128]{2,1,0:T(8,128)S(1)} %get-tuple-element.16), channel_id=1, source_target_pairs={{0,4},{4,0},{8,12},{12,8},{16,20},{20,16},{24,28},{28,24},{1,5},{5... | collective-permute-start | bytes 540680 | tf_op jit(solution)/shard_map/ppermute | solution.py:33
  11.8 0.0 collective-permute-done.halo_ref.refs_0_
  11.8 2.2 %collective-permute-start.4 = (f32[33,8,128]{2,1,0:T(8,128)S(1)}, f32[33,8,128]{2,1,0:T(8,128)S(1)}, u32[]{:S(2)}, u32[]{:S(2)}) collective-permute-start(f32[33,8,128]{2,1,0:T(8,128)S(1)} %get-tuple-element.19), channel_id=1, source_target_pairs={{1,2},{2,1},{5,6},{6,5},{9,10},{10,9},{13,14},{14,13},{17,18},{18,... | collective-permute-start | bytes 405512 | tf_op jit(solution)/shard_map/ppermute | solution.py:33
  14.0 0.1 collective-permute-start.5
  14.1 2.2 %collective-permute-done.1.refs_1_.halo_ref = f32[22,16,128]{2,1,0:T(8,128)S(1)} collective-permute-done((f32[22,16,128]{2,1,0:T(8,128)S(1)}, f32[22,16,128]{2,1,0:T(8,128)S(1)}, u32[]{:S(2)}, u32[]{:S(2)}) %collective-permute-start.1) | collective-permute-done | bytes 180256 | tf_op jit(solution)/shard_map/ppermute | solution.py:33
  16.4 2.8 %collective-permute-start.6 = (f32[33,8,128]{2,1,0:T(8,128)S(1)}, f32[33,8,128]{2,1,0:T(8,128)S(1)}, u32[]{:S(2)}, u32[]{:S(2)}) collective-permute-start(f32[33,8,128]{2,1,0:T(8,128)S(1)} %get-tuple-element.24), channel_id=1, source_target_pairs={{1,2},{2,1},{5,6},{6,5},{9,10},{10,9},{13,14},{14,13},{17,18},{18,... | collective-permute-start | bytes 405512 | tf_op jit(solution)/shard_map/ppermute | solution.py:33
  19.2 0.0 collective-permute-done.4.refs_4_
  19.2 0.1 collective-permute-start.7
  19.3 0.0 collective-permute-done.5.refs_5_
  19.3 0.0 collective-permute-done.2.refs_2_
  19.3 0.0 collective-permute-done.3.refs_3_
  19.3 1.4 %shard_map.44 = (f32[2,16,4,16,128]{4,3,2,1,0:T(8,128)S(1)}, f32[200,8,128]{2,1,0:T(8,128)S(1)}, f32[200,8,128]{2,1,0:T(8,128)S(1)}) custom-call(f32[2,16,2,16,128]{4,3,2,1,0:T(8,128)S(1)} %get-tuple-element.14.cells_ref, f32[22,16,128]{2,1,0:T(8,128)S(1)} %collective-permute-done.halo_ref.refs_0_, ...), custom_call_target="tpu_custom_call" | custom-call | tf_op jit(solution)/shard_map/pallas_call | solution.py:685
  20.7 2.0 %collective-permute-done.6.refs_2_ = f32[33,8,128]{2,1,0:T(8,128)S(1)} collective-permute-done((f32[33,8,128]{2,1,0:T(8,128)S(1)}, f32[33,8,128]{2,1,0:T(8,128)S(1)}, u32[]{:S(2)}, u32[]{:S(2)}) %collective-permute-start.6) | collective-permute-done | bytes 135200 | tf_op jit(solution)/shard_map/ppermute | solution.py:33
  22.7 0.0 collective-permute-done.7.refs_3_
  22.7 13.5 %shard_map.46 = (f32[16,16,256]{2,1,0:T(8,128)}, f32[16,16,256]{2,1,0:T(8,128)}) custom-call(f32[2,16,4,16,128]{4,3,2,1,0:T(8,128)S(1)} %get-tuple-element.21.own_ref, f32[200,8,128]{2,1,0:T(8,128)S(1)} %get-tuple-element.22.refs_0_, f32[200,8,128]{2,1,0:T(8,128)S(1)} %get-tuple-element.23.refs_1_, f32[33,8,128]{2,1,0:T(8,128)S(1)} %collective-permute-done.6.refs_2_, ...), custom_call_target="tpu_custom_call" | custom-call | tf_op jit(solution)/shard_map/pallas_call | solution.py:747
  (2 shorter events, 0.1 us)
Async XLA Ops:
  2.1 9.7 %collective-permute-start = (f32[22,16,128]{2,1,0:T(8,128)S(1)}, f32[22,16,128]{2,1,0:T(8,128)S(1)}, u32[]{:S(2)}, u32[]{:S(2)}) collective-permute-start(f32[22,16,128]{2,1,0:T(8,128)S(1)} %get-tuple-element.15), channel_id=1, source_target_pairs={{4,8},{8,4},{12,16},{16,12},{20,24},{24,20},{5,9},{9,5},{13,17},{1... | collective-permute-start | bytes 540680 | tf_op jit(solution)/shard_map/ppermute | solution.py:33
  3.1 16.2 %collective-permute-start.2 = (f32[100,8,128]{2,1,0:T(8,128)S(1)}, f32[100,8,128]{2,1,0:T(8,128)S(1)}, u32[]{:S(2)}, u32[]{:S(2)}) collective-permute-start(f32[100,8,128]{2,1,0:T(8,128)S(1)} %get-tuple-element.17), channel_id=1, source_target_pairs={{1,2},{2,1},{5,6},{6,5},{9,10},{10,9},{13,14},{14,13},{17,18},{18,... | collective-permute-start | bytes 1228808 | tf_op jit(solution)/shard_map/ppermute | solution.py:33
  7.6 11.6 %collective-permute-start.3 = (f32[100,8,128]{2,1,0:T(8,128)S(1)}, f32[100,8,128]{2,1,0:T(8,128)S(1)}, u32[]{:S(2)}, u32[]{:S(2)}) collective-permute-start(f32[100,8,128]{2,1,0:T(8,128)S(1)} %get-tuple-element.18), channel_id=1, source_target_pairs={{0,1},{1,0},{2,3},{3,2},{4,5},{5,4},{6,7},{7,6},{8,9},{9,8},{10,11... | collective-permute-start | bytes 1228808 | tf_op jit(solution)/shard_map/ppermute | solution.py:33
  7.7 8.6 %collective-permute-start.1 = (f32[22,16,128]{2,1,0:T(8,128)S(1)}, f32[22,16,128]{2,1,0:T(8,128)S(1)}, u32[]{:S(2)}, u32[]{:S(2)}) collective-permute-start(f32[22,16,128]{2,1,0:T(8,128)S(1)} %get-tuple-element.16), channel_id=1, source_target_pairs={{0,4},{4,0},{8,12},{12,8},{16,20},{20,16},{24,28},{28,24},{1,5},{5... | collective-permute-start | bytes 540680 | tf_op jit(solution)/shard_map/ppermute | solution.py:33
  11.8 7.4 %collective-permute-start.4 = (f32[33,8,128]{2,1,0:T(8,128)S(1)}, f32[33,8,128]{2,1,0:T(8,128)S(1)}, u32[]{:S(2)}, u32[]{:S(2)}) collective-permute-start(f32[33,8,128]{2,1,0:T(8,128)S(1)} %get-tuple-element.19), channel_id=1, source_target_pairs={{1,2},{2,1},{5,6},{6,5},{9,10},{10,9},{13,14},{14,13},{17,18},{18,... | collective-permute-start | bytes 405512 | tf_op jit(solution)/shard_map/ppermute | solution.py:33
  14.0 5.2 %collective-permute-start.5 = (f32[33,8,128]{2,1,0:T(8,128)S(1)}, f32[33,8,128]{2,1,0:T(8,128)S(1)}, u32[]{:S(2)}, u32[]{:S(2)}) collective-permute-start(f32[33,8,128]{2,1,0:T(8,128)S(1)} %get-tuple-element.20), channel_id=1, source_target_pairs={{0,1},{1,0},{2,3},{3,2},{4,5},{5,4},{6,7},{7,6},{8,9},{9,8},{10,11... | collective-permute-start | bytes 405512 | tf_op jit(solution)/shard_map/ppermute | solution.py:33
  16.4 6.3 %collective-permute-start.6 = (f32[33,8,128]{2,1,0:T(8,128)S(1)}, f32[33,8,128]{2,1,0:T(8,128)S(1)}, u32[]{:S(2)}, u32[]{:S(2)}) collective-permute-start(f32[33,8,128]{2,1,0:T(8,128)S(1)} %get-tuple-element.24), channel_id=1, source_target_pairs={{1,2},{2,1},{5,6},{6,5},{9,10},{10,9},{13,14},{14,13},{17,18},{18,... | collective-permute-start | bytes 405512 | tf_op jit(solution)/shard_map/ppermute | solution.py:33
  19.2 3.5 %collective-permute-start.7 = (f32[33,8,128]{2,1,0:T(8,128)S(1)}, f32[33,8,128]{2,1,0:T(8,128)S(1)}, u32[]{:S(2)}, u32[]{:S(2)}) collective-permute-start(f32[33,8,128]{2,1,0:T(8,128)S(1)} %get-tuple-element.25), channel_id=1, source_target_pairs={{0,1},{1,0},{2,3},{3,2},{4,5},{5,4},{6,7},{7,6},{8,9},{9,8},{10,11... | collective-permute-start | bytes 405512 | tf_op jit(solution)/shard_map/ppermute | solution.py:33

commit v10 on v9

--- a/solution.py
+++ b/solution.py
@@ -472,7 +472,8 @@
             upper[m][layers, c] = jnp.zeros((rows, LANES), jnp.float32)
 
     def pivots(some, layer_no, before, first):
-        after = []
+        after, lefts = [], []
+        number = sum(count[m] for m in some)
         for m in some:
             for c in range(count[m]):
                 above = upper[m][layer_no, c]
@@ -491,9 +492,16 @@
                     factor[m][layer_no, c] = share
                     pivot = centre - above * share
                 inverted = reciprocal(jnp.maximum(pivot, TINY))
-                inverse[m][layer_no, c] = relaxation * inverted
+                scaled = relaxation * inverted
+                inverse[m][layer_no, c] = scaled
                 after.append(inverted)
-        return tuple(after)
+                if m == 0:
+                    left = forcing[0][layer_no, c, 0:rows]
+                    if not first:
+                        left = left + share * before[number + c]
+                    value[0][layer_no, c, GUARD : GUARD + rows] = left * scaled
+                    lefts.append(left)
+        return tuple(after + lefts)
 
     for some in (range(1), range(1, levels)):
         lax.fori_loop(
@@ -522,7 +530,7 @@
             + south[m][layer_no, c + 1, span(low, high)] * ahead
         )
 
-    def solve(m, low, high, right_side, held, offset, store):
+    def solve(m, low, high, right_side, held, offset, store, forward=True):
         place = slice(offset + low, offset + high)
 
         def down(layer_no, before):
@@ -546,7 +554,7 @@
                 store(layer_no, c, each)
             return tuple(now)
 
-        for body in (down, up):
+        for body in (down, up) if forward else (up,):
             now = body(0, None)
             if count[m] > 1:
                 lax.fori_loop(1, layers, body, now, unroll=3 if count[m] == count[0] else 5)
@@ -558,7 +566,7 @@
         def store(layer_no, c, now):
             value[m][layer_no, c, GUARD : GUARD + rows] = now
 
-        solve(m, 0, rows, lambda z, c: forcing[m][z, c], value[m], GUARD, store)
+        solve(m, 0, rows, lambda z, c: forcing[m][z, c], value[m], GUARD, store, m > 0)
 
     def later_sweep(m, low, high, prolong):
         place = slice(GUARD + low, GUARD + high)
@@ -581,7 +589,7 @@
         first_sweep(m)
 
         def remain_of(layer_no, c, m=m):
-            kept = (1.0 - relaxation) * forcing[m][layer_no, c]
+            kept = (1.0 - relaxation) * forcing[m][layer_no, c, 0:rows]
             return kept + around(m, layer_no, c, 0, rows)
 
         def restrict(layer_no, m=m, remain_of=remain_of):
@@ -740,7 +748,7 @@
     scratch += [room(layers, n, total) for n in counts]
     scratch += [room(layers, n, total) for n in counts]
     scratch += [room(layers, n, high + GUARD) for n in counts]
-    scratch += [room(layers, counts[0], total)]
+    scratch += [room(layers, counts[0], total + 8)]
     scratch += [room(layers + 1, n, total) for n in counts[1:]]
     held = sum(math.prod(each.shape) for each in scratch) + sum(each.size for each in inputs)
     held = 4 * held

time: 36.4 us -> 36.4 us (level)
  no operation moved by 1% of the time
where the time goes in v10:
time: 36.4 us; the launch traced here: 36.2 us
  Pallas kernels  15.7 us (43%)
  starting transfers between devices  14.4 us (40%)
  waiting for transfers between devices  4.27 us (12%)
  other arithmetic  1.06 us (3%)
  between operations  0.75 us (2%)
    ppermute x8, starting transfers between devices, swapped(): return lax.ppermute(array, axis, pairs)  14.4 us
    pallas_call x1, Pallas kernels, per_device(): pl.pallas_call(functools.partial(cycle_kernel, plan), out_shape=[jax.Shap...  13.5 us
    ppermute x8, waiting for transfers between devices, swapped(): return lax.ppermute(array, axis, pairs)  4.27 us
    pallas_call x5, Pallas kernels, kernel(): pl.pallas_call(functools.partial(body, plan), out_shape=outputs, in_specs...  2.17 us
    another operation x1, other arithmetic, per_device(): both = jnp.stack([inv_density, source])  1.06 us
  transfers between devices with their start and end apart: 8, of which 2 were waited for; matrix products, arithmetic and copies ran while one was open for 0% of the time, Pallas kernels for 5%

profile of v10, /device:TPU:1, one launch (start us, length us, event | category | flops | bytes accessed | tf_op | source)
XLA Modules:
  0.0 36.2 jit_solution(9367013727652756643)
XLA Ops:
  0.6 1.1 %pad_maximum_fusion.both_ref = f32[2,16,16,256]{3,2,1,0:T(8,128)S(1)} fusion(f32[1,16,16,256]{3,2,1,0:T(8,128)} %bitcast.2, f32[1,16,16,256]{3,2,1,0:T(8,128)} %bitcast.3), kind=kLoop, calls=%fused_computation | loop fusion | flops 131072 | bytes 1048576 | tf_op jit(solution)/shard_map/stack | solution.py:711
  1.7 0.4 %shard_map.42 = (f32[22,16,128]{2,1,0:T(8,128)S(1)}, f32[22,16,128]{2,1,0:T(8,128)S(1)}) custom-call(f32[2,16,16,256]{3,2,1,0:T(8,128)S(1)} %pad_maximum_fusion.both_ref), custom_call_target="tpu_custom_call" | custom-call | tf_op jit(solution)/shard_map/pallas_call | solution.py:693
  2.1 0.7 %collective-permute-start = (f32[22,16,128]{2,1,0:T(8,128)S(1)}, f32[22,16,128]{2,1,0:T(8,128)S(1)}, u32[]{:S(2)}, u32[]{:S(2)}) collective-permute-start(f32[22,16,128]{2,1,0:T(8,128)S(1)} %get-tuple-element.15), channel_id=1, source_target_pairs={{4,8},{8,4},{12,16},{16,12},{20,24},{24,20},{5,9},{9,5},{13,17},{1... | collective-permute-start | bytes 540680 | tf_op jit(solution)/shard_map/ppermute | solution.py:33
  2.8 0.3 shard_map.41
  3.1 4.5 %collective-permute-start.2 = (f32[100,8,128]{2,1,0:T(8,128)S(1)}, f32[100,8,128]{2,1,0:T(8,128)S(1)}, u32[]{:S(2)}, u32[]{:S(2)}) collective-permute-start(f32[100,8,128]{2,1,0:T(8,128)S(1)} %get-tuple-element.17), channel_id=1, source_target_pairs={{1,2},{2,1},{5,6},{6,5},{9,10},{10,9},{13,14},{14,13},{17,18},{18,... | collective-permute-start | bytes 1228808 | tf_op jit(solution)/shard_map/ppermute | solution.py:33
  7.6 0.1 collective-permute-start.3
  7.7 4.1 %collective-permute-start.1 = (f32[22,16,128]{2,1,0:T(8,128)S(1)}, f32[22,16,128]{2,1,0:T(8,128)S(1)}, u32[]{:S(2)}, u32[]{:S(2)}) collective-permute-start(f32[22,16,128]{2,1,0:T(8,128)S(1)} %get-tuple-element.16), channel_id=1, source_target_pairs={{0,4},{4,0},{8,12},{12,8},{16,20},{20,16},{24,28},{28,24},{1,5},{5... | collective-permute-start | bytes 540680 | tf_op jit(solution)/shard_map/ppermute | solution.py:33
  11.8 0.0 collective-permute-done.halo_ref.refs_0_
  11.8 2.2 %collective-permute-start.4 = (f32[33,8,128]{2,1,0:T(8,128)S(1)}, f32[33,8,128]{2,1,0:T(8,128)S(1)}, u32[]{:S(2)}, u32[]{:S(2)}) collective-permute-start(f32[33,8,128]{2,1,0:T(8,128)S(1)} %get-tuple-element.19), channel_id=1, source_target_pairs={{1,2},{2,1},{5,6},{6,5},{9,10},{10,9},{13,14},{14,13},{17,18},{18,... | collective-permute-start | bytes 405512 | tf_op jit(solution)/shard_map/ppermute | solution.py:33
  14.0 0.1 collective-permute-start.5
  14.1 2.2 %collective-permute-done.1.refs_1_.halo_ref = f32[22,16,128]{2,1,0:T(8,128)S(1)} collective-permute-done((f32[22,16,128]{2,1,0:T(8,128)S(1)}, f32[22,16,128]{2,1,0:T(8,128)S(1)}, u32[]{:S(2)}, u32[]{:S(2)}) %collective-permute-start.1) | collective-permute-done | bytes 180256 | tf_op jit(solution)/shard_map/ppermute | solution.py:33
  16.4 2.8 %collective-permute-start.6 = (f32[33,8,128]{2,1,0:T(8,128)S(1)}, f32[33,8,128]{2,1,0:T(8,128)S(1)}, u32[]{:S(2)}, u32[]{:S(2)}) collective-permute-start(f32[33,8,128]{2,1,0:T(8,128)S(1)} %get-tuple-element.24), channel_id=1, source_target_pairs={{1,2},{2,1},{5,6},{6,5},{9,10},{10,9},{13,14},{14,13},{17,18},{18,... | collective-permute-start | bytes 405512 | tf_op jit(solution)/shard_map/ppermute | solution.py:33
  19.2 0.0 collective-permute-done.4.refs_4_
  19.2 0.1 collective-permute-start.7
  19.3 0.0 collective-permute-done.5.refs_5_
  19.3 0.0 collective-permute-done.2.refs_2_
  19.3 0.0 collective-permute-done.3.refs_3_
  19.3 1.4 %shard_map.44 = (f32[2,16,4,16,128]{4,3,2,1,0:T(8,128)S(1)}, f32[200,8,128]{2,1,0:T(8,128)S(1)}, f32[200,8,128]{2,1,0:T(8,128)S(1)}) custom-call(f32[2,16,2,16,128]{4,3,2,1,0:T(8,128)S(1)} %get-tuple-element.14.cells_ref, f32[22,16,128]{2,1,0:T(8,128)S(1)} %collective-permute-done.halo_ref.refs_0_, ...), custom_call_target="tpu_custom_call" | custom-call | tf_op jit(solution)/shard_map/pallas_call | solution.py:693
  20.7 2.0 %collective-permute-done.6.refs_2_ = f32[33,8,128]{2,1,0:T(8,128)S(1)} collective-permute-done((f32[33,8,128]{2,1,0:T(8,128)S(1)}, f32[33,8,128]{2,1,0:T(8,128)S(1)}, u32[]{:S(2)}, u32[]{:S(2)}) %collective-permute-start.6) | collective-permute-done | bytes 135200 | tf_op jit(solution)/shard_map/ppermute | solution.py:33
  22.7 0.0 collective-permute-done.7.refs_3_
  22.7 13.5 %shard_map.46 = (f32[16,16,256]{2,1,0:T(8,128)}, f32[16,16,256]{2,1,0:T(8,128)}) custom-call(f32[2,16,4,16,128]{4,3,2,1,0:T(8,128)S(1)} %get-tuple-element.21.own_ref, f32[200,8,128]{2,1,0:T(8,128)S(1)} %get-tuple-element.22.refs_0_, f32[200,8,128]{2,1,0:T(8,128)S(1)} %get-tuple-element.23.refs_1_, f32[33,8,128]{2,1,0:T(8,128)S(1)} %collective-permute-done.6.refs_2_, ...), custom_call_target="tpu_custom_call" | custom-call | tf_op jit(solution)/shard_map/pallas_call | solution.py:755
  (2 shorter events, 0.1 us)
Async XLA Ops:
  2.1 9.7 %collective-permute-start = (f32[22,16,128]{2,1,0:T(8,128)S(1)}, f32[22,16,128]{2,1,0:T(8,128)S(1)}, u32[]{:S(2)}, u32[]{:S(2)}) collective-permute-start(f32[22,16,128]{2,1,0:T(8,128)S(1)} %get-tuple-element.15), channel_id=1, source_target_pairs={{4,8},{8,4},{12,16},{16,12},{20,24},{24,20},{5,9},{9,5},{13,17},{1... | collective-permute-start | bytes 540680 | tf_op jit(solution)/shard_map/ppermute | solution.py:33
  3.1 16.2 %collective-permute-start.2 = (f32[100,8,128]{2,1,0:T(8,128)S(1)}, f32[100,8,128]{2,1,0:T(8,128)S(1)}, u32[]{:S(2)}, u32[]{:S(2)}) collective-permute-start(f32[100,8,128]{2,1,0:T(8,128)S(1)} %get-tuple-element.17), channel_id=1, source_target_pairs={{1,2},{2,1},{5,6},{6,5},{9,10},{10,9},{13,14},{14,13},{17,18},{18,... | collective-permute-start | bytes 1228808 | tf_op jit(solution)/shard_map/ppermute | solution.py:33
  7.6 11.6 %collective-permute-start.3 = (f32[100,8,128]{2,1,0:T(8,128)S(1)}, f32[100,8,128]{2,1,0:T(8,128)S(1)}, u32[]{:S(2)}, u32[]{:S(2)}) collective-permute-start(f32[100,8,128]{2,1,0:T(8,128)S(1)} %get-tuple-element.18), channel_id=1, source_target_pairs={{0,1},{1,0},{2,3},{3,2},{4,5},{5,4},{6,7},{7,6},{8,9},{9,8},{10,11... | collective-permute-start | bytes 1228808 | tf_op jit(solution)/shard_map/ppermute | solution.py:33
  7.7 8.6 %collective-permute-start.1 = (f32[22,16,128]{2,1,0:T(8,128)S(1)}, f32[22,16,128]{2,1,0:T(8,128)S(1)}, u32[]{:S(2)}, u32[]{:S(2)}) collective-permute-start(f32[22,16,128]{2,1,0:T(8,128)S(1)} %get-tuple-element.16), channel_id=1, source_target_pairs={{0,4},{4,0},{8,12},{12,8},{16,20},{20,16},{24,28},{28,24},{1,5},{5... | collective-permute-start | bytes 540680 | tf_op jit(solution)/shard_map/ppermute | solution.py:33
  11.8 7.4 %collective-permute-start.4 = (f32[33,8,128]{2,1,0:T(8,128)S(1)}, f32[33,8,128]{2,1,0:T(8,128)S(1)}, u32[]{:S(2)}, u32[]{:S(2)}) collective-permute-start(f32[33,8,128]{2,1,0:T(8,128)S(1)} %get-tuple-element.19), channel_id=1, source_target_pairs={{1,2},{2,1},{5,6},{6,5},{9,10},{10,9},{13,14},{14,13},{17,18},{18,... | collective-permute-start | bytes 405512 | tf_op jit(solution)/shard_map/ppermute | solution.py:33
  14.0 5.2 %collective-permute-start.5 = (f32[33,8,128]{2,1,0:T(8,128)S(1)}, f32[33,8,128]{2,1,0:T(8,128)S(1)}, u32[]{:S(2)}, u32[]{:S(2)}) collective-permute-start(f32[33,8,128]{2,1,0:T(8,128)S(1)} %get-tuple-element.20), channel_id=1, source_target_pairs={{0,1},{1,0},{2,3},{3,2},{4,5},{5,4},{6,7},{7,6},{8,9},{9,8},{10,11... | collective-permute-start | bytes 405512 | tf_op jit(solution)/shard_map/ppermute | solution.py:33
  16.4 6.3 %collective-permute-start.6 = (f32[33,8,128]{2,1,0:T(8,128)S(1)}, f32[33,8,128]{2,1,0:T(8,128)S(1)}, u32[]{:S(2)}, u32[]{:S(2)}) collective-permute-start(f32[33,8,128]{2,1,0:T(8,128)S(1)} %get-tuple-element.24), channel_id=1, source_target_pairs={{1,2},{2,1},{5,6},{6,5},{9,10},{10,9},{13,14},{14,13},{17,18},{18,... | collective-permute-start | bytes 405512 | tf_op jit(solution)/shard_map/ppermute | solution.py:33
  19.2 3.5 %collective-permute-start.7 = (f32[33,8,128]{2,1,0:T(8,128)S(1)}, f32[33,8,128]{2,1,0:T(8,128)S(1)}, u32[]{:S(2)}, u32[]{:S(2)}) collective-permute-start(f32[33,8,128]{2,1,0:T(8,128)S(1)} %get-tuple-element.25), channel_id=1, source_target_pairs={{0,1},{1,0},{2,3},{3,2},{4,5},{5,4},{6,7},{7,6},{8,9},{9,8},{10,11... | collective-permute-start | bytes 405512 | tf_op jit(solution)/shard_map/ppermute | solution.py:33
